TPU v7x, 32 devices: a whole 2x2x4 slice. The times are simulated.
32 devices in a mesh: ctx: 4 (over y, core), fsdp: 8 (over z, x).
Axes of the slice: x: 2, y: 2, z: 4, core: 2. Of those that a mesh axis runs over, the one named last changes fastest.
Arguments:
- inputs: bfloat16 [8, 512, 1024], P('fsdp', 'ctx'), may hold values from -6 to 6
- cotangent: bfloat16 [8, 512, 1024], P('fsdp', 'ctx'), may hold values from -6 to 6
- w_query: bfloat16 [1024, 1024], P('fsdp'), may hold values from -0.078125 to 0.078125
- w_key: bfloat16 [1024, 1024], P('fsdp'), may hold values from -0.078125 to 0.078125
- w_value: bfloat16 [1024, 1024], P('fsdp'), may hold values from -0.1875 to 0.1875
- w_out: bfloat16 [1024, 1024], P('fsdp'), may hold values from -1.5 to 1.5
- w_in: bfloat16 [1024, 4096], P('fsdp'), may hold values from -0.1875 to 0.1875
- w_down: bfloat16 [4096, 1024], P('fsdp'), may hold values from -0.125 to 0.125
- gain_attn: bfloat16 [1024], P('fsdp'), may hold values from 0.25 to 1.75
- gain_mlp: bfloat16 [1024], P('fsdp'), may hold values from 0.25 to 1.75
- rel_bias: bfloat16 [512], P('fsdp'), may hold values from -4 to 4
- buckets: int32 [1023], replicated, may hold values from 0 to 31, as said below
Outputs:
- output: bfloat16 [8, 512, 1024], P('fsdp', 'ctx')
- grad_inputs: bfloat16 [8, 512, 1024], P('fsdp', 'ctx')
- grad_w_query: float32 [1024, 1024], P('fsdp')
- grad_w_key: float32 [1024, 1024], P('fsdp')
- grad_w_value: float32 [1024, 1024], P('fsdp')
- grad_w_out: float32 [1024, 1024], P('fsdp')
- grad_w_in: float32 [1024, 4096], P('fsdp')
- grad_w_down: float32 [4096, 1024], P('fsdp')
- grad_gain_attn: float32 [1024], P('fsdp')
- grad_gain_mlp: float32 [1024], P('fsdp')
- grad_rel_bias: float32 [512], P('fsdp')
Inputs may be any that keep to these rules, and one draw needn't show every extreme that they name: `buckets`: entry 511 + k - q is the bucket of key position k for query position q: 0 where k = q; below 16 and not falling as q - k grows where k < q; 16 or more and not falling as k - q grows where k > q; each side reaches its top bucket.
All inputs are finite; a program needn't handle non-finite values.
Results may differ from a plain program's by a relative error of at most 0.019.
Values may be sent and summed in bfloat16 or wider, within the bound.
A program may use at most 192 MiB of HBM per device.

v0:
```python
import jax
import jax.numpy as jnp
from jax import lax
from jax.sharding import PartitionSpec as P

HEADS = 16
HEAD = 64
BUCKETS = 32


EPS = 1e-06


def norm_rows(values, gain):
    return values * lax.rsqrt(jnp.mean(values * values, axis=-1, keepdims=True) + EPS) * gain


def smooth_gelu(values):
    return 0.5 * values * (1.0 + jax.scipy.special.erf(values * 0.7071067811865476))


def gelu_slope(values):
    return (
        0.5 * (1.0 + jax.scipy.special.erf(values * 0.7071067811865476))
        + values * jnp.exp(-0.5 * values * values) * 0.3989422804014327
    )


def bucket_offsets(buckets, first_query, query_count):
    seq_length = (buckets.shape[0] + 1) // 2
    key_place = jnp.arange(seq_length, dtype=jnp.int32)
    query_place = first_query + jnp.arange(query_count, dtype=jnp.int32)
    return key_place[None, :] - query_place[:, None] + (seq_length - 1)


def make_bias(flat_table, buckets, first_query, query_count):
    bias_table = flat_table.reshape(BUCKETS, HEADS)
    one_hot = (buckets[:, None] == jnp.arange(BUCKETS, dtype=jnp.int32)[None, :]).astype(
        flat_table.dtype
    )
    per_offset = jnp.dot(one_hot, bias_table, precision=lax.Precision.HIGHEST)
    offsets = bucket_offsets(buckets, first_query, query_count)
    return jnp.take(per_offset.T, offsets, axis=1)


def pair_table(buckets, first_query, query_count):
    offsets = bucket_offsets(buckets, first_query, query_count)
    pair_bucket = jnp.take(buckets, offsets.reshape(-1), axis=0)
    return (pair_bucket[:, None] == jnp.arange(BUCKETS, dtype=jnp.int32)[None, :]).astype(
        jnp.bfloat16
    )


def fetch_attention(w_query, w_key, w_value, w_out, gain_attn, rel_bias):
    return (
        lax.all_gather(w_query, "fsdp", axis=0, tiled=True),
        lax.all_gather(w_key, "fsdp", axis=0, tiled=True),
        lax.all_gather(w_value, "fsdp", axis=0, tiled=True),
        lax.all_gather(w_out, "fsdp", axis=0, tiled=True),
        lax.all_gather(gain_attn, "fsdp", axis=0, tiled=True),
        lax.all_gather(rel_bias, "fsdp", axis=0, tiled=True),
    )


def fetch_mlp(w_in, w_down, gain_mlp):
    return (
        lax.all_gather(w_in, "fsdp", axis=0, tiled=True),
        lax.all_gather(w_down, "fsdp", axis=0, tiled=True),
        lax.all_gather(gain_mlp, "fsdp", axis=0, tiled=True),
    )


def share_keys(key_rows, value_rows):
    return (
        lax.all_gather(key_rows, "ctx", axis=1, tiled=True),
        lax.all_gather(value_rows, "ctx", axis=1, tiled=True),
    )


def scores_of(query_part, key_part, bias_values):
    return (
        jnp.einsum("qhd,khd->hqk", query_part, key_part, preferred_element_type=jnp.float32)
        + bias_values
    )


def shards(
    inputs,
    cotangent,
    w_query,
    w_key,
    w_value,
    w_out,
    w_in,
    w_down,
    gain_attn,
    gain_mlp,
    rel_bias,
    buckets,
):
    seq_count, row_count, width = inputs.shape
    total_rows = seq_count * row_count
    first_query = lax.axis_index("ctx") * row_count
    query_w, key_w, value_w, out_w, attn_gain, bias_flat = fetch_attention(
        w_query, w_key, w_value, w_out, gain_attn, rel_bias
    )
    in_w, down_w, mlp_gain = fetch_mlp(w_in, w_down, gain_mlp)
    bias_values = make_bias(bias_flat.astype(jnp.float32), buckets, first_query, row_count)
    inputs_flat = inputs.astype(jnp.float32).reshape(total_rows, width)
    attn_scale = attn_gain.astype(jnp.float32)
    normed_one = norm_rows(inputs_flat, attn_scale).astype(jnp.bfloat16)
    query_rows = jnp.dot(normed_one, query_w, preferred_element_type=jnp.float32).astype(
        jnp.bfloat16
    )
    key_rows = (
        jnp.dot(normed_one, key_w, preferred_element_type=jnp.float32)
        .astype(jnp.bfloat16)
        .reshape(seq_count, row_count, width)
    )
    value_rows = (
        jnp.dot(normed_one, value_w, preferred_element_type=jnp.float32)
        .astype(jnp.bfloat16)
        .reshape(seq_count, row_count, width)
    )
    all_keys, all_values = share_keys(key_rows, value_rows)
    query_heads = query_rows.reshape(seq_count, row_count, HEADS, HEAD)
    seq_index = 0
    key_heads = all_keys[seq_index].reshape(-1, HEADS, HEAD)
    value_heads = all_values[seq_index].reshape(-1, HEADS, HEAD)
    scores = scores_of(query_heads[seq_index], key_heads, bias_values)
    top_score = jnp.max(scores, axis=-1, keepdims=True)
    weights_exp = jnp.exp(scores - top_score)
    totals = jnp.sum(weights_exp, axis=-1, keepdims=True)
    probs_low = (weights_exp / totals).astype(jnp.bfloat16)
    mixed = jnp.einsum("hqk,khd->qhd", probs_low, value_heads, preferred_element_type=jnp.float32)
    mixed_list = mixed.reshape(row_count, width)
    lse_list = [top_score + jnp.log(totals)]
    attended = mixed_list.astype(jnp.bfloat16)
    hidden_res = inputs_flat + jnp.dot(attended, out_w, preferred_element_type=jnp.float32)
    mlp_scale = mlp_gain.astype(jnp.float32)
    normed_two = norm_rows(hidden_res, mlp_scale).astype(jnp.bfloat16)
    pre_act = jnp.dot(normed_two, in_w, preferred_element_type=jnp.float32)
    activated = smooth_gelu(pre_act).astype(jnp.bfloat16)
    result = hidden_res + jnp.dot(activated, down_w, preferred_element_type=jnp.float32)
    in_w, down_w, mlp_gain = fetch_mlp(w_in, w_down, gain_mlp)
    query_w, key_w, value_w, out_w, attn_gain, bias_flat = fetch_attention(
        w_query, w_key, w_value, w_out, gain_attn, rel_bias
    )
    all_keys, all_values = share_keys(key_rows, value_rows)
    grad_rows = cotangent.reshape(total_rows, width)
    grad_down = jnp.einsum("nf,nd->fd", activated, grad_rows, preferred_element_type=jnp.float32)
    grad_act = jnp.einsum("nd,fd->nf", grad_rows, down_w, preferred_element_type=jnp.float32)
    grad_pre = (grad_act * gelu_slope(pre_act)).astype(jnp.bfloat16)
    grad_in = jnp.einsum("nd,nf->df", normed_two, grad_pre, preferred_element_type=jnp.float32)
    grad_normed_two = jnp.einsum("nf,df->nd", grad_pre, in_w, preferred_element_type=jnp.float32)
    back_hidden, grad_mlp_gain = jax.vjp(norm_rows, hidden_res, mlp_scale)[1](grad_normed_two)
    grad_hidden = grad_rows.astype(jnp.float32) + back_hidden
    grad_attn_low = grad_hidden.astype(jnp.bfloat16)
    grad_out = jnp.einsum("nd,ne->de", attended, grad_attn_low, preferred_element_type=jnp.float32)
    grad_attended = jnp.einsum(
        "ne,de->nd", grad_attn_low, out_w, preferred_element_type=jnp.float32
    ).astype(jnp.bfloat16)
    grad_heads = grad_attended.reshape(seq_count, row_count, HEADS, HEAD)
    pair_buckets = pair_table(buckets, first_query, row_count)
    seq_index = 0
    key_heads = all_keys[seq_index].reshape(-1, HEADS, HEAD)
    value_heads = all_values[seq_index].reshape(-1, HEADS, HEAD)
    scores = scores_of(query_heads[seq_index], key_heads, bias_values)
    probs = jnp.exp(scores - lse_list[seq_index])
    grad_probs = jnp.einsum(
        "qhd,khd->hqk", grad_heads[seq_index], value_heads, preferred_element_type=jnp.float32
    )
    row_inner = jnp.sum(probs * grad_probs, axis=-1, keepdims=True)
    grad_scores = (probs * (grad_probs - row_inner)).astype(jnp.bfloat16)
    bias_grad = jnp.dot(
        grad_scores.reshape(HEADS, -1), pair_buckets, preferred_element_type=jnp.float32
    )
    query_grads = jnp.einsum(
        "hqk,khd->qhd", grad_scores, key_heads, preferred_element_type=jnp.float32
    ).reshape(row_count, width)
    key_grads = [
        jnp.einsum(
            "hqk,qhd->khd", grad_scores, query_heads[seq_index], preferred_element_type=jnp.float32
        ).reshape(-1, width)
    ]
    value_grads = [
        jnp.einsum(
            "hqk,qhd->khd",
            probs.astype(jnp.bfloat16),
            grad_heads[seq_index],
            preferred_element_type=jnp.float32,
        ).reshape(-1, width)
    ]
    key_back, value_back = (
        lax.psum_scatter(
            jnp.stack(key_grads).astype(jnp.bfloat16), "ctx", scatter_dimension=1, tiled=True
        ).astype(jnp.float32),
        lax.psum_scatter(
            jnp.stack(value_grads).astype(jnp.bfloat16), "ctx", scatter_dimension=1, tiled=True
        ).astype(jnp.float32),
    )
    grad_query_rows = query_grads.astype(jnp.bfloat16)
    grad_key_rows = key_back.reshape(total_rows, width).astype(jnp.bfloat16)
    grad_value_rows = value_back.reshape(total_rows, width).astype(jnp.bfloat16)
    grad_query = jnp.einsum(
        "nd,ne->de", normed_one, grad_query_rows, preferred_element_type=jnp.float32
    )
    grad_key = jnp.einsum(
        "nd,ne->de", normed_one, grad_key_rows, preferred_element_type=jnp.float32
    )
    grad_value = jnp.einsum(
        "nd,ne->de", normed_one, grad_value_rows, preferred_element_type=jnp.float32
    )
    grad_normed_one = jnp.einsum(
        "ne,de->nd", grad_query_rows, query_w, preferred_element_type=jnp.float32
    )
    grad_normed_one = grad_normed_one + jnp.einsum(
        "ne,de->nd", grad_key_rows, key_w, preferred_element_type=jnp.float32
    )
    grad_normed_one = grad_normed_one + jnp.einsum(
        "ne,de->nd", grad_value_rows, value_w, preferred_element_type=jnp.float32
    )
    back_inputs, grad_attn_gain = jax.vjp(norm_rows, inputs_flat, attn_scale)[1](grad_normed_one)
    grad_inputs = (
        (grad_hidden + back_inputs).astype(jnp.bfloat16).reshape(seq_count, row_count, width)
    )
    grad_bias_flat = bias_grad.T.reshape(BUCKETS * HEADS)
    (
        part_query,
        part_key,
        part_value,
        part_out,
        part_in,
        part_down,
        part_attn_gain,
        part_mlp_gain,
        part_bias,
    ) = (
        lax.psum_scatter(grad_query, "fsdp", scatter_dimension=0, tiled=True),
        lax.psum_scatter(grad_key, "fsdp", scatter_dimension=0, tiled=True),
        lax.psum_scatter(grad_value, "fsdp", scatter_dimension=0, tiled=True),
        lax.psum_scatter(grad_out, "fsdp", scatter_dimension=0, tiled=True),
        lax.psum_scatter(grad_in, "fsdp", scatter_dimension=0, tiled=True),
        lax.psum_scatter(grad_down, "fsdp", scatter_dimension=0, tiled=True),
        lax.psum_scatter(grad_attn_gain, "fsdp", scatter_dimension=0, tiled=True),
        lax.psum_scatter(grad_mlp_gain, "fsdp", scatter_dimension=0, tiled=True),
        lax.psum_scatter(grad_bias_flat, "fsdp", scatter_dimension=0, tiled=True),
    )
    summed = (
        lax.psum(part_query.astype(jnp.bfloat16), "ctx").astype(jnp.float32),
        lax.psum(part_key.astype(jnp.bfloat16), "ctx").astype(jnp.float32),
        lax.psum(part_value.astype(jnp.bfloat16), "ctx").astype(jnp.float32),
        lax.psum(part_out.astype(jnp.bfloat16), "ctx").astype(jnp.float32),
        lax.psum(part_in.astype(jnp.bfloat16), "ctx").astype(jnp.float32),
        lax.psum(part_down.astype(jnp.bfloat16), "ctx").astype(jnp.float32),
        lax.psum(part_attn_gain.astype(jnp.bfloat16), "ctx").astype(jnp.float32),
        lax.psum(part_mlp_gain.astype(jnp.bfloat16), "ctx").astype(jnp.float32),
        lax.psum(part_bias.astype(jnp.bfloat16), "ctx").astype(jnp.float32),
    )
    output = result.astype(jnp.bfloat16).reshape(seq_count, row_count, width)
    return (
        output,
        grad_inputs,
        summed[0],
        summed[1],
        summed[2],
        summed[3],
        summed[4],
        summed[5],
        summed[6],
        summed[7],
        summed[8],
    )


def solution(mesh):
    placed = (
        P("fsdp", "ctx", None),
        P("fsdp", "ctx", None),
        P("fsdp", None),
        P("fsdp", None),
        P("fsdp", None),
        P("fsdp", None),
        P("fsdp", None),
        P("fsdp", None),
        P("fsdp"),
        P("fsdp"),
        P("fsdp"),
        P(),
    )
    return jax.shard_map(
        shards,
        mesh=mesh,
        in_specs=placed,
        out_specs=(
            P("fsdp", "ctx", None),
            P("fsdp", "ctx", None),
            P("fsdp", None),
            P("fsdp", None),
            P("fsdp", None),
            P("fsdp", None),
            P("fsdp", None),
            P("fsdp", None),
            P("fsdp"),
            P("fsdp"),
            P("fsdp"),
        ),
        check_vma=False,
    )
```

profile of v0, /device:TPU:0, one launch (start us, length us, event | category | flops | bytes accessed | tf_op | source)
XLA Modules:
  0.0 1607.3 jit_solution(11784132070798079456)
XLA Ops:
  9.5 22.3 %all-gather.2 = bf16[8,1,128]{2,1,0:T(2,128)(2,1)S(1)} all-gather(bf16[1,1,128]{2,1,0:T(2,128)(2,1)} %bitcast.193), channel_id=1, replica_groups=mesh['ctx'=4,'fsdp'=8] {'fsdp'}, dimensions={0}, use_global_device_ids=true | all-gather | bytes 2304 | tf_op jit(solution)/shard_map/all_gather | solution.py:60
  32.9 29.3 %all-gather.13.cloned.1.call-done = bf16[1024,1024]{1,0:T(8,128)(2,1)} async-done(((bf16[128,1024]{1,0:T(8,128)(2,1)}), bf16[1024,1024]{1,0:T(8,128)(2,1)}) %all-gather.13.cloned.1.call-update) | async-done | bytes 2097168 | tf_op jit(solution)/shard_map/all_gather | solution.py:58
  65.2 46.9 %all-gather.17.cloned.1.call-done = bf16[1024,1024]{1,0:T(8,128)(2,1)} async-done(((bf16[128,1024]{1,0:T(8,128)(2,1)}), bf16[1024,1024]{1,0:T(8,128)(2,1)}) %all-gather.17.cloned.1.call-update) | async-done | bytes 2097168 | tf_op jit(solution)/shard_map/all_gather | solution.py:57
  118.6 19.1 %all-reduce = bf16[512]{0:T(512)(128)(2,1)S(1)} all-reduce(bf16[512]{0:T(512)(128)(2,1)S(1)} %dynamic-update-slice), channel_id=1, replica_groups=mesh['ctx'=4,'fsdp'=8] {'fsdp'}, use_global_device_ids=true, to_apply=%add | all-reduce | flops 512 | bytes 2048
  138.4 217.1 %gather_fusion = f32[65536,16]{1,0:T(8,128)} fusion(f32[16,1023]{0,1:T(8,128)S(1)} %fusion.34, s32[65536]{0:T(1024)S(1)} %broadcast_clamp_fusion.1), kind=kCustom, calls=%fused_computation | custom fusion | bytes 8650752 | tf_op jit(solution)/shard_map/jit(_take)/gather | solution.py:43
  355.5 20.9 %copy.56 = f32[128,512,16]{1,0,2:T(8,128)} copy(f32[128,512,16]{2,1,0:T(8,128)} %bitcast.154) | data formatting | bytes 8388608 | tf_op jit(solution)/shard_map/jit(_take)/gather | solution.py:43
  376.4 16.5 %all-gather.3 = bf16[8,1,128]{2,1,0:T(2,128)(2,1)S(1)} all-gather(bf16[1,1,128]{2,1,0:T(2,128)(2,1)S(1)} %bitcast.194), channel_id=1, replica_groups=mesh['ctx'=4,'fsdp'=8] {'fsdp'}, dimensions={0}, use_global_device_ids=true | all-gather | bytes 2304 | tf_op jit(solution)/shard_map/all_gather | solution.py:69
  399.1 3.5 fusion.72
  408.5 4.8 fusion.63
  413.3 87.0 %all-gather.23.cloned.1.call-done = bf16[4096,1024]{1,0:T(8,128)(2,1)} async-done(((bf16[512,1024]{1,0:T(8,128)(2,1)}), bf16[4096,1024]{1,0:T(8,128)(2,1)}) %all-gather.23.cloned.1.call-update) | async-done | bytes 8388624 | tf_op jit(solution)/shard_map/all_gather | solution.py:68
  500.3 6.6 fusion.1
  506.9 3.0 multiply_reduce_fusion.1
  513.5 4.2 multiply_reduce_fusion
  521.8 6.0 copy.57
  527.7 3.0 copy.72
  530.8 4.2 fusion.13
  535.0 6.0 copy.59
  541.0 3.0 copy.71
  550.5 3.6 fusion.57
  558.1 3.8 fusion.41
  562.0 19.4 %reduce-scatter.27.cloned.1.call-done = bf16[128,1024]{1,0:T(8,128)(2,1)} async-done(((bf16[512,1024]{1,0:T(8,128)(2,1)}), bf16[128,1024]{1,0:T(8,128)(2,1)}) %reduce-scatter.27.cloned.1.call-update) | async-done | bytes 262160
  585.3 3.8 fusion.38
  589.2 9.4 fusion.62
  598.6 9.1 fusion.44
  610.6 531.8 %gather_fusion.1 = s32[65536]{0:T(1024)} fusion(s32[1023]{0:T(1024)S(1)} %copy-done, s32[65536]{0:T(1024)} %broadcast_clamp_fusion), kind=kCustom, calls=%fused_computation.1 | custom fusion | bytes 786432 | tf_op jit(solution)/shard_map/jit(_take)/gather | solution.py:48
  1149.0 4.1 copy.68
  1153.1 5.6 fusion.18
  1165.9 67.9 %reduce-scatter.21.cloned.1.call-done = f32[128,4096]{1,0:T(8,128)} async-done(((f32[1024,4096]{1,0:T(8,128)}), f32[128,4096]{1,0:T(8,128)}) %reduce-scatter.21.cloned.1.call-update) | async-done | bytes 2097168 | tf_op jit(solution)/shard_map/reduce_scatter | solution.py:243
  1236.4 283.2 %reduce-scatter.23.cloned.1.call-done = f32[512,1024]{1,0:T(8,128)} async-done(((f32[4096,1024]{1,0:T(8,128)}), f32[512,1024]{1,0:T(8,128)}) %reduce-scatter.23.cloned.1.call-update) | async-done | bytes 2097168 | tf_op jit(solution)/shard_map/reduce_scatter | solution.py:244
  1530.5 35.1 %all-reduce.4 = (bf16[1024]{0:T(1024)(128)(2,1)S(1)}, bf16[1024]{0:T(1024)(128)(2,1)S(1)}, bf16[512]{0:T(512)(128)(2,1)S(1)}) all-reduce(f32[1024]{0:T(1024)S(1)} %get-tuple-element.13, f32[1024]{0:T(1024)S(1)} %get-tuple-element.11, f32[512]{0:T(512)S(1)} %reshape.311), channel_id=12, replica_groups=mesh['ctx'=4,'fsdp'=8] {'fsdp'}, use_global_device_ids=true, to_apply=%region_22.23.clone | all-reduce | flops 2560 | bytes 15360
  1565.9 6.1 all-reduce.5
  1574.5 16.9 %all-reduce.9.cloned.1.call-done = (bf16[128,1024]{1,0:T(8,128)(2,1)}, bf16[128,1024]{1,0:T(8,128)(2,1)}, bf16[128,1024]{1,0:T(8,128)(2,1)}, bf16[128,1024]{1,0:...) async-done(((bf16[128,1024]{1,0:T(8,128)(2,1)}, bf16[128,1024]{1,0:T(8,128)(2,1)}, bf16[128,1024]{1,0:T(8,128)(2,1)}, bf16[128,1024]{1,0:T(8,128)(2,1)}, ...) | async-done | bytes 3145744 | tf_op jit(solution)/shard_map/psum | solution.py:250
  (176 shorter events, 87.6 us)
Async XLA Ops:
  7.2 104.9 %copy-start.5 = (bf16[1,128,1024]{2,1,0:T(8,128)(2,1)S(1)}, bf16[1,128,1024]{2,1,0:T(8,128)(2,1)}, u32[]{:S(2)}) copy-start(bf16[1,128,1024]{2,1,0:T(8,128)(2,1)} %param.12) | copy-start | bytes 786436
  7.2 55.0 %all-gather.13.cloned.1.call-start = ((), (), s32[]{:S(2)}) async-start(), calls=%async_computation.8 | async-start | bytes 2359296 | tf_op jit(solution)/shard_map/all_gather | solution.py:58
  7.9 104.2 %all-gather.17.cloned.1.call-start = ((), (), s32[]{:S(2)}) async-start(), calls=%async_computation.10 | async-start | bytes 2359296 | tf_op jit(solution)/shard_map/all_gather | solution.py:57
  8.7 384.5 %all-gather.15.cloned.1.call-start = ((), (), s32[]{:S(2)}) async-start(), calls=%async_computation.9 | async-start | bytes 2359296 | tf_op jit(solution)/shard_map/all_gather | solution.py:56
  9.4 386.1 %all-gather.25.cloned.1.call-start = ((), (), s32[]{:S(2)}) async-start(), calls=%async_computation.20 | async-start | bytes 1310720 | tf_op jit(solution)/shard_map/all_gather | solution.py:76
  32.8 79.3 %copy-start.27 = (f32[128]{0:T(128)}, f32[128]{0:T(128)S(1)}, u32[]{:S(2)}) copy-start(f32[128]{0:T(128)S(1)} %fusion.27) | copy-start | bytes 1540
  65.1 52.0 %copy-start.26 = (u32[32]{0:T(128)S(1)}, u32[32]{0:T(128)}, u32[]{:S(2)}) copy-start(u32[32]{0:T(128)} %constant.68) | copy-start | bytes 388
  65.1 53.2 %copy-start.30 = (bf16[64]{0:T(256)(128)(2,1)S(1)}, bf16[64]{0:T(256)(128)(2,1)}, u32[]{:S(2)}) copy-start(bf16[64]{0:T(256)(128)(2,1)} %param.22) | copy-start | bytes 388
  65.1 332.1 %all-gather.27.cloned.1.call-start = ((), (), s32[]{:S(2)}) async-start(), calls=%async_computation.21 | async-start | bytes 1310720 | tf_op jit(solution)/shard_map/all_gather | solution.py:75
  114.9 23.1 %copy-start = (s32[1023]{0:T(1024)S(1)}, s32[1023]{0:T(1024)}, u32[]{:S(2)}) copy-start(s32[1023]{0:T(1024)} %param.23) | copy-start | bytes 12280
  114.9 291.2 %all-gather.19.cloned.1.call-start = ((), (), s32[]{:S(2)}) async-start(), calls=%async_computation.11 | async-start | bytes 2359296 | tf_op jit(solution)/shard_map/all_gather | solution.py:59
  115.5 292.9 %all-gather.21.cloned.1.call-start = ((), (), s32[]{:S(2)}) async-start(), calls=%async_computation.12 | async-start | bytes 9437184 | tf_op jit(solution)/shard_map/all_gather | solution.py:67
  116.3 384.0 %all-gather.23.cloned.1.call-start = ((), (), s32[]{:S(2)}) async-start(), calls=%async_computation.13 | async-start | bytes 9437184 | tf_op jit(solution)/shard_map/all_gather | solution.py:68
  117.0 437.2 %reduce-scatter.25.cloned.1.call-start = ((), (), s32[]{:S(2)}) async-start(), calls=%async_computation.22 | async-start | bytes 1310720
  355.5 20.9 %copy-start.29 = (bf16[128]{0:T(256)(128)(2,1)S(1)}, bf16[128]{0:T(256)(128)(2,1)}, u32[]{:S(2)}) copy-start(bf16[128]{0:T(256)(128)(2,1)} %param.21) | copy-start | bytes 772
  395.5 3.6 copy-start.14
  397.2 6.7 copy-start.10
  399.1 3.5 copy-start.6
  408.5 91.8 %copy-start.19 = (bf16[1,128,1024]{2,1,0:T(8,128)(2,1)S(1)}, bf16[1,128,1024]{2,1,0:T(8,128)(2,1)}, u32[]{:S(2)}) copy-start(bf16[1,128,1024]{2,1,0:T(8,128)(2,1)} %param.13) | copy-start | bytes 786436
  500.3 6.6 copy-start.3
  513.5 4.2 copy-start.2
  530.8 50.6 %reduce-scatter.27.cloned.1.call-start = ((), (), s32[]{:S(2)}) async-start(), calls=%async_computation.23 | async-start | bytes 1310720
  544.0 614.7 %reduce-scatter.13.cloned.1.call-start = ((), (), s32[]{:S(2)}) async-start(), calls=%async_computation.14 | async-start | bytes 4718592 | tf_op jit(solution)/shard_map/reduce_scatter | solution.py:239
  550.4 610.0 %reduce-scatter.19.cloned.1.call-start = ((), (), s32[]{:S(2)}) async-start(), calls=%async_computation.17 | async-start | bytes 4718592 | tf_op jit(solution)/shard_map/reduce_scatter | solution.py:242
  554.1 608.2 %reduce-scatter.15.cloned.1.call-start = ((), (), s32[]{:S(2)}) async-start(), calls=%async_computation.15 | async-start | bytes 4718592 | tf_op jit(solution)/shard_map/reduce_scatter | solution.py:240
  561.9 602.2 %reduce-scatter.17.cloned.1.call-start = ((), (), s32[]{:S(2)}) async-start(), calls=%async_computation.16 | async-start | bytes 4718592 | tf_op jit(solution)/shard_map/reduce_scatter | solution.py:241
  589.1 644.6 %reduce-scatter.21.cloned.1.call-start = ((), (), s32[]{:S(2)}) async-start(), calls=%async_computation.18 | async-start | bytes 18874368 | tf_op jit(solution)/shard_map/reduce_scatter | solution.py:243
  598.6 921.0 %reduce-scatter.23.cloned.1.call-start = ((), (), s32[]{:S(2)}) async-start(), calls=%async_computation.19 | async-start | bytes 18874368 | tf_op jit(solution)/shard_map/reduce_scatter | solution.py:244
  607.7 983.6 %all-reduce.9.cloned.1.call-start = ((), (), s32[]{:S(2)}) async-start(), calls=%async_computation.24 | async-start | bytes 6291456 | tf_op jit(solution)/shard_map/psum | solution.py:250
  1529.5 44.0 %copy-start.28 = (f32[128]{0:T(128)S(1)}, f32[128]{0:T(128)}, u32[]{:S(2)}) copy-start(f32[128]{0:T(128)} %copy-done.27) | copy-start | bytes 1540
  1591.4 5.5 copy-start.24
  1591.4 6.3 copy-start.22
  (16 other events, 33.7 us)
Sparse Core Ops, SparseCore 0:
  10.1 51.9 all-gather.12
  64.3 47.7 all-gather.16
  114.2 47.8 all-gather.14
  164.1 15.2 all-gather.24
  181.4 16.7 all-gather.26
  200.1 49.2 all-gather.18
  251.5 123.4 all-gather.20
  377.1 123.1 all-gather.22
  530.9 23.0 reduce-scatter.24
  556.5 24.8 reduce-scatter.26
  585.0 87.9 reduce-scatter.12
  676.9 87.6 reduce-scatter.18
  768.2 87.6 reduce-scatter.14
  859.8 87.8 reduce-scatter.16
  951.3 282.3 reduce-scatter.20
  1237.8 281.7 reduce-scatter.22
  1522.8 68.5 all-reduce.8
where the time goes:
time: 1610 us
  local copies, waits for them, and re-layouts  816 us (51%)
  waiting for transfers between devices  555 us (34%)
  blocking collectives  99.3 us (6%)
  matrix products  87.8 us (5%)
  other arithmetic  32.4 us (2%)
  between operations  16.5 us (1%)
    gather x1, local copies, waits for them, and re-layouts, pair_table(): pair_bucket = jnp.take(buckets, offsets.reshape(-1), axis=0)  532 us
    reduce_scatter x1, waiting for transfers between devices, shards(): lax.psum_scatter(grad_down, 'fsdp', scatter_dimension=0, tiled=True)  283 us
    gather x2, local copies, waits for them, and re-layouts, make_bias(): return jnp.take(per_offset.T, offsets, axis=1)  238 us
    all_gather x1, waiting for transfers between devices, fetch_mlp(): lax.all_gather(w_down, 'fsdp', axis=0, tiled=True)  87 us
    reduce_scatter x1, waiting for transfers between devices, shards(): lax.psum_scatter(grad_in, 'fsdp', scatter_dimension=0, tiled=True)  67.9 us
    unnamed x2, blocking collectives  54.3 us
    all_gather x1, waiting for transfers between devices, fetch_attention(): lax.all_gather(w_key, 'fsdp', axis=0, tiled=True)  46.9 us
    unnamed x82, local copies, waits for them, and re-layouts  40.1 us
  transfers between devices with their start and end apart: 17, of which 7 were waited for; matrix products, arithmetic and copies ran while one was open for 55% of the time, Pallas kernels for 0%

commit v1 on v0

--- a/solution.py
+++ b/solution.py
@@ -1,6 +1,8 @@
 import jax
 import jax.numpy as jnp
 from jax import lax
+from jax.experimental import pallas as pl
+from jax.experimental.pallas import tpu as pltpu
 from jax.sharding import PartitionSpec as P
 
 HEADS = 16
@@ -273,6 +275,787 @@
     )
 
 
+MESH_ID = pl.DeviceIdType.MESH
+BF = jnp.bfloat16
+F32 = jnp.float32
+WIDTH = 1024
+TOKENS = 128
+NT_DIMS = (((1,), (1,)), ((), ()))
+TN_DIMS = (((0,), (0,)), ((), ()))
+
+
+def dot_nn(left, right):
+    return jnp.dot(left, right, preferred_element_type=F32)
+
+
+def dot_nt(left, right):
+    return lax.dot_general(left, right, NT_DIMS, preferred_element_type=F32)
+
+
+def dot_tn(left, right):
+    return lax.dot_general(left, right, TN_DIMS, preferred_element_type=F32)
+
+
+def rows_at(start, count):
+    return pl.ds(pl.multiple_of(start, count), count)
+
+
+def remote(src, dst, send, recv, device):
+    return pltpu.make_async_remote_copy(
+        src_ref=src, dst_ref=dst, send_sem=send, recv_sem=recv, device_id=device, device_id_type=MESH_ID
+    )
+
+
+def fused_layer(
+    x_in, cot_in, wq_in, wk_in, wv_in, wo_in, wi_in, wd_in, pack_in, bucket_in,
+    out_ref, gin_ref, oqkv, oout, oin, odown, small_ref,
+    XO, CO, GP, XB, COT, N1, NTB, GAL, WQKV, WOUT, WIN, WDOWN,
+    QKV, PROB, BIAS, AT, ACT, GACT, GPRE, GATT, DQKV, DKACC, DVACC, BACC,
+    SA, SG, SO, SN, RA, RG, RO, RN, HID, GH, NTS, GALS,
+    DQ, DO, DI, DD, SIBQ, SIBO, SIBI, SIBD, ZQ, ZO, ZI, ZD, RZQ, RZO, RZI, RZD, FQ, FO, FI, FD,
+    SMALL, RSMALL, PSMALL, RZSMALL,
+    loc, gpx_s, gpx_r, gpz_s, gpz_r, xb_s, xb_r, co_s, co_r, nt_s, nt_r, ga_s, ga_r,
+    a_s, a_r, g_s, g_r, o_s, o_r, n_s, n_r,
+    wx_s, wx_r, wqz_s, wqz_r, wqb_s, wqb_r, wiz_s, wiz_r, wib_s, wib_r, wdz_s, wdz_r, wdb_s, wdb_r,
+    woz_s, woz_r, wob_s, wob_r,
+    sib_s, sib_r, zq_s, zq_r, zo_s, zo_r, zi_s, zi_r, zd_s, zd_r,
+    fq_s, fq_r, fo_s, fo_r, fi_s, fi_r, fd_s, fd_r, sp_s, sp_r, sz_s, sz_r,
+):
+    c = lax.axis_index("ctx")
+    f = lax.axis_index("fsdp")
+    y, k = c // 2, lax.rem(c, 2)
+    z, x = f // 2, lax.rem(f, 2)
+    x1, y1, k1 = 1 - x, 1 - y, 1 - k
+    f1 = 2 * z + x1
+    q = 2 * x + y
+    sib = (2 * y + k1, f)
+    xdev = (c, f1)
+    zs = [lax.rem(z + d, 4) for d in (1, 2, 3)]
+
+    def zdev(target):
+        return (c, 2 * target + x)
+
+    plane = []
+    for i in range(4):
+        ci = lax.rem(c + i, 4)
+        for j, xj in enumerate((x, x1)):
+            if i or j:
+                plane.append((ci, 2 * z + xj))
+
+    barrier = pltpu.get_barrier_semaphore()
+    for device in plane + [zdev(t) for t in zs]:
+        pl.semaphore_signal(barrier, inc=1, device_id=device, device_id_type=MESH_ID)
+    pl.semaphore_wait(barrier, 10)
+
+    def recv(dst, sem):
+        remote(dst, dst, sem, sem, sib).wait_recv()
+
+    def sent(src, sem):
+        remote(src, src, sem, sem, sib).wait_send()
+
+    def gather_send(src, dst, send, got):
+        mine = dst.at[rows_at(c * TOKENS, TOKENS)]
+
+        @pl.when(k == x)
+        def _():
+            pltpu.make_async_copy(src, mine, got.at[c]).start()
+
+        @pl.when(k != x)
+        def _():
+            remote(src, mine, send.at[0], got.at[c], sib).start()
+
+        remote(src, mine, send.at[3], got.at[c], (2 * y1 + x, f1)).start()
+        remote(src, mine, send.at[1], got.at[c], (2 * y + x, f1)).start()
+        remote(src, mine, send.at[2], got.at[c], (2 * y1 + x, f)).start()
+
+    def gather_sent(src, send):
+        @pl.when(k != x)
+        def _():
+            sent(src, send.at[0])
+
+        for i in (1, 2, 3):
+            sent(src, send.at[i])
+
+    def scatter_send(buf, dst, send, got, b):
+        src = buf.at[rows_at(b * TOKENS, TOKENS)]
+        here = (b == c) & (x == k)
+
+        @pl.when(here)
+        def _():
+            pltpu.make_async_copy(src, dst.at[q], got.at[q]).start()
+
+        @pl.when(jnp.logical_not(here))
+        def _():
+            remote(src, dst.at[q], send.at[b], got.at[q], (b, 2 * z + k)).start()
+
+    def scatter_sent(buf, send):
+        for b in range(4):
+
+            @pl.when(jnp.logical_not((c == b) & (x == k)))
+            def _():
+                sent(buf.at[pl.ds(b * TOKENS, TOKENS)], send.at[b])
+
+    def half(fb, kk):
+        return rows_at(fb * 128 + kk * 64, 64)
+
+    own_x = pltpu.make_async_copy(x_in.at[0], XO, loc.at[0])
+    own_x.start()
+    own_c = pltpu.make_async_copy(cot_in.at[0], CO, loc.at[1])
+    own_c.start()
+    own_pack = pltpu.make_async_copy(pack_in, GP.at[f], loc.at[2])
+    own_pack.start()
+    remote(pack_in, GP.at[f], gpx_s, gpx_r, xdev).start()
+    proj = (wq_in, wk_in, wv_in)
+    myrows = pl.ds(pl.multiple_of(128 * f, 128), 128)
+    for w in range(3):
+        for j in range(2):
+            src = proj[w].at[:, pl.ds(pl.multiple_of(128 * (2 * (2 * y + j) + x), 128), 128)]
+            pltpu.make_async_copy(src, WQKV.at[myrows, pl.ds(256 * w + 128 * j, 128)], loc.at[3]).start()
+    for w in range(3):
+        for j in range(2):
+            src = proj[w].at[rows_at(64 * k, 64), pl.ds(pl.multiple_of(128 * (2 * (2 * y + j) + x1), 128), 128)]
+            remote(src, WQKV.at[half(f, k), pl.ds(256 * w + 128 * j, 128)], wx_s.at[0], wx_r.at[0], xdev).start()
+    gather_send(x_in.at[0], XB, xb_s, xb_r)
+    pltpu.make_async_copy(WQKV.at[myrows], WQKV.at[myrows], loc.at[3]).wait()
+    for t in zs:
+        remote(WQKV.at[half(f, k)], WQKV.at[half(f, k)], wqz_s.at[0, t], wqz_r.at[f], zdev(t)).start()
+    for j in range(4):
+        src = wi_in.at[:, pl.ds(pl.multiple_of(512 * (2 * j + x) + 256 * y, 256), 256)]
+        pltpu.make_async_copy(src, WIN.at[myrows, pl.ds(256 * j, 256)], loc.at[4]).start()
+    pltpu.make_async_copy(
+        wd_in.at[rows_at(256 * y, 256)], WDOWN.at[rows_at(256 * z, 256)], loc.at[5]
+    ).start()
+
+    @pl.when(z // 2 == y)
+    def _():
+        pltpu.make_async_copy(wo_in, WOUT.at[rows_at(128 * lax.rem(z, 2), 128)], loc.at[6]).start()
+
+    own_pack.wait()
+    recv(GP.at[f1], gpx_r)
+    for t in zs:
+        remote(GP.at[pl.ds(2 * z, 2)], GP.at[pl.ds(2 * z, 2)], gpz_s.at[t], gpz_r.at[z], zdev(t)).start()
+    for t in zs:
+        recv(GP.at[pl.ds(2 * t, 2)], gpz_r.at[t])
+
+    def row_of(index):
+        return jnp.concatenate([GP[g, index : index + 1, :] for g in range(8)], axis=1)
+
+    lane = lax.broadcasted_iota(jnp.int32, (8, 128), 1)
+    head_row = lax.broadcasted_iota(jnp.int32, (8, 128), 0)
+    head_of = 8 * y + 4 * lax.div(head_row, 2) + 2 * x + lax.rem(head_row, 2)
+    head_mask = (lax.rem(lane, 16) == head_of) & (head_row < 4)
+
+    def bucket_hot(g):
+        index = lax.broadcasted_iota(jnp.int32, (128, WIDTH), 0)
+        wanted = jnp.where(index < 64, 4 * g + lax.div(index, 16), -1)
+        return (bucket_in[0:1, :] == wanted)
+
+    def add_bias(g, total):
+        table = jnp.where(head_mask, jnp.broadcast_to(GP[g, 2:3, :], (8, 128)), 0.0).astype(BF)
+        return total + dot_nn(table, bucket_hot(g).astype(BF))
+
+    offsets = lax.fori_loop(0, 8, add_bias, jnp.zeros((8, WIDTH), F32))
+    for h in range(4):
+        spread = jnp.broadcast_to(offsets[h : h + 1, :], (128, WIDTH))
+        BIAS[h] = pltpu.roll(spread, WIDTH - 127, 1, stride=1, stride_axis=0)
+        BACC[h] = jnp.zeros((128, WIDTH), F32)
+
+    recv(WQKV.at[half(f1, k)], wx_r.at[0])
+    for t in zs:
+        remote(WQKV.at[half(f1, k)], WQKV.at[half(f1, k)], wqz_s.at[1, t], wqz_r.at[f1], zdev(t)).start()
+    remote(WQKV.at[half(f1, k)], WQKV.at[half(f1, k)], wqb_s.at[f1], wqb_r.at[f1], sib).start()
+
+    gain_one = row_of(0)
+
+    def norm_block(i, carry):
+        b = lax.rem(2 * y + i, 4)
+        recv(XB.at[rows_at(b * TOKENS, TOKENS)], xb_r.at[b])
+
+        def chunk(r, inner):
+            rows = rows_at(b * TOKENS + r * 32, 32)
+            values = XB[rows, :].astype(F32)
+            scale = lax.rsqrt(jnp.mean(values * values, axis=-1, keepdims=True) + EPS)
+            N1[rows, :] = (values * scale * gain_one).astype(BF)
+            return inner
+
+        return lax.fori_loop(0, 4, chunk, carry)
+
+    lax.fori_loop(0, 4, norm_block, 0)
+    gather_send(cot_in.at[0], COT, co_s, co_r)
+    for j in range(4):
+        src = wi_in.at[rows_at(64 * k, 64), pl.ds(pl.multiple_of(512 * (2 * j + x1) + 256 * y, 256), 256)]
+        remote(src, WIN.at[half(f, k), pl.ds(256 * j, 256)], wx_s.at[1], wx_r.at[1], xdev).start()
+
+    for t in zs:
+        for xx in (x, x1):
+            piece = WQKV.at[half(2 * t + xx, k)]
+            recv(piece, wqz_r.at[2 * t + xx])
+            remote(piece, piece, wqb_s.at[2 * t + xx], wqb_r.at[2 * t + xx], sib).start()
+
+    out_piece = WOUT.at[rows_at(128 * k, 128)]
+    out_other = WOUT.at[rows_at(128 * k1, 128)]
+
+    @pl.when(z // 2 == y)
+    def _():
+        pltpu.make_async_copy(wo_in, out_piece, loc.at[6]).wait()
+
+    @pl.when(z == c)
+    def _():
+        for t in zs:
+            remote(out_piece, out_piece, woz_s.at[t], woz_r, zdev(t)).start()
+
+    pltpu.make_async_copy(WIN.at[myrows], WIN.at[myrows], loc.at[4]).wait()
+    for t in zs:
+        remote(WIN.at[half(f, k)], WIN.at[half(f, k)], wiz_s.at[0, t], wiz_r.at[f], zdev(t)).start()
+
+    for t in zs:
+        for xx in (x, x1):
+            recv(WQKV.at[half(2 * t + xx, k1)], wqb_r.at[2 * t + xx])
+    recv(WQKV.at[half(f1, k1)], wqb_r.at[f1])
+
+    def project(n, carry):
+        cols = rows_at(256 * n, 256)
+        QKV[:, cols] = dot_nn(N1[...], WQKV[:, cols]).astype(BF)
+        return carry
+
+    lax.fori_loop(0, 3, project, 0)
+
+    recv(WIN.at[half(f1, k)], wx_r.at[1])
+    for t in zs:
+        remote(WIN.at[half(f1, k)], WIN.at[half(f1, k)], wiz_s.at[1, t], wiz_r.at[f1], zdev(t)).start()
+    remote(WIN.at[half(f1, k)], WIN.at[half(f1, k)], wib_s.at[f1], wib_r.at[f1], sib).start()
+
+    @pl.when(z != c)
+    def _():
+        recv(out_piece, woz_r)
+        remote(out_piece, out_piece, wob_s, wob_r, sib).start()
+
+    @pl.when(z != 2 * y + k1)
+    def _():
+        recv(out_other, wob_r)
+
+    low_lanes = lax.broadcasted_iota(jnp.int32, (TOKENS, 128), 1) < 64
+
+    def pick(values, hh):
+        keep = low_lanes if hh == 0 else jnp.logical_not(low_lanes)
+        return jnp.where(keep, values, jnp.zeros_like(values))
+
+    def attend(i, carry):
+        b = lax.rem(2 * y1 + i, 4)
+        rows = rows_at(b * TOKENS, TOKENS)
+        window = rows_at(384 - 128 * b, 128)
+        window = pl.ds(pl.multiple_of(384 - 128 * b, 128), 512)
+        for j in range(2):
+            outs = []
+            for hh in range(2):
+                h = 2 * j + hh
+                query = pick(QKV[rows, 128 * j : 128 * j + 128], hh)
+                scores = dot_nt(query, QKV[:, 256 + 128 * j : 384 + 128 * j]) + BIAS[h, :, window]
+                weights = jnp.exp(scores - jnp.max(scores, axis=-1, keepdims=True))
+                probs = weights * (1.0 / jnp.sum(weights, axis=-1, keepdims=True))
+                PROB[h, rows, :] = probs
+                outs.append(dot_nn(probs.astype(BF), QKV[:, 512 + 128 * j : 640 + 128 * j]))
+            AT[rows, 128 * j : 128 * j + 128] = jnp.where(low_lanes, outs[0], outs[1]).astype(BF)
+        SA[rows, :] = dot_nn(AT[rows, :], WOUT[...]).astype(BF)
+        scatter_send(SA, RA, a_s, a_r, b)
+        return carry
+
+    lax.fori_loop(0, 4, attend, 0)
+
+    down_half = rows_at(256 * z + 128 * k, 128)
+    pltpu.make_async_copy(WDOWN.at[rows_at(256 * z, 256)], WDOWN.at[rows_at(256 * z, 256)], loc.at[5]).wait()
+    for t in zs:
+        remote(WDOWN.at[down_half], WDOWN.at[down_half], wdz_s.at[t], wdz_r.at[z], zdev(t)).start()
+
+    own_x.wait()
+    own_c.wait()
+    gain_two = row_of(1)
+    for s in range(4):
+        recv(RA.at[s], a_r.at[s])
+
+    def home_forward(r, carry):
+        rows = rows_at(r * 32, 32)
+        hidden = XO[rows, :].astype(F32)
+        for s in range(4):
+            hidden = hidden + RA[s, rows, :].astype(F32)
+        HID[rows, :] = hidden
+        scale = lax.rsqrt(jnp.mean(hidden * hidden, axis=-1, keepdims=True) + EPS)
+        NTS[rows, :] = (hidden * scale * gain_two).astype(BF)
+        return carry
+
+    lax.fori_loop(0, 4, home_forward, 0)
+    gather_send(NTS, NTB, nt_s, nt_r)
+
+    for t in zs:
+        for xx in (x, x1):
+            piece = WIN.at[half(2 * t + xx, k)]
+            recv(piece, wiz_r.at[2 * t + xx])
+            remote(piece, piece, wib_s.at[2 * t + xx], wib_r.at[2 * t + xx], sib).start()
+    for t in zs:
+        piece = WDOWN.at[rows_at(256 * t + 128 * k, 128)]
+        recv(piece, wdz_r.at[t])
+        remote(piece, piece, wdb_s.at[t], wdb_r.at[t], sib).start()
+    for t in zs:
+        recv(WDOWN.at[rows_at(256 * t + 128 * k1, 128)], wdb_r.at[t])
+        for xx in (x, x1):
+            recv(WIN.at[half(2 * t + xx, k1)], wib_r.at[2 * t + xx])
+    recv(WIN.at[half(f1, k1)], wib_r.at[f1])
+
+    for b in range(4):
+        recv(COT.at[pl.ds(b * TOKENS, TOKENS)], co_r.at[b])
+
+    def back_act(n, carry):
+        cols = rows_at(256 * n, 256)
+        GACT[:, cols] = dot_nt(COT[...], WDOWN[cols, :])
+        return carry
+
+    lax.fori_loop(0, 4, back_act, 0)
+
+    def feed(i, carry):
+        yy = lax.rem(y + i, 2)
+        rows = rows_at(256 * yy, 256)
+        for b in (2 * yy, 2 * yy + 1):
+            recv(NTB.at[rows_at(b * TOKENS, TOKENS)], nt_r.at[b])
+
+        def hidden_units(n, inner):
+            cols = rows_at(256 * n, 256)
+            pre = dot_nn(NTB[rows, :], WIN[:, cols])
+            cdf = 0.5 * (1.0 + lax.erf(pre * 0.7071067811865476))
+            ACT[rows, cols] = (pre * cdf).astype(BF)
+            slope = cdf + pre * jnp.exp(-0.5 * pre * pre) * 0.3989422804014327
+            GPRE[rows, cols] = (GACT[rows, cols] * slope).astype(BF)
+            return inner
+
+        lax.fori_loop(0, 4, hidden_units, 0)
+
+        def back_normed(n, inner):
+            cols = rows_at(256 * n, 256)
+            SG[rows, cols] = dot_nt(GPRE[rows, :], WIN[cols, :]).astype(BF)
+            return inner
+
+        lax.fori_loop(0, 4, back_normed, 0)
+        scatter_send(SG, RG, g_s, g_r, 2 * yy)
+        scatter_send(SG, RG, g_s, g_r, 2 * yy + 1)
+        return carry
+
+    lax.fori_loop(0, 2, feed, 0)
+
+    def down_project(n, carry):
+        cols = rows_at(256 * n, 256)
+        SO[:, cols] = dot_nn(ACT[...], WDOWN[:, cols]).astype(BF)
+        return carry
+
+    lax.fori_loop(0, 4, down_project, 0)
+
+    def grad_down(m, carry):
+        tile = dot_tn(ACT[:, rows_at(256 * m, 256)], COT[...]).astype(BF)
+        DD[0, m] = tile[0:128]
+        DD[1, m] = tile[128:256]
+        return carry
+
+    lax.fori_loop(0, 4, grad_down, 0)
+    remote(DD.at[k1], SIBD, sib_s.at[0], sib_r.at[0], sib).start()
+
+    def grad_in(m, carry):
+        tile = dot_tn(NTB[:, rows_at(256 * m, 256)], GPRE[...]).astype(BF)
+        for part in range(2):
+            DI[0, 2 * m + part] = tile[128 * part : 128 * part + 64]
+            DI[1, 2 * m + part] = tile[128 * part + 64 : 128 * part + 128]
+        return carry
+
+    lax.fori_loop(0, 4, grad_in, 0)
+    remote(DI.at[k1], SIBI, sib_s.at[1], sib_r.at[1], sib).start()
+    recv(SIBD, sib_r.at[0])
+
+    def join_down(m, carry):
+        ZD[m] = (DD[k, m].astype(F32) + SIBD[m].astype(F32)).astype(BF)
+        return carry
+
+    lax.fori_loop(0, 4, join_down, 0)
+    for t in zs:
+        remote(ZD.at[t], RZD.at[z], zd_s.at[t], zd_r.at[z], zdev(t)).start()
+
+    for s in range(4):
+        recv(RG.at[s], g_r.at[s])
+
+    def home_back(r, total):
+        rows = rows_at(r * 32, 32)
+        grad = RG[0, rows, :].astype(F32)
+        for s in range(1, 4):
+            grad = grad + RG[s, rows, :].astype(F32)
+        hidden = HID[rows, :]
+        scale = lax.rsqrt(jnp.mean(hidden * hidden, axis=-1, keepdims=True) + EPS)
+        scaled = grad * gain_two
+        inner = jnp.mean(scaled * hidden, axis=-1, keepdims=True)
+        back = CO[rows, :].astype(F32) + scale * scaled - hidden * (scale * scale * scale * inner)
+        GH[rows, :] = back
+        GALS[rows, :] = back.astype(BF)
+        return total + jnp.sum((grad * hidden * scale).reshape(4, 8, WIDTH), axis=0)
+
+    mlp_gain_grad = lax.fori_loop(0, 4, home_back, jnp.zeros((8, WIDTH), F32))
+    gather_send(GALS, GAL, ga_s, ga_r)
+    for b in range(4):
+        scatter_send(SO, RO, o_s, o_r, lax.rem(2 * y1 + b, 4))
+    mlp_gain_grad = jnp.sum(mlp_gain_grad, axis=0, keepdims=True)
+    for g in range(8):
+        SMALL[g] = jnp.zeros((8, 128), F32)
+        SMALL[g, 1:2, :] = mlp_gain_grad[:, 128 * g : 128 * g + 128]
+
+    recv(SIBI, sib_r.at[1])
+
+    def join_in(m, carry):
+        ZI[m] = (DI[k, m].astype(F32) + SIBI[m].astype(F32)).astype(BF)
+        return carry
+
+    lax.fori_loop(0, 8, join_in, 0)
+    for t in zs:
+        remote(ZI.at[pl.ds(2 * t, 2)], RZI.at[z], zi_s.at[t], zi_r.at[z], zdev(t)).start()
+
+    DKACC[...] = jnp.zeros_like(DKACC)
+    DVACC[...] = jnp.zeros_like(DVACC)
+
+    def attend_back(i, carry):
+        b = lax.rem(2 * y + i, 4)
+        rows = rows_at(b * TOKENS, TOKENS)
+        window = pl.ds(pl.multiple_of(384 - 128 * b, 128), 512)
+        recv(GAL.at[rows], ga_r.at[b])
+        GATT[...] = dot_nt(GAL[rows, :], WOUT[...]).astype(BF)
+        for j in range(2):
+            pair = slice(128 * j, 128 * j + 128)
+            keys = QKV[:, 256 + 128 * j : 384 + 128 * j]
+            values = QKV[:, 512 + 128 * j : 640 + 128 * j]
+            outs = []
+            for hh in range(2):
+                h = 2 * j + hh
+                query = pick(QKV[rows, pair], hh)
+                grad_att = pick(GATT[:, pair], hh)
+                probs = PROB[h, rows, :]
+                grad_probs = dot_nt(grad_att, values)
+                inner = jnp.sum(probs * grad_probs, axis=-1, keepdims=True)
+                grad_scores = (probs * (grad_probs - inner)).astype(BF)
+                BACC[h, :, window] = BACC[h, :, window] + grad_scores.astype(F32)
+                outs.append(dot_nn(grad_scores, keys))
+                DKACC[:, pair] = DKACC[:, pair] + dot_tn(grad_scores, query)
+                DVACC[:, pair] = DVACC[:, pair] + dot_tn(probs.astype(BF), grad_att)
+            DQKV[rows, pair] = jnp.where(low_lanes, outs[0], outs[1]).astype(BF)
+        return carry
+
+    lax.fori_loop(0, 4, attend_back, 0)
+    DQKV[:, 256:512] = DKACC[...].astype(BF)
+    DQKV[:, 512:768] = DVACC[...].astype(BF)
+
+    def back_project(i, carry):
+        yy = lax.rem(y1 + i, 2)
+        rows = rows_at(256 * yy, 256)
+        SN[rows, :] = dot_nt(DQKV[rows, :], WQKV[...]).astype(BF)
+        scatter_send(SN, RN, n_s, n_r, 2 * yy)
+        scatter_send(SN, RN, n_s, n_r, 2 * yy + 1)
+        return carry
+
+    lax.fori_loop(0, 2, back_project, 0)
+
+    def grad_proj(m, carry):
+        tile = dot_tn(N1[:, rows_at(256 * m, 256)], DQKV[...]).astype(BF)
+        for part in range(2):
+            DQ[0, 2 * m + part] = tile[128 * part : 128 * part + 64]
+            DQ[1, 2 * m + part] = tile[128 * part + 64 : 128 * part + 128]
+        return carry
+
+    lax.fori_loop(0, 4, grad_proj, 0)
+    remote(DQ.at[k1], SIBQ, sib_s.at[2], sib_r.at[2], sib).start()
+
+    def grad_out_rows(m, carry):
+        DO[m] = dot_tn(AT[:, rows_at(128 * m, 128)], GAL[...]).astype(BF)
+        return carry
+
+    lax.fori_loop(0, 2, grad_out_rows, 0)
+    remote(DO.at[k1], SIBO, sib_s.at[3], sib_r.at[3], sib).start()
+    recv(SIBQ, sib_r.at[2])
+
+    def join_proj(m, carry):
+        ZQ[m] = (DQ[k, m].astype(F32) + SIBQ[m].astype(F32)).astype(BF)
+        return carry
+
+    lax.fori_loop(0, 8, join_proj, 0)
+    for t in zs:
+        remote(ZQ.at[pl.ds(2 * t, 2)], RZQ.at[z], zq_s.at[t], zq_r.at[z], zdev(t)).start()
+    recv(SIBO, sib_r.at[3])
+    ZO[...] = (DO[k].astype(F32) + SIBO[...].astype(F32)).astype(BF)
+
+    @pl.when(z != c)
+    def _():
+        remote(ZO, RZO.at[z], zo_s, zo_r.at[z], zdev(c)).start()
+
+    for t in zs:
+        recv(RZD.at[t], zd_r.at[t])
+    total = ZD[z].astype(F32)
+    for t in zs:
+        total = total + RZD[t].astype(F32)
+    FD[...] = total.astype(BF)
+    down_rows = odown.at[rows_at(128 * c, 128)]
+    pltpu.make_async_copy(FD, down_rows, fd_r.at[c]).start()
+    for i in range(1, 4):
+        ci = lax.rem(c + i, 4)
+        remote(FD, down_rows, fd_s.at[i], fd_r.at[c], (ci, f)).start()
+    for t in zs:
+        recv(RZI.at[t], zi_r.at[t])
+    for xx in range(2):
+        total = ZI[2 * z + xx].astype(F32)
+        for t in zs:
+            total = total + RZI[t, xx].astype(F32)
+        for j in range(4):
+            FI[xx, j] = total[:, 256 * j : 256 * j + 256].astype(BF)
+    in_rows = oin.at[:, q, rows_at(64 * k, 64), :]
+    pltpu.make_async_copy(FI.at[x], in_rows, fi_r.at[c, x]).start()
+    for i in range(4):
+        ci = lax.rem(c + i, 4)
+        for j, xj in enumerate((x, x1)):
+            if i or j:
+                remote(FI.at[xj], in_rows, fi_s.at[i, j], fi_r.at[c, x], (ci, 2 * z + xj)).start()
+
+    for s in range(4):
+        recv(RO.at[s], o_r.at[s])
+
+    def home_out(r, carry):
+        rows = rows_at(r * 32, 32)
+        result = HID[rows, :]
+        for s in range(4):
+            result = result + RO[s, rows, :].astype(F32)
+        out_ref[0, rows, :] = result.astype(BF)
+        return carry
+
+    lax.fori_loop(0, 4, home_out, 0)
+    for s in range(4):
+        recv(RN.at[s], n_r.at[s])
+
+    def home_inputs(r, total):
+        rows = rows_at(r * 32, 32)
+        grad = RN[0, rows, :].astype(F32)
+        for s in range(1, 4):
+            grad = grad + RN[s, rows, :].astype(F32)
+        values = XO[rows, :].astype(F32)
+        scale = lax.rsqrt(jnp.mean(values * values, axis=-1, keepdims=True) + EPS)
+        scaled = grad * gain_one
+        inner = jnp.mean(scaled * values, axis=-1, keepdims=True)
+        back = GH[rows, :] + scale * scaled - values * (scale * scale * scale * inner)
+        gin_ref[0, rows, :] = back.astype(BF)
+        return total + jnp.sum((grad * values * scale).reshape(4, 8, WIDTH), axis=0)
+
+    attn_gain_grad = lax.fori_loop(0, 4, home_inputs, jnp.zeros((8, WIDTH), F32))
+    attn_gain_grad = jnp.sum(attn_gain_grad, axis=0, keepdims=True)
+
+    head_sums = []
+    for h in range(4):
+        rest = BACC[h]
+        count = 64
+        while count >= 8:
+            rest = pltpu.roll(rest[0:count, :], count, 1) + rest[count : 2 * count, :]
+            count //= 2
+        for bit in (1, 2, 4):
+            shift_row = 7 - lax.broadcasted_iota(jnp.int32, (8, WIDTH), 0)
+            rest = jnp.where(lax.rem(lax.div(shift_row, bit), 2) == 1, pltpu.roll(rest, bit, 1), rest)
+        head_sums.append(jnp.sum(rest, axis=0, keepdims=True))
+    head_sums = jnp.concatenate(head_sums + [jnp.zeros((4, WIDTH), F32)], axis=0)
+    coarse = head_sums.astype(BF)
+    split_sums = jnp.concatenate([coarse, (head_sums - coarse.astype(F32)).astype(BF)], axis=0)
+
+    both_masks = jnp.concatenate([head_mask.astype(F32)] * 2, axis=0) > 0.5
+
+    def bucket_sums(g, carry):
+        sums = dot_nt(split_sums, bucket_hot(g).astype(BF))
+        SMALL[g, 2:3, :] = jnp.sum(jnp.where(both_masks, sums, 0.0), axis=0, keepdims=True)
+        return carry
+
+    lax.fori_loop(0, 8, bucket_sums, 0)
+    for g in range(8):
+        SMALL[g, 0:1, :] = attn_gain_grad[:, 128 * g : 128 * g + 128]
+
+    for i in range(4):
+        ci = lax.rem(c + i, 4)
+        for j, xj in enumerate((x, x1)):
+            if i or j:
+                remote(SMALL, RSMALL.at[2 * c + x], sp_s.at[i, j], sp_r.at[2 * c + x], (ci, 2 * z + xj)).start()
+
+    for t in zs:
+        recv(RZQ.at[t], zq_r.at[t])
+    for xx in range(2):
+        total = ZQ[2 * z + xx].astype(F32)
+        for t in zs:
+            total = total + RZQ[t, xx].astype(F32)
+        FQ[xx] = total.astype(BF)
+    proj_rows = oqkv.at[q, rows_at(64 * k, 64), :]
+    pltpu.make_async_copy(FQ.at[x], proj_rows, fq_r.at[c, x]).start()
+    for i in range(4):
+        ci = lax.rem(c + i, 4)
+        for j, xj in enumerate((x, x1)):
+            if i or j:
+                remote(FQ.at[xj], proj_rows, fq_s.at[i, j], fq_r.at[c, x], (ci, 2 * z + xj)).start()
+
+    @pl.when(z == c)
+    def _():
+        for t in zs:
+            recv(RZO.at[t], zo_r.at[t])
+        total = ZO[...].astype(F32)
+        for t in zs:
+            total = total + RZO[t].astype(F32)
+        FO[...] = total.astype(BF)
+        pltpu.make_async_copy(FO, oout, fo_r).start()
+        for i in range(1, 4):
+            remote(FO, oout, fo_s.at[i], fo_r, (lax.rem(c + i, 4), f)).start()
+
+    plane_sum = SMALL[...]
+    for i in range(4):
+        ci = lax.rem(c + i, 4)
+        for j, xj in enumerate((x, x1)):
+            if i or j:
+                recv(RSMALL.at[2 * ci + xj], sp_r.at[2 * ci + xj])
+                plane_sum = plane_sum + RSMALL[2 * ci + xj]
+    PSMALL[...] = plane_sum
+    for t in zs:
+        remote(PSMALL.at[2 * t + x], RZSMALL.at[z], sz_s.at[t], sz_r.at[z], zdev(t)).start()
+    total = PSMALL[f]
+    for t in zs:
+        recv(RZSMALL.at[t], sz_r.at[t])
+        total = total + RZSMALL[t]
+    small_ref[...] = total
+
+    recv(oout, fo_r)
+    for i in range(4):
+        ci = lax.rem(c + i, 4)
+        recv(odown.at[rows_at(128 * ci, 128)], fd_r.at[ci])
+        for xj in (x, x1):
+            qi = 2 * xj + ci // 2
+            ki = lax.rem(ci, 2)
+            recv(oin.at[:, qi, rows_at(64 * ki, 64), :], fi_r.at[ci, xj])
+            recv(oqkv.at[qi, rows_at(64 * ki, 64), :], fq_r.at[ci, xj])
+
+    sent(pack_in, gpx_s)
+    gather_sent(x_in.at[0], xb_s)
+    gather_sent(cot_in.at[0], co_s)
+    gather_sent(NTS, nt_s)
+    gather_sent(GALS, ga_s)
+    scatter_sent(SA, a_s)
+    scatter_sent(SG, g_s)
+    scatter_sent(SO, o_s)
+    scatter_sent(SN, n_s)
+    sent(WQKV.at[half(f, k)], wx_s.at[0])
+    sent(WIN.at[half(f, k)], wx_s.at[1])
+    sent(WQKV.at[half(f1, k)], wqb_s.at[f1])
+    sent(WIN.at[half(f1, k)], wib_s.at[f1])
+    for t in zs:
+        sent(GP.at[pl.ds(2 * z, 2)], gpz_s.at[t])
+        for r, own in enumerate((f, f1)):
+            sent(WQKV.at[half(own, k)], wqz_s.at[r, t])
+            sent(WIN.at[half(own, k)], wiz_s.at[r, t])
+        for xx in (x, x1):
+            sent(WQKV.at[half(2 * t + xx, k)], wqb_s.at[2 * t + xx])
+            sent(WIN.at[half(2 * t + xx, k)], wib_s.at[2 * t + xx])
+        sent(WDOWN.at[down_half], wdz_s.at[t])
+        sent(WDOWN.at[rows_at(256 * t + 128 * k, 128)], wdb_s.at[t])
+        sent(ZD.at[t], zd_s.at[t])
+        sent(ZI.at[pl.ds(2 * t, 2)], zi_s.at[t])
+        sent(ZQ.at[pl.ds(2 * t, 2)], zq_s.at[t])
+        sent(PSMALL.at[2 * t + x], sz_s.at[t])
+
+    @pl.when(z == c)
+    def _():
+        for t in zs:
+            sent(out_piece, woz_s.at[t])
+        for i in range(1, 4):
+            sent(FO, fo_s.at[i])
+
+    @pl.when(z != c)
+    def _():
+        sent(out_piece, wob_s)
+        sent(ZO, zo_s)
+
+    sent(DD.at[k1], sib_s.at[0])
+    sent(DI.at[k1], sib_s.at[1])
+    sent(DQ.at[k1], sib_s.at[2])
+    sent(DO.at[k1], sib_s.at[3])
+    for i in range(1, 4):
+        sent(FD, fd_s.at[i])
+    for i in range(4):
+        for j, xj in enumerate((x, x1)):
+            if i or j:
+                sent(SMALL, sp_s.at[i, j])
+                sent(FI.at[xj], fi_s.at[i, j])
+                sent(FQ.at[xj], fq_s.at[i, j])
+
+
+def plane_shards(
+    inputs, cotangent, w_query, w_key, w_value, w_out, w_in, w_down, gain_attn, gain_mlp, rel_bias, buckets
+):
+    pack = jnp.concatenate(
+        [
+            gain_attn.astype(F32)[None],
+            gain_mlp.astype(F32)[None],
+            jnp.pad(rel_bias.astype(F32), (0, 64))[None],
+            jnp.zeros((5, 128), F32),
+        ],
+        axis=0,
+    )
+    bucket_row = jnp.pad(buckets, (0, 1))[None]
+    vm = pltpu.VMEM
+    dma = pltpu.SemaphoreType.DMA
+    block = lambda kind: vm((TOKENS, WIDTH), kind)
+    tokens = lambda width, kind: vm((512, width), kind)
+    scratch = [
+        block(BF), block(BF), vm((8, 8, 128), F32),
+        tokens(1024, BF), tokens(1024, BF), tokens(1024, BF), tokens(1024, BF), tokens(1024, BF),
+        vm((1024, 768), BF), vm((256, 1024), BF), vm((1024, 1024), BF), vm((1024, 1024), BF),
+        tokens(768, BF), vm((4, 512, 512), F32), vm((4, 128, 1024), F32), tokens(256, BF),
+        tokens(1024, BF), tokens(1024, F32), tokens(1024, BF),
+        vm((128, 256), BF), tokens(768, BF), tokens(256, F32), tokens(256, F32), vm((4, 128, 1024), F32),
+        tokens(1024, BF), tokens(1024, BF), tokens(1024, BF), tokens(1024, BF),
+        vm((4, 128, 1024), BF), vm((4, 128, 1024), BF), vm((4, 128, 1024), BF), vm((4, 128, 1024), BF),
+        block(F32), block(F32), block(BF), block(BF),
+        vm((2, 8, 64, 768), BF), vm((2, 128, 1024), BF), vm((2, 8, 64, 1024), BF), vm((2, 4, 128, 1024), BF),
+        vm((8, 64, 768), BF), vm((128, 1024), BF), vm((8, 64, 1024), BF), vm((4, 128, 1024), BF),
+        vm((8, 64, 768), BF), vm((128, 1024), BF), vm((8, 64, 1024), BF), vm((4, 128, 1024), BF),
+        vm((4, 2, 64, 768), BF), vm((4, 128, 1024), BF), vm((4, 2, 64, 1024), BF), vm((4, 128, 1024), BF),
+        vm((2, 64, 768), BF), vm((128, 1024), BF), vm((2, 4, 64, 256), BF), vm((128, 1024), BF),
+        vm((8, 8, 128), F32), vm((8, 8, 8, 128), F32), vm((8, 8, 128), F32), vm((4, 8, 128), F32),
+        dma((7,)), dma, dma, dma((4,)), dma((4,)),
+        dma((4,)), dma((4,)), dma((4,)), dma((4,)), dma((4,)), dma((4,)), dma((4,)), dma((4,)),
+        dma((4,)), dma((4,)), dma((4,)), dma((4,)), dma((4,)), dma((4,)), dma((4,)), dma((4,)),
+        dma((2,)), dma((2,)), dma((2, 4)), dma((8,)), dma((8,)), dma((8,)),
+        dma((2, 4)), dma((8,)), dma((8,)), dma((8,)), dma((4,)), dma((4,)), dma((4,)), dma((4,)),
+        dma((4,)), dma, dma, dma,
+        dma((4,)), dma((4,)), dma((4,)), dma((4,)), dma, dma((4,)), dma((4,)), dma((4,)), dma((4,)), dma((4,)),
+        dma((4, 2)), dma((4, 2)), dma((4,)), dma, dma((4, 2)), dma((4, 2)), dma((4,)), dma((4,)),
+        dma((4, 2)), dma((8,)), dma((4,)), dma((4,)),
+    ]
+    anywhere = pl.BlockSpec(memory_space=pl.ANY)
+    in_vmem = pl.BlockSpec(memory_space=pltpu.VMEM)
+    shape = jax.ShapeDtypeStruct
+    output, grad_inputs, proj, out, hidden, down, small = pl.pallas_call(
+        fused_layer,
+        out_shape=(
+            shape((1, TOKENS, WIDTH), BF),
+            shape((1, TOKENS, WIDTH), BF),
+            shape((4, 128, 768), BF),
+            shape((128, 1024), BF),
+            shape((4, 4, 128, 256), BF),
+            shape((512, 1024), BF),
+            shape((8, 128), F32),
+        ),
+        in_specs=[anywhere] * 9 + [in_vmem],
+        out_specs=(in_vmem, in_vmem, anywhere, anywhere, anywhere, anywhere, in_vmem),
+        scratch_shapes=scratch,
+        compiler_params=pltpu.CompilerParams(
+            collective_id=0, has_side_effects=True, vmem_limit_bytes=63 << 20
+        ),
+        cost_estimate=pl.CostEstimate(flops=11 * 10**9, bytes_accessed=16 * 2**20, transcendentals=3 * 2**20),
+    )(inputs, cotangent, w_query, w_key, w_value, w_out, w_in, w_down, pack, bucket_row)
+    proj = proj.reshape(2, 2, 128, 3, 2, 128).transpose(3, 2, 1, 4, 0, 5).reshape(3, 128, 1024).astype(F32)
+    hidden = hidden.transpose(2, 0, 1, 3).reshape(128, 4096).astype(F32)
+    return (
+        output, grad_inputs, proj[0], proj[1], proj[2], out.astype(F32), hidden, down.astype(F32),
+        small[0], small[1], small[2, :64],
+    )
+
+
 def solution(mesh):
     placed = (
         P("fsdp", "ctx", None),
@@ -288,8 +1071,9 @@
         P("fsdp"),
         P(),
     )
+    by_planes = mesh.shape["ctx"] == 4 and mesh.shape["fsdp"] == 8
     return jax.shard_map(
-        shards,
+        plane_shards if by_planes else shards,
         mesh=mesh,
         in_specs=placed,
         out_specs=(

time: 1610 us -> 221 us (0.14)
  the two profiles are of different devices: /device:TPU:0 before, /device:TPU:27 now
where the time goes in v1:
time: 221 us
  Pallas kernels  198 us (90%)
  local copies, waits for them, and re-layouts  17.4 us (8%)
  other arithmetic  4.62 us (2%)
    pallas_call x1, Pallas kernels, plane_shards(): pl.pallas_call(fused_layer, out_shape=(shape((1, TOKENS, WIDTH), BF), sha...  198 us

profile of v1, /device:TPU:27, one launch (start us, length us, event | category | flops | bytes accessed | tf_op | source)
XLA Modules:
  0.0 220.6 jit_solution(2648758400068623206)
XLA Ops:
  0.6 0.7 bitcast_convert_fusion
  1.3 0.1 pad.14.clone
  1.4 0.7 bitcast_convert_fusion.2
  2.1 0.7 maximum_maximum_fusion.pack_in
  2.7 1.3 pad.10
  4.0 197.8 %shard_map.203 = (bf16[1,128,1024]{2,1,0:T(8,128)(2,1)}, bf16[1,128,1024]{2,1,0:T(8,128)(2,1)}, bf16[4,128,768]{2,1,0:T(8,128)(2,1)}, bf16[128,1024]{1,0:T(8,128...) custom-call(bf16[1,128,1024]{2,1,0:T(8,128)(2,1)} %x_in.1, ...), custom_call_target="tpu_custom_call" | custom-call | flops 11000000512 | bytes 16777216 | tf_op jit(solution)/shard_map/pallas_call | solution.py:1032
  201.8 2.0 reshape.40
  203.9 0.5 fusion
  204.4 0.4 copy.26
  204.8 1.2 squeeze.18
  206.1 0.4 copy.27
  206.5 0.0 copy-start.1
  206.5 1.2 squeeze.19
  207.7 0.4 copy.28
  208.1 1.2 squeeze.20
  209.3 1.3 slice_bitcast_fusion.1
  210.6 1.2 slice_bitcast_fusion
  211.8 0.0 copy-done.1
  211.8 0.2 convert_bitcast_fusion
  212.0 1.8 copy.29
  213.8 0.0 copy-start
  213.8 3.0 %copy.30 = f32[128,4096]{1,0:T(8,128)} copy(f32[128,4096]{0,1:T(8,128)} %bitcast.20) | data formatting | bytes 4194304
  216.8 0.0 copy-start.2
  216.8 0.0 copy-done
  216.8 0.0 copy-start.3
  216.8 1.6 convert_element_type.37
  218.4 0.0 copy-done.2
  218.4 0.8 convert_element_type.33
  219.2 0.0 copy-done.4
  219.2 0.7 copy.33
  219.9 0.0 copy-done.3
  219.9 0.7 copy.34
  (2 shorter events, 0.0 us)
Async XLA Ops:
  206.5 5.3 %copy-start.1 = (bf16[4,4,128,256]{3,2,1,0:T(8,128)(2,1)S(1)}, bf16[4,4,128,256]{3,2,1,0:T(8,128)(2,1)}, u32[]{:S(2)}) copy-start(bf16[4,4,128,256]{3,2,1,0:T(8,128)(2,1)} %get-tuple-element.22) | copy-start | bytes 3145732
  213.8 3.0 %copy-start = (bf16[512,1024]{1,0:T(8,128)(2,1)S(1)}, bf16[512,1024]{1,0:T(8,128)(2,1)}, u32[]{:S(2)}) copy-start(bf16[512,1024]{1,0:T(8,128)(2,1)} %get-tuple-element.23) | copy-start | bytes 3145732
  216.8 1.6 copy-start.2
  216.8 2.4 %copy-start.4 = (bf16[1,128,1024]{2,1,0:T(8,128)(2,1)S(1)}, bf16[1,128,1024]{2,1,0:T(8,128)(2,1)}, u32[]{:S(2)}) copy-start(bf16[1,128,1024]{2,1,0:T(8,128)(2,1)} %get-tuple-element.54) | copy-start | bytes 786436
  216.8 3.1 %copy-start.3 = (bf16[1,128,1024]{2,1,0:T(8,128)(2,1)S(1)}, bf16[1,128,1024]{2,1,0:T(8,128)(2,1)}, u32[]{:S(2)}) copy-start(bf16[1,128,1024]{2,1,0:T(8,128)(2,1)} %get-tuple-element.55) | copy-start | bytes 786436

commit v2 on v1

--- a/solution.py
+++ b/solution.py
@@ -310,16 +310,16 @@
     x_in, cot_in, wq_in, wk_in, wv_in, wo_in, wi_in, wd_in, pack_in, bucket_in,
     out_ref, gin_ref, oqkv, oout, oin, odown, small_ref,
     XO, CO, GP, XB, COT, N1, NTB, GAL, WQKV, WOUT, WIN, WDOWN,
-    QKV, PROB, BIAS, AT, ACT, GACT, GPRE, GATT, DQKV, DKACC, DVACC, BACC,
+    QKV, PROB, PLOW, BIAS, AT, ACT, SLOPE, GPRE, GATT, DQKV, DS, BACC,
     SA, SG, SO, SN, RA, RG, RO, RN, HID, GH, NTS, GALS,
-    DQ, DO, DI, DD, SIBQ, SIBO, SIBI, SIBD, ZQ, ZO, ZI, ZD, RZQ, RZO, RZI, RZD, FQ, FO, FI, FD,
+    DQ, DO, DI, DD, SIBQ, SIBO, SIBI, SIBD, ZQ, ZO, ZI, ZD, RZQ, RZO, REI, RED, RCI, RCD, FQ, FO, FI, FD,
     SMALL, RSMALL, PSMALL, RZSMALL,
     loc, gpx_s, gpx_r, gpz_s, gpz_r, xb_s, xb_r, co_s, co_r, nt_s, nt_r, ga_s, ga_r,
     a_s, a_r, g_s, g_r, o_s, o_r, n_s, n_r,
-    wx_s, wx_r, wqz_s, wqz_r, wqb_s, wqb_r, wiz_s, wiz_r, wib_s, wib_r, wdz_s, wdz_r, wdb_s, wdb_r,
-    woz_s, woz_r, wob_s, wob_r,
-    sib_s, sib_r, zq_s, zq_r, zo_s, zo_r, zi_s, zi_r, zd_s, zd_r,
-    fq_s, fq_r, fo_s, fo_r, fi_s, fi_r, fd_s, fd_r, sp_s, sp_r, sz_s, sz_r,
+    wx_s, wx_r, wqz_s, wqf_s, wqz_r, wqb_s, wqb_r, wiz_s, wif_s, wiz_r, wib_s, wib_r,
+    wdz_s, wdf_s, wdz_r, wdb_s, wdb_r, woz_s, woz_r, wob_s, wob_r,
+    sib_s, sib_r, zq_s, zq_r, zv_s, zv_r, zo_s, zo_r, zi_s, zie_s, zi_r, zic_r, zd_s, zde_s, zd_r, zdc_r,
+    fq_s, fqb_s, fq_r, fo_s, fo_r, fi_s, fib_s, fi_r, fd_s, fd_r, sp_s, sp_r, sz_s, sz_r,
 ):
     c = lax.axis_index("ctx")
     f = lax.axis_index("fsdp")
@@ -331,6 +331,12 @@
     sib = (2 * y + k1, f)
     xdev = (c, f1)
     zs = [lax.rem(z + d, 4) for d in (1, 2, 3)]
+    near = z + 1 - 2 * lax.rem(z, 2)
+    other = 2 - 2 * (z // 2)
+    others = (other, other + 1)
+    far = 2 - z // 2
+    middle = (z == 1) | (z == 2)
+    at_end = jnp.logical_not(middle)
 
     def zdev(target):
         return (c, 2 * target + x)
@@ -353,28 +359,54 @@
     def sent(src, sem):
         remote(src, src, sem, sem, sib).wait_send()
 
+    def block_half(buf, b, h):
+        return buf.at[rows_at(b * TOKENS + 64 * h, 64)]
+
     def gather_send(src, dst, send, got):
-        mine = dst.at[rows_at(c * TOKENS, TOKENS)]
-
-        @pl.when(k == x)
-        def _():
-            pltpu.make_async_copy(src, mine, got.at[c]).start()
-
-        @pl.when(k != x)
-        def _():
-            remote(src, mine, send.at[0], got.at[c], sib).start()
-
-        remote(src, mine, send.at[3], got.at[c], (2 * y1 + x, f1)).start()
-        remote(src, mine, send.at[1], got.at[c], (2 * y + x, f1)).start()
-        remote(src, mine, send.at[2], got.at[c], (2 * y1 + x, f)).start()
-
-    def gather_sent(src, send):
-        @pl.when(k != x)
-        def _():
-            sent(src, send.at[0])
-
-        for i in (1, 2, 3):
-            sent(src, send.at[i])
+        for h in range(2):
+            half_src = src.at[pl.ds(64 * h, 64)]
+            remote(half_src, block_half(dst, c, h), send.at[1, h], got.at[c, h], (2 * y + x, f1)).start()
+        for h in (1, 0):
+            half_src = src.at[pl.ds(64 * h, 64)]
+            remote(half_src, block_half(dst, c, h), send.at[2, h], got.at[c, h], (2 * y1 + x, f)).start()
+        for h in range(2):
+            half_src = src.at[pl.ds(64 * h, 64)]
+
+            @pl.when(k == x)
+            def _():
+                pltpu.make_async_copy(half_src, block_half(dst, c, h), got.at[c, h]).start()
+
+            @pl.when(k != x)
+            def _():
+                remote(half_src, block_half(dst, c, h), send.at[0, h], got.at[c, h], sib).start()
+
+    same = 1 - lax.rem(x + k, 2)
+    pass_y = y + same * (1 - 2 * y)
+    pass_to = (same * c + (1 - same) * (2 * y1 + k), same * f1 + (1 - same) * f)
+
+    def gather_pass(dst, send, got):
+        for i in range(2):
+            piece = block_half(dst, 2 * pass_y + i, same)
+            recv(piece, got.at[2 * pass_y + i, same])
+            remote(piece, piece, send.at[3, i], got.at[2 * pass_y + i, same], pass_to).start()
+
+    def gather_wait(dst, got, b):
+        for h in range(2):
+
+            @pl.when(jnp.logical_not((b // 2 == pass_y) & (same == h)))
+            def _():
+                recv(block_half(dst, b, h), got.at[b, h])
+
+    def gather_sent(src, dst, send):
+        for h in range(2):
+            half_src = src.at[pl.ds(64 * h, 64)]
+            sent(half_src, send.at[1, h])
+            sent(half_src, send.at[2, h])
+            sent(block_half(dst, 2 * pass_y + h, same), send.at[3, h])
+
+            @pl.when(k != x)
+            def _():
+                sent(half_src, send.at[0, h])
 
     def scatter_send(buf, dst, send, got, b):
         src = buf.at[rows_at(b * TOKENS, TOKENS)]
@@ -397,6 +429,24 @@
 
     def half(fb, kk):
         return rows_at(fb * 128 + kk * 64, 64)
+
+    def z_send(piece, send, got):
+        remote(piece, piece, send.at[1], got, zdev(far)).start()
+        remote(piece, piece, send.at[0], got, zdev(near)).start()
+
+    def z_sent(piece, send):
+        sent(piece, send.at[0])
+        sent(piece, send.at[1])
+
+    def take(piece, got, bsend, bgot):
+        recv(piece, got)
+        remote(piece, piece, bsend, bgot, sib).start()
+
+    def pass_on(piece, send, got):
+        remote(piece, piece, send, got, zdev(near)).start()
+
+    def of_row(t, xx):
+        return 2 * t + xx
 
     own_x = pltpu.make_async_copy(x_in.at[0], XO, loc.at[0])
     own_x.start()
@@ -416,9 +466,14 @@
             src = proj[w].at[rows_at(64 * k, 64), pl.ds(pl.multiple_of(128 * (2 * (2 * y + j) + x1), 128), 128)]
             remote(src, WQKV.at[half(f, k), pl.ds(256 * w + 128 * j, 128)], wx_s.at[0], wx_r.at[0], xdev).start()
     gather_send(x_in.at[0], XB, xb_s, xb_r)
+    for j in range(4):
+        src = wi_in.at[rows_at(64 * k, 64), pl.ds(pl.multiple_of(512 * (2 * j + x1) + 256 * y, 256), 256)]
+        remote(src, WIN.at[half(f, k), pl.ds(256 * j, 256)], wx_s.at[1], wx_r.at[1], xdev).start()
+    out_piece = WOUT.at[rows_at(128 * k, 128)]
+    out_other = WOUT.at[rows_at(128 * k1, 128)]
+
     pltpu.make_async_copy(WQKV.at[myrows], WQKV.at[myrows], loc.at[3]).wait()
-    for t in zs:
-        remote(WQKV.at[half(f, k)], WQKV.at[half(f, k)], wqz_s.at[0, t], wqz_r.at[f], zdev(t)).start()
+    z_send(WQKV.at[half(f, k)], wqz_s.at[0], wqz_r.at[f])
     for j in range(4):
         src = wi_in.at[:, pl.ds(pl.multiple_of(512 * (2 * j + x) + 256 * y, 256), 256)]
         pltpu.make_async_copy(src, WIN.at[myrows, pl.ds(256 * j, 256)], loc.at[4]).start()
@@ -461,15 +516,19 @@
         BACC[h] = jnp.zeros((128, WIDTH), F32)
 
     recv(WQKV.at[half(f1, k)], wx_r.at[0])
-    for t in zs:
-        remote(WQKV.at[half(f1, k)], WQKV.at[half(f1, k)], wqz_s.at[1, t], wqz_r.at[f1], zdev(t)).start()
+    z_send(WQKV.at[half(f1, k)], wqz_s.at[1], wqz_r.at[f1])
     remote(WQKV.at[half(f1, k)], WQKV.at[half(f1, k)], wqb_s.at[f1], wqb_r.at[f1], sib).start()
+
+    @pl.when(z == c)
+    def _():
+        remote(wo_in, out_piece, woz_s.at[1], woz_r, zdev(far)).start()
+        remote(wo_in, out_piece, woz_s.at[0], woz_r, zdev(near)).start()
 
     gain_one = row_of(0)
 
     def norm_block(i, carry):
         b = lax.rem(2 * y + i, 4)
-        recv(XB.at[rows_at(b * TOKENS, TOKENS)], xb_r.at[b])
+        gather_wait(XB, xb_r, b)
 
         def chunk(r, inner):
             rows = rows_at(b * TOKENS + r * 32, 32)
@@ -480,33 +539,45 @@
 
         return lax.fori_loop(0, 4, chunk, carry)
 
+    gather_pass(XB, xb_s, xb_r)
+    gather_send(cot_in.at[0], COT, co_s, co_r)
     lax.fori_loop(0, 4, norm_block, 0)
-    gather_send(cot_in.at[0], COT, co_s, co_r)
-    for j in range(4):
-        src = wi_in.at[rows_at(64 * k, 64), pl.ds(pl.multiple_of(512 * (2 * j + x1) + 256 * y, 256), 256)]
-        remote(src, WIN.at[half(f, k), pl.ds(256 * j, 256)], wx_s.at[1], wx_r.at[1], xdev).start()
-
-    for t in zs:
-        for xx in (x, x1):
-            piece = WQKV.at[half(2 * t + xx, k)]
-            recv(piece, wqz_r.at[2 * t + xx])
-            remote(piece, piece, wqb_s.at[2 * t + xx], wqb_r.at[2 * t + xx], sib).start()
-
-    out_piece = WOUT.at[rows_at(128 * k, 128)]
-    out_other = WOUT.at[rows_at(128 * k1, 128)]
-
-    @pl.when(z // 2 == y)
-    def _():
-        pltpu.make_async_copy(wo_in, out_piece, loc.at[6]).wait()
-
-    @pl.when(z == c)
-    def _():
-        for t in zs:
-            remote(out_piece, out_piece, woz_s.at[t], woz_r, zdev(t)).start()
-
+
+    for r, own in enumerate((f, f1)):
+        z_sent(WQKV.at[half(own, k)], wqz_s.at[r])
     pltpu.make_async_copy(WIN.at[myrows], WIN.at[myrows], loc.at[4]).wait()
-    for t in zs:
-        remote(WIN.at[half(f, k)], WIN.at[half(f, k)], wiz_s.at[0, t], wiz_r.at[f], zdev(t)).start()
+    z_send(WIN.at[half(f, k)], wiz_s.at[0], wiz_r.at[f])
+    recv(WIN.at[half(f1, k)], wx_r.at[1])
+    z_send(WIN.at[half(f1, k)], wiz_s.at[1], wiz_r.at[f1])
+    remote(WIN.at[half(f1, k)], WIN.at[half(f1, k)], wib_s.at[f1], wib_r.at[f1], sib).start()
+    for xx in (x, x1):
+        g = of_row(near, xx)
+        take(WQKV.at[half(g, k)], wqz_r.at[g], wqb_s.at[g], wqb_r.at[g])
+    for i, xx in enumerate((x, x1)):
+        for n in range(2):
+            g = of_row(others[n], xx)
+            piece = WQKV.at[half(g, k)]
+            recv(piece, wqz_r.at[g])
+
+            @pl.when(middle)
+            def _():
+                pass_on(piece, wqf_s.at[n, i], wqz_r.at[g])
+
+            remote(piece, piece, wqb_s.at[g], wqb_r.at[g], sib).start()
+
+    @pl.when(z != c)
+    def _():
+        recv(out_piece, woz_r)
+
+        @pl.when(middle & (z // 2 != c // 2))
+        def _():
+            pass_on(out_piece, woz_s.at[0], woz_r)
+
+        remote(out_piece, out_piece, wob_s, wob_r, sib).start()
+
+    down_half = rows_at(256 * z + 128 * k, 128)
+    pltpu.make_async_copy(WDOWN.at[rows_at(256 * z, 256)], WDOWN.at[rows_at(256 * z, 256)], loc.at[5]).wait()
+    z_send(WDOWN.at[down_half], wdz_s, wdz_r.at[z])
 
     for t in zs:
         for xx in (x, x1):
@@ -520,19 +591,16 @@
 
     lax.fori_loop(0, 3, project, 0)
 
-    recv(WIN.at[half(f1, k)], wx_r.at[1])
-    for t in zs:
-        remote(WIN.at[half(f1, k)], WIN.at[half(f1, k)], wiz_s.at[1, t], wiz_r.at[f1], zdev(t)).start()
-    remote(WIN.at[half(f1, k)], WIN.at[half(f1, k)], wib_s.at[f1], wib_r.at[f1], sib).start()
-
-    @pl.when(z != c)
-    def _():
-        recv(out_piece, woz_r)
-        remote(out_piece, out_piece, wob_s, wob_r, sib).start()
+
+    @pl.when(z // 2 == y)
+    def _():
+        pltpu.make_async_copy(wo_in, out_piece, loc.at[6]).wait()
 
     @pl.when(z != 2 * y + k1)
     def _():
         recv(out_other, wob_r)
+
+    gather_pass(COT, co_s, co_r)
 
     low_lanes = lax.broadcasted_iota(jnp.int32, (TOKENS, 128), 1) < 64
 
@@ -554,7 +622,9 @@
                 weights = jnp.exp(scores - jnp.max(scores, axis=-1, keepdims=True))
                 probs = weights * (1.0 / jnp.sum(weights, axis=-1, keepdims=True))
                 PROB[h, rows, :] = probs
-                outs.append(dot_nn(probs.astype(BF), QKV[:, 512 + 128 * j : 640 + 128 * j]))
+                low = probs.astype(BF)
+                PLOW[h, rows, :] = low
+                outs.append(dot_nn(low, QKV[:, 512 + 128 * j : 640 + 128 * j]))
             AT[rows, 128 * j : 128 * j + 128] = jnp.where(low_lanes, outs[0], outs[1]).astype(BF)
         SA[rows, :] = dot_nn(AT[rows, :], WOUT[...]).astype(BF)
         scatter_send(SA, RA, a_s, a_r, b)
@@ -562,10 +632,18 @@
 
     lax.fori_loop(0, 4, attend, 0)
 
-    down_half = rows_at(256 * z + 128 * k, 128)
-    pltpu.make_async_copy(WDOWN.at[rows_at(256 * z, 256)], WDOWN.at[rows_at(256 * z, 256)], loc.at[5]).wait()
-    for t in zs:
-        remote(WDOWN.at[down_half], WDOWN.at[down_half], wdz_s.at[t], wdz_r.at[z], zdev(t)).start()
+    for xx in (x, x1):
+        g = of_row(near, xx)
+        take(WIN.at[half(g, k)], wiz_r.at[g], wib_s.at[g], wib_r.at[g])
+
+    @pl.when(middle)
+    def _():
+        for i, xx in enumerate((x, x1)):
+            for n in range(2):
+                g = of_row(others[n], xx)
+                recv(WIN.at[half(g, k)], wiz_r.at[g])
+                pass_on(WIN.at[half(g, k)], wif_s.at[n, i], wiz_r.at[g])
+                remote(WIN.at[half(g, k)], WIN.at[half(g, k)], wib_s.at[g], wib_r.at[g], sib).start()
 
     own_x.wait()
     own_c.wait()
@@ -586,47 +664,99 @@
     lax.fori_loop(0, 4, home_forward, 0)
     gather_send(NTS, NTB, nt_s, nt_r)
 
+    def down_piece(t, kk):
+        return WDOWN.at[rows_at(256 * t + 128 * kk, 128)]
+
+    take(down_piece(near, k), wdz_r.at[near], wdb_s.at[near], wdb_r.at[near])
+
+    @pl.when(middle)
+    def _():
+        for n in range(2):
+            t = others[n]
+            recv(down_piece(t, k), wdz_r.at[t])
+            pass_on(down_piece(t, k), wdf_s.at[n], wdz_r.at[t])
+            remote(down_piece(t, k), down_piece(t, k), wdb_s.at[t], wdb_r.at[t], sib).start()
+
+    @pl.when(at_end)
+    def _():
+        for xx in (x, x1):
+            for t in others:
+                g = of_row(t, xx)
+                take(WIN.at[half(g, k)], wiz_r.at[g], wib_s.at[g], wib_r.at[g])
+
+    recv(WIN.at[half(f1, k1)], wib_r.at[f1])
     for t in zs:
         for xx in (x, x1):
-            piece = WIN.at[half(2 * t + xx, k)]
-            recv(piece, wiz_r.at[2 * t + xx])
-            remote(piece, piece, wib_s.at[2 * t + xx], wib_r.at[2 * t + xx], sib).start()
-    for t in zs:
-        piece = WDOWN.at[rows_at(256 * t + 128 * k, 128)]
-        recv(piece, wdz_r.at[t])
-        remote(piece, piece, wdb_s.at[t], wdb_r.at[t], sib).start()
-    for t in zs:
-        recv(WDOWN.at[rows_at(256 * t + 128 * k1, 128)], wdb_r.at[t])
-        for xx in (x, x1):
             recv(WIN.at[half(2 * t + xx, k1)], wib_r.at[2 * t + xx])
-    recv(WIN.at[half(f1, k1)], wib_r.at[f1])
-
-    for b in range(4):
-        recv(COT.at[pl.ds(b * TOKENS, TOKENS)], co_r.at[b])
-
-    def back_act(n, carry):
-        cols = rows_at(256 * n, 256)
-        GACT[:, cols] = dot_nt(COT[...], WDOWN[cols, :])
-        return carry
-
-    lax.fori_loop(0, 4, back_act, 0)
+
+    gather_pass(NTB, nt_s, nt_r)
 
     def feed(i, carry):
         yy = lax.rem(y + i, 2)
         rows = rows_at(256 * yy, 256)
         for b in (2 * yy, 2 * yy + 1):
-            recv(NTB.at[rows_at(b * TOKENS, TOKENS)], nt_r.at[b])
+            gather_wait(NTB, nt_r, b)
 
         def hidden_units(n, inner):
             cols = rows_at(256 * n, 256)
             pre = dot_nn(NTB[rows, :], WIN[:, cols])
             cdf = 0.5 * (1.0 + lax.erf(pre * 0.7071067811865476))
             ACT[rows, cols] = (pre * cdf).astype(BF)
-            slope = cdf + pre * jnp.exp(-0.5 * pre * pre) * 0.3989422804014327
-            GPRE[rows, cols] = (GACT[rows, cols] * slope).astype(BF)
+            SLOPE[rows, cols] = cdf + pre * jnp.exp(-0.5 * pre * pre) * 0.3989422804014327
             return inner
 
-        lax.fori_loop(0, 4, hidden_units, 0)
+        return lax.fori_loop(0, 4, hidden_units, carry)
+
+    lax.fori_loop(0, 2, feed, 0)
+
+    for b in range(4):
+        gather_wait(COT, co_r, b)
+
+    def grad_down(m, carry):
+        tile = dot_tn(ACT[:, rows_at(256 * m, 256)], COT[...]).astype(BF)
+        DD[0, m] = tile[0:128]
+        DD[1, m] = tile[128:256]
+        return carry
+
+    lax.fori_loop(0, 4, grad_down, 0)
+    remote(DD.at[k1], SIBD, sib_s.at[0], sib_r.at[0], sib).start()
+
+    @pl.when(at_end)
+    def _():
+        for t in others:
+            take(down_piece(t, k), wdz_r.at[t], wdb_s.at[t], wdb_r.at[t])
+
+    for t in zs:
+        recv(down_piece(t, k1), wdb_r.at[t])
+
+    def z_reduce_send(terms, got, send, esend, recv_sem):
+        @pl.when(at_end)
+        def _():
+            for n in range(2):
+                t = others[n]
+                remote(terms(t), got(t), esend.at[n], recv_sem.at[t], zdev(near)).start()
+
+        remote(terms(near), got(near), send, recv_sem.at[near], zdev(near)).start()
+
+    recv(SIBD, sib_r.at[0])
+
+    def join_down(m, carry):
+        ZD[m] = (DD[k, m].astype(F32) + SIBD[m].astype(F32)).astype(BF)
+        return carry
+
+    lax.fori_loop(0, 4, join_down, 0)
+    z_reduce_send(lambda t: ZD.at[t], lambda t: RED.at[t], zd_s, zde_s, zd_r)
+
+    def back_feed(i, carry):
+        yy = lax.rem(y1 + i, 2)
+        rows = rows_at(256 * yy, 256)
+
+        def back_act(n, inner):
+            cols = rows_at(256 * n, 256)
+            GPRE[rows, cols] = (dot_nt(COT[rows, :], WDOWN[cols, :]) * SLOPE[rows, cols]).astype(BF)
+            return inner
+
+        lax.fori_loop(0, 4, back_act, 0)
 
         def back_normed(n, inner):
             cols = rows_at(256 * n, 256)
@@ -638,23 +768,7 @@
         scatter_send(SG, RG, g_s, g_r, 2 * yy + 1)
         return carry
 
-    lax.fori_loop(0, 2, feed, 0)
-
-    def down_project(n, carry):
-        cols = rows_at(256 * n, 256)
-        SO[:, cols] = dot_nn(ACT[...], WDOWN[:, cols]).astype(BF)
-        return carry
-
-    lax.fori_loop(0, 4, down_project, 0)
-
-    def grad_down(m, carry):
-        tile = dot_tn(ACT[:, rows_at(256 * m, 256)], COT[...]).astype(BF)
-        DD[0, m] = tile[0:128]
-        DD[1, m] = tile[128:256]
-        return carry
-
-    lax.fori_loop(0, 4, grad_down, 0)
-    remote(DD.at[k1], SIBD, sib_s.at[0], sib_r.at[0], sib).start()
+    lax.fori_loop(0, 2, back_feed, 0)
 
     def grad_in(m, carry):
         tile = dot_tn(NTB[:, rows_at(256 * m, 256)], GPRE[...]).astype(BF)
@@ -665,15 +779,32 @@
 
     lax.fori_loop(0, 4, grad_in, 0)
     remote(DI.at[k1], SIBI, sib_s.at[1], sib_r.at[1], sib).start()
-    recv(SIBD, sib_r.at[0])
-
-    def join_down(m, carry):
-        ZD[m] = (DD[k, m].astype(F32) + SIBD[m].astype(F32)).astype(BF)
-        return carry
-
-    lax.fori_loop(0, 4, join_down, 0)
-    for t in zs:
-        remote(ZD.at[t], RZD.at[z], zd_s.at[t], zd_r.at[z], zdev(t)).start()
+
+    def down_project(n, carry):
+        cols = rows_at(256 * n, 256)
+        SO[:, cols] = dot_nn(ACT[...], WDOWN[:, cols]).astype(BF)
+        return carry
+
+    lax.fori_loop(0, 4, down_project, 0)
+
+    recv(SIBI, sib_r.at[1])
+
+    def join_in(m, carry):
+        ZI[m] = (DI[k, m].astype(F32) + SIBI[m].astype(F32)).astype(BF)
+        return carry
+
+    lax.fori_loop(0, 8, join_in, 0)
+    z_reduce_send(
+        lambda t: ZI.at[pl.ds(2 * t, 2)], lambda t: REI.at[pl.ds(2 * t, 2)], zi_s, zie_s, zi_r
+    )
+
+    @pl.when(middle)
+    def _():
+        for n in range(2):
+            t = others[n]
+            recv(RED.at[t], zd_r.at[t])
+            ZD[t] = (ZD[t].astype(F32) + RED[t].astype(F32)).astype(BF)
+            remote(ZD.at[t], RCD, zde_s.at[n], zdc_r, zdev(t)).start()
 
     for s in range(4):
         recv(RG.at[s], g_r.at[s])
@@ -694,32 +825,107 @@
 
     mlp_gain_grad = lax.fori_loop(0, 4, home_back, jnp.zeros((8, WIDTH), F32))
     gather_send(GALS, GAL, ga_s, ga_r)
-    for b in range(4):
-        scatter_send(SO, RO, o_s, o_r, lax.rem(2 * y1 + b, 4))
     mlp_gain_grad = jnp.sum(mlp_gain_grad, axis=0, keepdims=True)
     for g in range(8):
-        SMALL[g] = jnp.zeros((8, 128), F32)
-        SMALL[g, 1:2, :] = mlp_gain_grad[:, 128 * g : 128 * g + 128]
-
-    recv(SIBI, sib_r.at[1])
-
-    def join_in(m, carry):
-        ZI[m] = (DI[k, m].astype(F32) + SIBI[m].astype(F32)).astype(BF)
-        return carry
-
-    lax.fori_loop(0, 8, join_in, 0)
-    for t in zs:
-        remote(ZI.at[pl.ds(2 * t, 2)], RZI.at[z], zi_s.at[t], zi_r.at[z], zdev(t)).start()
-
-    DKACC[...] = jnp.zeros_like(DKACC)
-    DVACC[...] = jnp.zeros_like(DVACC)
-
-    def attend_back(i, carry):
+        SMALL[1, g : g + 1, :] = mlp_gain_grad[:, 128 * g : 128 * g + 128]
+
+    gather_pass(GAL, ga_s, ga_r)
+
+    def back_out(i, carry):
         b = lax.rem(2 * y + i, 4)
         rows = rows_at(b * TOKENS, TOKENS)
-        window = pl.ds(pl.multiple_of(384 - 128 * b, 128), 512)
-        recv(GAL.at[rows], ga_r.at[b])
-        GATT[...] = dot_nt(GAL[rows, :], WOUT[...]).astype(BF)
+        gather_wait(GAL, ga_r, b)
+        GATT[rows, :] = dot_nt(GAL[rows, :], WOUT[...]).astype(BF)
+        return carry
+
+    lax.fori_loop(0, 4, back_out, 0)
+    for i in range(4):
+        scatter_send(SO, RO, o_s, o_r, lax.rem(2 * y1 + i, 4))
+    all_low = lax.broadcasted_iota(jnp.int32, (512, 128), 1) < 64
+
+    def pick_all(values, hh):
+        keep = all_low if hh == 0 else jnp.logical_not(all_low)
+        return jnp.where(keep, values, jnp.zeros_like(values))
+
+    def grad_values(j, carry):
+        grad_att = GATT[:, rows_at(128 * j, 128)]
+        first = dot_tn(PLOW[2 * j], pick_all(grad_att, 0))
+        second = dot_tn(PLOW[2 * j + 1], pick_all(grad_att, 1))
+        DQKV[:, pl.ds(pl.multiple_of(512 + 128 * j, 128), 128)] = jnp.where(all_low, first, second).astype(BF)
+        return carry
+
+    lax.fori_loop(0, 2, grad_values, 0)
+
+    def grad_proj(first, width):
+        def step(m, carry):
+            tile = dot_tn(N1[:, rows_at(256 * m, 256)], DQKV[:, first : first + width]).astype(BF)
+            for part in range(2):
+                DQ[0, 2 * m + part, :, first : first + width] = tile[128 * part : 128 * part + 64]
+                DQ[1, 2 * m + part, :, first : first + width] = tile[128 * part + 64 : 128 * part + 128]
+            return carry
+
+        lax.fori_loop(0, 4, step, 0)
+
+    def join_proj(first, width):
+        def step(m, carry):
+            total = DQ[k, m, :, first : first + width].astype(F32) + SIBQ[m, :, first : first + width].astype(F32)
+            ZQ[m, :, first : first + width] = total.astype(BF)
+            return carry
+
+        lax.fori_loop(0, 8, step, 0)
+
+    value_cols, other_cols = pl.ds(512, 256), pl.ds(0, 512)
+    grad_proj(512, 256)
+    remote(DQ.at[k1, :, :, value_cols], SIBQ.at[:, :, value_cols], sib_s.at[2], sib_r.at[2], sib).start()
+
+    def grad_out_rows(m, carry):
+        DO[m] = dot_tn(AT[:, rows_at(128 * m, 128)], GAL[...]).astype(BF)
+        return carry
+
+    lax.fori_loop(0, 2, grad_out_rows, 0)
+    remote(DO.at[k1], SIBO, sib_s.at[3], sib_r.at[3], sib).start()
+
+    def z_scatter(cols, send, got):
+        for t in zs:
+            remote(
+                ZQ.at[pl.ds(2 * t, 2), :, cols], RZQ.at[z, :, :, cols], send.at[t], got.at[z], zdev(t)
+            ).start()
+
+    recv(SIBQ.at[:, :, value_cols], sib_r.at[2])
+    join_proj(512, 256)
+    z_scatter(value_cols, zv_s, zv_r)
+
+    recv(SIBO, sib_r.at[3])
+    ZO[...] = (DO[k].astype(F32) + SIBO[...].astype(F32)).astype(BF)
+
+    out_near = z // 2 == c // 2
+
+    @pl.when((z != c) & out_near)
+    def _():
+        remote(ZO, RZO.at[0], zo_s, zo_r.at[0], zdev(c)).start()
+
+    @pl.when(jnp.logical_not(out_near) & at_end)
+    def _():
+        remote(ZO, RZO.at[0], zo_s, zo_r.at[0], zdev(near)).start()
+
+    @pl.when(middle)
+    def _():
+        for n in range(2):
+            t = others[n]
+            recv(REI.at[pl.ds(2 * t, 2)], zi_r.at[t])
+            for xx in range(2):
+                ZI[2 * t + xx] = (ZI[2 * t + xx].astype(F32) + REI[2 * t + xx].astype(F32)).astype(BF)
+            remote(ZI.at[pl.ds(2 * t, 2)], RCI, zie_s.at[n], zic_r, zdev(t)).start()
+
+    @pl.when(jnp.logical_not(out_near) & middle)
+    def _():
+        recv(RZO.at[0], zo_r.at[0])
+        ZO[...] = (ZO[...].astype(F32) + RZO[0].astype(F32)).astype(BF)
+        remote(ZO, RZO.at[1], zo_s, zo_r.at[1], zdev(c)).start()
+
+    def attend_back(i, carry):
+        rows = rows_at(i * TOKENS, TOKENS)
+        window = pl.ds(pl.multiple_of(384 - 128 * i, 128), 512)
         for j in range(2):
             pair = slice(128 * j, 128 * j + 128)
             keys = QKV[:, 256 + 128 * j : 384 + 128 * j]
@@ -727,23 +933,30 @@
             outs = []
             for hh in range(2):
                 h = 2 * j + hh
-                query = pick(QKV[rows, pair], hh)
-                grad_att = pick(GATT[:, pair], hh)
+                grad_att = pick(GATT[rows, pair], hh)
                 probs = PROB[h, rows, :]
                 grad_probs = dot_nt(grad_att, values)
                 inner = jnp.sum(probs * grad_probs, axis=-1, keepdims=True)
                 grad_scores = (probs * (grad_probs - inner)).astype(BF)
+                DS[h, rows, :] = grad_scores
                 BACC[h, :, window] = BACC[h, :, window] + grad_scores.astype(F32)
                 outs.append(dot_nn(grad_scores, keys))
-                DKACC[:, pair] = DKACC[:, pair] + dot_tn(grad_scores, query)
-                DVACC[:, pair] = DVACC[:, pair] + dot_tn(probs.astype(BF), grad_att)
             DQKV[rows, pair] = jnp.where(low_lanes, outs[0], outs[1]).astype(BF)
         return carry
 
     lax.fori_loop(0, 4, attend_back, 0)
-    DQKV[:, 256:512] = DKACC[...].astype(BF)
-    DQKV[:, 512:768] = DVACC[...].astype(BF)
-
+
+    def grad_keys(j, carry):
+        query = QKV[:, rows_at(128 * j, 128)]
+        first = dot_tn(DS[2 * j], pick_all(query, 0))
+        second = dot_tn(DS[2 * j + 1], pick_all(query, 1))
+        DQKV[:, pl.ds(pl.multiple_of(256 + 128 * j, 128), 128)] = jnp.where(all_low, first, second).astype(BF)
+        return carry
+
+    lax.fori_loop(0, 2, grad_keys, 0)
+
+    grad_proj(0, 512)
+    remote(DQ.at[k1, :, :, other_cols], SIBQ.at[:, :, other_cols], sib_s.at[4], sib_r.at[4], sib).start()
     def back_project(i, carry):
         yy = lax.rem(y1 + i, 2)
         rows = rows_at(256 * yy, 256)
@@ -754,95 +967,9 @@
 
     lax.fori_loop(0, 2, back_project, 0)
 
-    def grad_proj(m, carry):
-        tile = dot_tn(N1[:, rows_at(256 * m, 256)], DQKV[...]).astype(BF)
-        for part in range(2):
-            DQ[0, 2 * m + part] = tile[128 * part : 128 * part + 64]
-            DQ[1, 2 * m + part] = tile[128 * part + 64 : 128 * part + 128]
-        return carry
-
-    lax.fori_loop(0, 4, grad_proj, 0)
-    remote(DQ.at[k1], SIBQ, sib_s.at[2], sib_r.at[2], sib).start()
-
-    def grad_out_rows(m, carry):
-        DO[m] = dot_tn(AT[:, rows_at(128 * m, 128)], GAL[...]).astype(BF)
-        return carry
-
-    lax.fori_loop(0, 2, grad_out_rows, 0)
-    remote(DO.at[k1], SIBO, sib_s.at[3], sib_r.at[3], sib).start()
-    recv(SIBQ, sib_r.at[2])
-
-    def join_proj(m, carry):
-        ZQ[m] = (DQ[k, m].astype(F32) + SIBQ[m].astype(F32)).astype(BF)
-        return carry
-
-    lax.fori_loop(0, 8, join_proj, 0)
-    for t in zs:
-        remote(ZQ.at[pl.ds(2 * t, 2)], RZQ.at[z], zq_s.at[t], zq_r.at[z], zdev(t)).start()
-    recv(SIBO, sib_r.at[3])
-    ZO[...] = (DO[k].astype(F32) + SIBO[...].astype(F32)).astype(BF)
-
-    @pl.when(z != c)
-    def _():
-        remote(ZO, RZO.at[z], zo_s, zo_r.at[z], zdev(c)).start()
-
-    for t in zs:
-        recv(RZD.at[t], zd_r.at[t])
-    total = ZD[z].astype(F32)
-    for t in zs:
-        total = total + RZD[t].astype(F32)
-    FD[...] = total.astype(BF)
-    down_rows = odown.at[rows_at(128 * c, 128)]
-    pltpu.make_async_copy(FD, down_rows, fd_r.at[c]).start()
-    for i in range(1, 4):
-        ci = lax.rem(c + i, 4)
-        remote(FD, down_rows, fd_s.at[i], fd_r.at[c], (ci, f)).start()
-    for t in zs:
-        recv(RZI.at[t], zi_r.at[t])
-    for xx in range(2):
-        total = ZI[2 * z + xx].astype(F32)
-        for t in zs:
-            total = total + RZI[t, xx].astype(F32)
-        for j in range(4):
-            FI[xx, j] = total[:, 256 * j : 256 * j + 256].astype(BF)
-    in_rows = oin.at[:, q, rows_at(64 * k, 64), :]
-    pltpu.make_async_copy(FI.at[x], in_rows, fi_r.at[c, x]).start()
-    for i in range(4):
-        ci = lax.rem(c + i, 4)
-        for j, xj in enumerate((x, x1)):
-            if i or j:
-                remote(FI.at[xj], in_rows, fi_s.at[i, j], fi_r.at[c, x], (ci, 2 * z + xj)).start()
-
-    for s in range(4):
-        recv(RO.at[s], o_r.at[s])
-
-    def home_out(r, carry):
-        rows = rows_at(r * 32, 32)
-        result = HID[rows, :]
-        for s in range(4):
-            result = result + RO[s, rows, :].astype(F32)
-        out_ref[0, rows, :] = result.astype(BF)
-        return carry
-
-    lax.fori_loop(0, 4, home_out, 0)
-    for s in range(4):
-        recv(RN.at[s], n_r.at[s])
-
-    def home_inputs(r, total):
-        rows = rows_at(r * 32, 32)
-        grad = RN[0, rows, :].astype(F32)
-        for s in range(1, 4):
-            grad = grad + RN[s, rows, :].astype(F32)
-        values = XO[rows, :].astype(F32)
-        scale = lax.rsqrt(jnp.mean(values * values, axis=-1, keepdims=True) + EPS)
-        scaled = grad * gain_one
-        inner = jnp.mean(scaled * values, axis=-1, keepdims=True)
-        back = GH[rows, :] + scale * scaled - values * (scale * scale * scale * inner)
-        gin_ref[0, rows, :] = back.astype(BF)
-        return total + jnp.sum((grad * values * scale).reshape(4, 8, WIDTH), axis=0)
-
-    attn_gain_grad = lax.fori_loop(0, 4, home_inputs, jnp.zeros((8, WIDTH), F32))
-    attn_gain_grad = jnp.sum(attn_gain_grad, axis=0, keepdims=True)
+    recv(SIBQ.at[:, :, other_cols], sib_r.at[4])
+    join_proj(0, 512)
+    z_scatter(other_cols, zq_s, zq_r)
 
     head_sums = []
     for h in range(4):
@@ -858,17 +985,99 @@
     head_sums = jnp.concatenate(head_sums + [jnp.zeros((4, WIDTH), F32)], axis=0)
     coarse = head_sums.astype(BF)
     split_sums = jnp.concatenate([coarse, (head_sums - coarse.astype(F32)).astype(BF)], axis=0)
-
     both_masks = jnp.concatenate([head_mask.astype(F32)] * 2, axis=0) > 0.5
 
     def bucket_sums(g, carry):
         sums = dot_nt(split_sums, bucket_hot(g).astype(BF))
-        SMALL[g, 2:3, :] = jnp.sum(jnp.where(both_masks, sums, 0.0), axis=0, keepdims=True)
+        SMALL[2, pl.ds(g, 1), :] = jnp.sum(jnp.where(both_masks, sums, 0.0), axis=0, keepdims=True)
         return carry
 
     lax.fori_loop(0, 8, bucket_sums, 0)
+
+    recv(RED.at[z], zd_r.at[z])
+    recv(RCD, zdc_r)
+    FD[...] = (ZD[z].astype(F32) + RED[z].astype(F32) + RCD[...].astype(F32)).astype(BF)
+
+    def down_rows(cc):
+        return odown.at[rows_at(128 * cc, 128)]
+
+    y_core = (2 * y1 + k, f)
+    remote(FD, down_rows(c), fd_s.at[1], fd_r.at[c], y_core).start()
+    remote(FD, down_rows(c), fd_s.at[0], fd_r.at[c], sib).start()
+    pltpu.make_async_copy(FD, down_rows(c), fd_r.at[c]).start()
+
+    def spread(final, place, send, bsend, got):
+        remote(final.at[x1], place(q, k), send.at[2], got.at[q, k], (2 * y1 + k, f1)).start()
+        remote(final.at[x1], place(q, k), send.at[1], got.at[q, k], (c, f1)).start()
+        remote(final.at[x], place(q, k), send.at[0], got.at[q, k], y_core).start()
+        remote(final.at[x], place(q, k), bsend.at[0], got.at[q, k], sib).start()
+        pltpu.make_async_copy(final.at[x], place(q, k), got.at[q, k]).start()
+
+    chips = (2 * x + y1, 2 * x1 + y, 2 * x1 + y1)
+
+    def spread_on(place, bsend, got):
+        for i in range(3):
+            piece = place(chips[i], k)
+            recv(piece, got.at[chips[i], k])
+            remote(piece, piece, bsend.at[i + 1], got.at[chips[i], k], sib).start()
+
+    def spread_done(final, place, send, bsend, got):
+        recv(place(q, k), got.at[q, k])
+        for qq in (q,) + chips:
+            recv(place(qq, k1), got.at[qq, k1])
+        sent(final.at[x1], send.at[2])
+        sent(final.at[x1], send.at[1])
+        sent(final.at[x], send.at[0])
+        sent(final.at[x], bsend.at[0])
+        for i in range(3):
+            sent(place(chips[i], k), bsend.at[i + 1])
+
+    def in_place(qq, kk):
+        return oin.at[:, qq, rows_at(64 * kk, 64), :]
+
+    def proj_place(qq, kk):
+        return oqkv.at[qq, rows_at(64 * kk, 64), :]
+
+    recv(REI.at[pl.ds(2 * z, 2)], zi_r.at[z])
+    recv(RCI, zic_r)
+    for xx in range(2):
+        total = ZI[2 * z + xx].astype(F32) + REI[2 * z + xx].astype(F32) + RCI[xx].astype(F32)
+        for j in range(4):
+            FI[xx, j] = total[:, 256 * j : 256 * j + 256].astype(BF)
+    spread(FI, in_place, fi_s, fib_s, fi_r)
+
+    for s in range(4):
+        recv(RO.at[s], o_r.at[s])
+
+    def home_out(r, carry):
+        rows = rows_at(r * 32, 32)
+        result = HID[rows, :]
+        for s in range(4):
+            result = result + RO[s, rows, :].astype(F32)
+        out_ref[0, rows, :] = result.astype(BF)
+        return carry
+
+    lax.fori_loop(0, 4, home_out, 0)
+    for s in range(4):
+        recv(RN.at[s], n_r.at[s])
+
+    def home_inputs(r, total):
+        rows = rows_at(r * 32, 32)
+        grad = RN[0, rows, :].astype(F32)
+        for s in range(1, 4):
+            grad = grad + RN[s, rows, :].astype(F32)
+        values = XO[rows, :].astype(F32)
+        scale = lax.rsqrt(jnp.mean(values * values, axis=-1, keepdims=True) + EPS)
+        scaled = grad * gain_one
+        inner = jnp.mean(scaled * values, axis=-1, keepdims=True)
+        back = GH[rows, :] + scale * scaled - values * (scale * scale * scale * inner)
+        gin_ref[0, rows, :] = back.astype(BF)
+        return total + jnp.sum((grad * values * scale).reshape(4, 8, WIDTH), axis=0)
+
+    attn_gain_grad = lax.fori_loop(0, 4, home_inputs, jnp.zeros((8, WIDTH), F32))
+    attn_gain_grad = jnp.sum(attn_gain_grad, axis=0, keepdims=True)
     for g in range(8):
-        SMALL[g, 0:1, :] = attn_gain_grad[:, 128 * g : 128 * g + 128]
+        SMALL[0, g : g + 1, :] = attn_gain_grad[:, 128 * g : 128 * g + 128]
 
     for i in range(4):
         ci = lax.rem(c + i, 4)
@@ -877,31 +1086,23 @@
                 remote(SMALL, RSMALL.at[2 * c + x], sp_s.at[i, j], sp_r.at[2 * c + x], (ci, 2 * z + xj)).start()
 
     for t in zs:
-        recv(RZQ.at[t], zq_r.at[t])
+        recv(RZQ.at[t, :, :, value_cols], zv_r.at[t])
+        recv(RZQ.at[t, :, :, other_cols], zq_r.at[t])
     for xx in range(2):
         total = ZQ[2 * z + xx].astype(F32)
         for t in zs:
             total = total + RZQ[t, xx].astype(F32)
         FQ[xx] = total.astype(BF)
-    proj_rows = oqkv.at[q, rows_at(64 * k, 64), :]
-    pltpu.make_async_copy(FQ.at[x], proj_rows, fq_r.at[c, x]).start()
-    for i in range(4):
-        ci = lax.rem(c + i, 4)
-        for j, xj in enumerate((x, x1)):
-            if i or j:
-                remote(FQ.at[xj], proj_rows, fq_s.at[i, j], fq_r.at[c, x], (ci, 2 * z + xj)).start()
+    spread(FQ, proj_place, fq_s, fqb_s, fq_r)
 
     @pl.when(z == c)
     def _():
-        for t in zs:
-            recv(RZO.at[t], zo_r.at[t])
-        total = ZO[...].astype(F32)
-        for t in zs:
-            total = total + RZO[t].astype(F32)
-        FO[...] = total.astype(BF)
+        for s in range(2):
+            recv(RZO.at[s], zo_r.at[s])
+        FO[...] = (ZO[...].astype(F32) + RZO[0].astype(F32) + RZO[1].astype(F32)).astype(BF)
         pltpu.make_async_copy(FO, oout, fo_r).start()
-        for i in range(1, 4):
-            remote(FO, oout, fo_s.at[i], fo_r, (lax.rem(c + i, 4), f)).start()
+        remote(FO, oout, fo_s.at[1], fo_r, y_core).start()
+        remote(FO, oout, fo_s.at[0], fo_r, sib).start()
 
     plane_sum = SMALL[...]
     for i in range(4):
@@ -910,77 +1111,107 @@
             if i or j:
                 recv(RSMALL.at[2 * ci + xj], sp_r.at[2 * ci + xj])
                 plane_sum = plane_sum + RSMALL[2 * ci + xj]
-    PSMALL[...] = plane_sum
+    for t in range(4):
+        for n in range(3):
+            pair = plane_sum[n, 2 * t : 2 * t + 2, :]
+            PSMALL[t, n : n + 1, :] = jnp.where(x == 0, pair[0:1], pair[1:2])
     for t in zs:
-        remote(PSMALL.at[2 * t + x], RZSMALL.at[z], sz_s.at[t], sz_r.at[z], zdev(t)).start()
-    total = PSMALL[f]
+        remote(PSMALL.at[t], RZSMALL.at[z], sz_s.at[t], sz_r.at[z], zdev(t)).start()
+
+    y_rows = down_rows(2 * y1 + k)
+    recv(y_rows, fd_r.at[2 * y1 + k])
+    remote(y_rows, y_rows, fd_s.at[2], fd_r.at[2 * y1 + k], sib).start()
+    spread_on(in_place, fib_s, fi_r)
+    spread_on(proj_place, fqb_s, fq_r)
+    recv(oout, fo_r)
+    out_on = (y != z // 2) & (k == lax.rem(z, 2))
+
+    @pl.when(out_on)
+    def _():
+        remote(oout, oout, fo_s.at[0], fo_r, sib).start()
+
+    total = PSMALL[z]
     for t in zs:
         recv(RZSMALL.at[t], sz_r.at[t])
         total = total + RZSMALL[t]
     small_ref[...] = total
 
-    recv(oout, fo_r)
-    for i in range(4):
-        ci = lax.rem(c + i, 4)
-        recv(odown.at[rows_at(128 * ci, 128)], fd_r.at[ci])
-        for xj in (x, x1):
-            qi = 2 * xj + ci // 2
-            ki = lax.rem(ci, 2)
-            recv(oin.at[:, qi, rows_at(64 * ki, 64), :], fi_r.at[ci, xj])
-            recv(oqkv.at[qi, rows_at(64 * ki, 64), :], fq_r.at[ci, xj])
+    recv(down_rows(c), fd_r.at[c])
+    recv(down_rows(2 * y + k1), fd_r.at[2 * y + k1])
+    recv(down_rows(2 * y1 + k1), fd_r.at[2 * y1 + k1])
+    spread_done(FI, in_place, fi_s, fib_s, fi_r)
+    spread_done(FQ, proj_place, fq_s, fqb_s, fq_r)
 
     sent(pack_in, gpx_s)
-    gather_sent(x_in.at[0], xb_s)
-    gather_sent(cot_in.at[0], co_s)
-    gather_sent(NTS, nt_s)
-    gather_sent(GALS, ga_s)
+    gather_sent(x_in.at[0], XB, xb_s)
+    gather_sent(cot_in.at[0], COT, co_s)
+    gather_sent(NTS, NTB, nt_s)
+    gather_sent(GALS, GAL, ga_s)
     scatter_sent(SA, a_s)
     scatter_sent(SG, g_s)
     scatter_sent(SO, o_s)
     scatter_sent(SN, n_s)
     sent(WQKV.at[half(f, k)], wx_s.at[0])
     sent(WIN.at[half(f, k)], wx_s.at[1])
+    for r, own in enumerate((f, f1)):
+        z_sent(WIN.at[half(own, k)], wiz_s.at[r])
+    z_sent(WDOWN.at[down_half], wdz_s)
     sent(WQKV.at[half(f1, k)], wqb_s.at[f1])
     sent(WIN.at[half(f1, k)], wib_s.at[f1])
     for t in zs:
         sent(GP.at[pl.ds(2 * z, 2)], gpz_s.at[t])
-        for r, own in enumerate((f, f1)):
-            sent(WQKV.at[half(own, k)], wqz_s.at[r, t])
-            sent(WIN.at[half(own, k)], wiz_s.at[r, t])
         for xx in (x, x1):
             sent(WQKV.at[half(2 * t + xx, k)], wqb_s.at[2 * t + xx])
             sent(WIN.at[half(2 * t + xx, k)], wib_s.at[2 * t + xx])
-        sent(WDOWN.at[down_half], wdz_s.at[t])
-        sent(WDOWN.at[rows_at(256 * t + 128 * k, 128)], wdb_s.at[t])
-        sent(ZD.at[t], zd_s.at[t])
-        sent(ZI.at[pl.ds(2 * t, 2)], zi_s.at[t])
-        sent(ZQ.at[pl.ds(2 * t, 2)], zq_s.at[t])
-        sent(PSMALL.at[2 * t + x], sz_s.at[t])
+        sent(down_piece(t, k), wdb_s.at[t])
+        sent(ZQ.at[pl.ds(2 * t, 2), :, value_cols], zv_s.at[t])
+        sent(ZQ.at[pl.ds(2 * t, 2), :, other_cols], zq_s.at[t])
+        sent(PSMALL.at[t], sz_s.at[t])
+    sent(ZD.at[near], zd_s)
+    sent(ZI.at[pl.ds(2 * near, 2)], zi_s)
+    for n in range(2):
+        sent(ZD.at[others[n]], zde_s.at[n])
+        sent(ZI.at[pl.ds(2 * others[n], 2)], zie_s.at[n])
+
+    @pl.when(middle)
+    def _():
+        for n in range(2):
+            sent(down_piece(others[n], k), wdf_s.at[n])
+            for i, xx in enumerate((x, x1)):
+                g = of_row(others[n], xx)
+                sent(WQKV.at[half(g, k)], wqf_s.at[n, i])
+                sent(WIN.at[half(g, k)], wif_s.at[n, i])
 
     @pl.when(z == c)
     def _():
-        for t in zs:
-            sent(out_piece, woz_s.at[t])
-        for i in range(1, 4):
-            sent(FO, fo_s.at[i])
+        z_sent(out_piece, woz_s)
+        sent(FO, fo_s.at[0])
+        sent(FO, fo_s.at[1])
+
+    @pl.when(out_on)
+    def _():
+        sent(oout, fo_s.at[0])
 
     @pl.when(z != c)
     def _():
         sent(out_piece, wob_s)
         sent(ZO, zo_s)
 
+        @pl.when(middle & (z // 2 != c // 2))
+        def _():
+            sent(out_piece, woz_s.at[0])
+
     sent(DD.at[k1], sib_s.at[0])
     sent(DI.at[k1], sib_s.at[1])
-    sent(DQ.at[k1], sib_s.at[2])
+    sent(DQ.at[k1, :, :, value_cols], sib_s.at[2])
     sent(DO.at[k1], sib_s.at[3])
-    for i in range(1, 4):
+    sent(DQ.at[k1, :, :, other_cols], sib_s.at[4])
+    for i in range(3):
         sent(FD, fd_s.at[i])
     for i in range(4):
         for j, xj in enumerate((x, x1)):
             if i or j:
                 sent(SMALL, sp_s.at[i, j])
-                sent(FI.at[xj], fi_s.at[i, j])
-                sent(FQ.at[xj], fq_s.at[i, j])
 
 
 def plane_shards(
@@ -1004,26 +1235,28 @@
         block(BF), block(BF), vm((8, 8, 128), F32),
         tokens(1024, BF), tokens(1024, BF), tokens(1024, BF), tokens(1024, BF), tokens(1024, BF),
         vm((1024, 768), BF), vm((256, 1024), BF), vm((1024, 1024), BF), vm((1024, 1024), BF),
-        tokens(768, BF), vm((4, 512, 512), F32), vm((4, 128, 1024), F32), tokens(256, BF),
-        tokens(1024, BF), tokens(1024, F32), tokens(1024, BF),
-        vm((128, 256), BF), tokens(768, BF), tokens(256, F32), tokens(256, F32), vm((4, 128, 1024), F32),
+        tokens(768, BF), vm((4, 512, 512), F32), vm((4, 512, 512), BF), vm((4, 128, 1024), F32),
+        tokens(256, BF), tokens(1024, BF), tokens(1024, F32), tokens(1024, BF),
+        tokens(256, BF), tokens(768, BF), vm((4, 512, 512), BF), vm((4, 128, 1024), F32),
         tokens(1024, BF), tokens(1024, BF), tokens(1024, BF), tokens(1024, BF),
         vm((4, 128, 1024), BF), vm((4, 128, 1024), BF), vm((4, 128, 1024), BF), vm((4, 128, 1024), BF),
         block(F32), block(F32), block(BF), block(BF),
         vm((2, 8, 64, 768), BF), vm((2, 128, 1024), BF), vm((2, 8, 64, 1024), BF), vm((2, 4, 128, 1024), BF),
         vm((8, 64, 768), BF), vm((128, 1024), BF), vm((8, 64, 1024), BF), vm((4, 128, 1024), BF),
         vm((8, 64, 768), BF), vm((128, 1024), BF), vm((8, 64, 1024), BF), vm((4, 128, 1024), BF),
-        vm((4, 2, 64, 768), BF), vm((4, 128, 1024), BF), vm((4, 2, 64, 1024), BF), vm((4, 128, 1024), BF),
+        vm((4, 2, 64, 768), BF), vm((2, 128, 1024), BF), vm((8, 64, 1024), BF), vm((4, 128, 1024), BF),
+        vm((2, 64, 1024), BF), vm((128, 1024), BF),
         vm((2, 64, 768), BF), vm((128, 1024), BF), vm((2, 4, 64, 256), BF), vm((128, 1024), BF),
-        vm((8, 8, 128), F32), vm((8, 8, 8, 128), F32), vm((8, 8, 128), F32), vm((4, 8, 128), F32),
+        vm((3, 8, 128), F32), vm((8, 3, 8, 128), F32), vm((4, 8, 128), F32), vm((4, 8, 128), F32),
         dma((7,)), dma, dma, dma((4,)), dma((4,)),
+        dma((4, 2)), dma((4, 2)), dma((4, 2)), dma((4, 2)), dma((4, 2)), dma((4, 2)), dma((4, 2)), dma((4, 2)),
         dma((4,)), dma((4,)), dma((4,)), dma((4,)), dma((4,)), dma((4,)), dma((4,)), dma((4,)),
-        dma((4,)), dma((4,)), dma((4,)), dma((4,)), dma((4,)), dma((4,)), dma((4,)), dma((4,)),
-        dma((2,)), dma((2,)), dma((2, 4)), dma((8,)), dma((8,)), dma((8,)),
-        dma((2, 4)), dma((8,)), dma((8,)), dma((8,)), dma((4,)), dma((4,)), dma((4,)), dma((4,)),
-        dma((4,)), dma, dma, dma,
-        dma((4,)), dma((4,)), dma((4,)), dma((4,)), dma, dma((4,)), dma((4,)), dma((4,)), dma((4,)), dma((4,)),
-        dma((4, 2)), dma((4, 2)), dma((4,)), dma, dma((4, 2)), dma((4, 2)), dma((4,)), dma((4,)),
+        dma((2,)), dma((2,)), dma((2, 2)), dma((2, 2)), dma((8,)), dma((8,)), dma((8,)),
+        dma((2, 2)), dma((2, 2)), dma((8,)), dma((8,)), dma((8,)),
+        dma((2,)), dma((2,)), dma((4,)), dma((4,)), dma((4,)), dma((2,)), dma, dma, dma,
+        dma((5,)), dma((5,)), dma((4,)), dma((4,)), dma((4,)), dma((4,)), dma, dma((2,)),
+        dma, dma((2,)), dma((4,)), dma, dma, dma((2,)), dma((4,)), dma,
+        dma((3,)), dma((4,)), dma((4, 2)), dma((2,)), dma, dma((3,)), dma((4,)), dma((4, 2)), dma((3,)), dma((4,)),
         dma((4, 2)), dma((8,)), dma((4,)), dma((4,)),
     ]
     anywhere = pl.BlockSpec(memory_space=pl.ANY)
@@ -1048,12 +1281,98 @@
         ),
         cost_estimate=pl.CostEstimate(flops=11 * 10**9, bytes_accessed=16 * 2**20, transcendentals=3 * 2**20),
     )(inputs, cotangent, w_query, w_key, w_value, w_out, w_in, w_down, pack, bucket_row)
-    proj = proj.reshape(2, 2, 128, 3, 2, 128).transpose(3, 2, 1, 4, 0, 5).reshape(3, 128, 1024).astype(F32)
-    hidden = hidden.transpose(2, 0, 1, 3).reshape(128, 4096).astype(F32)
-    return (
-        output, grad_inputs, proj[0], proj[1], proj[2], out.astype(F32), hidden, down.astype(F32),
-        small[0], small[1], small[2, :64],
-    )
+    return finish(output, grad_inputs, proj, out, hidden, down, small)
+
+
+def finish_kernel(
+    output, grad_inputs, proj, out, hidden, down, small,
+    o_output, o_inputs, o_query, o_key, o_value, o_out, o_in, o_down, o_attn, o_mlp, o_bias,
+    b_output, b_inputs, b_proj, b_out, b_hidden, b_down, b_small, w_proj, w_out, w_in, w_down, got, left,
+):
+    moves = [
+        pltpu.make_async_copy(proj, b_proj, got.at[0]),
+        pltpu.make_async_copy(hidden, b_hidden, got.at[1]),
+        pltpu.make_async_copy(down, b_down, got.at[2]),
+        pltpu.make_async_copy(out, b_out, got.at[3]),
+        pltpu.make_async_copy(small, b_small, got.at[4]),
+        pltpu.make_async_copy(output, b_output, got.at[5]),
+        pltpu.make_async_copy(grad_inputs, b_inputs, got.at[6]),
+    ]
+    for move in moves:
+        move.start()
+    sends = []
+
+    def write(src, dst, slot):
+        copy = pltpu.make_async_copy(src, dst, left.at[slot])
+        copy.start()
+        sends.append(copy)
+
+    moves[0].wait()
+    for w, place in enumerate((o_query, o_key, o_value)):
+        for q in range(4):
+            x, y = q // 2, q % 2
+            for j in range(2):
+                first = 512 * y + 256 * j + 128 * x
+                w_proj[w, :, first : first + 128] = b_proj[q, :, 256 * w + 128 * j : 256 * w + 128 * j + 128].astype(F32)
+        write(w_proj.at[w], place, w)
+    moves[1].wait()
+    for r in range(4):
+        rows = slice(32 * r, 32 * r + 32)
+        for z in range(4):
+            for q in range(4):
+                w_in[rows, 256 * (4 * z + q) : 256 * (4 * z + q) + 256] = b_hidden[z, q, rows, :].astype(F32)
+        write(w_in.at[pl.ds(32 * r, 32)], o_in.at[pl.ds(32 * r, 32)], 3 + r)
+    moves[2].wait()
+    for r in range(4):
+        rows = slice(128 * r, 128 * r + 128)
+        w_down[rows, :] = b_down[rows, :].astype(F32)
+        write(w_down.at[pl.ds(128 * r, 128)], o_down.at[pl.ds(128 * r, 128)], 7 + r)
+    moves[3].wait()
+    w_out[...] = b_out[...].astype(F32)
+    write(w_out, o_out, 11)
+    moves[4].wait()
+    o_attn[...] = b_small[0:1, :]
+    o_mlp[...] = b_small[1:2, :]
+    o_bias[...] = b_small[2:3, 0:64]
+    moves[5].wait()
+    write(b_output, o_output, 12)
+    moves[6].wait()
+    write(b_inputs, o_inputs, 13)
+    for copy in sends:
+        copy.wait()
+
+
+def finish(output, grad_inputs, proj, out, hidden, down, small):
+    shape = jax.ShapeDtypeStruct
+    vm = pltpu.VMEM
+    anywhere = pl.BlockSpec(memory_space=pl.ANY)
+    in_vmem = pl.BlockSpec(memory_space=pltpu.VMEM)
+    results = pl.pallas_call(
+        finish_kernel,
+        out_shape=(
+            shape(output.shape, BF),
+            shape(grad_inputs.shape, BF),
+            shape((128, 1024), F32),
+            shape((128, 1024), F32),
+            shape((128, 1024), F32),
+            shape((128, 1024), F32),
+            shape((128, 4096), F32),
+            shape((512, 1024), F32),
+            shape((1, 128), F32),
+            shape((1, 128), F32),
+            shape((1, 64), F32),
+        ),
+        in_specs=[anywhere] * 7,
+        out_specs=(anywhere,) * 8 + (in_vmem,) * 3,
+        scratch_shapes=[
+            vm(output.shape, BF), vm(grad_inputs.shape, BF), vm(proj.shape, BF), vm(out.shape, BF), vm(hidden.shape, BF), vm(down.shape, BF), vm(small.shape, F32),
+            vm((3, 128, 1024), F32), vm((128, 1024), F32), vm((128, 4096), F32), vm((512, 1024), F32),
+            pltpu.SemaphoreType.DMA((7,)), pltpu.SemaphoreType.DMA((14,)),
+        ],
+        compiler_params=pltpu.CompilerParams(vmem_limit_bytes=63 << 20),
+        cost_estimate=pl.CostEstimate(flops=0, bytes_accessed=10 * 2**20, transcendentals=0),
+    )(output, grad_inputs, proj, out, hidden, down, small)
+    return results[:8] + (results[8].reshape(128), results[9].reshape(128), results[10].reshape(64))
 
 
 def solution(mesh):

time: 221 us -> 172 us (0.78)
  the two profiles are of different devices: /device:TPU:27 before, /device:TPU:0 now
where the time goes in v2:
time: 172 us; the launch traced here: 169 us
  Pallas kernels  165 us (96%)
  other arithmetic  1.99 us (1%)
    pallas_call x1, Pallas kernels, plane_shards(): pl.pallas_call(fused_layer, out_shape=(shape((1, TOKENS, WIDTH), BF), sha...  160 us
    pallas_call x1, Pallas kernels, finish(): pl.pallas_call(finish_kernel, out_shape=(shape(output.shape, BF), shape(g...  4.68 us

profile of v2, /device:TPU:0, one launch (start us, length us, event | category | flops | bytes accessed | tf_op | source)
XLA Modules:
  0.0 169.1 jit_solution(15621816770316837427)
XLA Ops:
  0.6 0.7 bitcast_convert_fusion.2
  1.3 0.1 pad.14.clone
  1.4 0.7 bitcast_convert_fusion
  2.1 0.7 maximum_maximum_fusion.pack_in
  2.7 1.3 pad.10
  4.0 160.4 %shard_map.203 = (bf16[1,128,1024]{2,1,0:T(8,128)(2,1)}, bf16[1,128,1024]{2,1,0:T(8,128)(2,1)}, bf16[4,128,768]{2,1,0:T(8,128)(2,1)}, bf16[128,1024]{1,0:T(8,128...) custom-call(bf16[1,128,1024]{2,1,0:T(8,128)(2,1)} %x_in.1, ...), custom_call_target="tpu_custom_call" | custom-call | flops 11000000512 | bytes 16777216 | tf_op jit(solution)/shard_map/pallas_call | solution.py:1265
  164.4 4.7 %shard_map.204 = (bf16[1,128,1024]{2,1,0:T(8,128)(2,1)}, bf16[1,128,1024]{2,1,0:T(8,128)(2,1)}, f32[128,1024]{1,0:T(8,128)}, f32[128,1024]{1,0:T(8,128)}, f32[12...) custom-call(bf16[1,128,1024]{2,1,0:T(8,128)(2,1)} %get-tuple-element, ...), custom_call_target="tpu_custom_call" | custom-call | bytes 10485760 | tf_op jit(solution)/shard_map/pallas_call | solution.py:1350
  (1 shorter events, 0.0 us)

commit v3 on v2

--- a/solution.py
+++ b/solution.py
@@ -312,14 +312,14 @@
     XO, CO, GP, XB, COT, N1, NTB, GAL, WQKV, WOUT, WIN, WDOWN,
     QKV, PROB, PLOW, BIAS, AT, ACT, SLOPE, GPRE, GATT, DQKV, DS, BACC,
     SA, SG, SO, SN, RA, RG, RO, RN, HID, GH, NTS, GALS,
-    DQ, DO, DI, DD, SIBQ, SIBO, SIBI, SIBD, ZQ, ZO, ZI, ZD, RZQ, RZO, REI, RED, RCI, RCD, FQ, FO, FI, FD,
+    DQ, DO, DI, DD, SIBQ, SIBO, SIBI, SIBD, ZQ, ZO, ZI, ZD, RZQ, RZO, REI, RZD, RCI, FQ, FO, FI, FD,
     SMALL, RSMALL, PSMALL, RZSMALL,
-    loc, gpx_s, gpx_r, gpz_s, gpz_r, xb_s, xb_r, co_s, co_r, nt_s, nt_r, ga_s, ga_r,
+    loc, gpx_s, gpx_r, gpz_s, gpz_r, xb_s, xb_r, xb_p, co_s, co_r, co_p, nt_s, nt_r, nt_p, ga_s, ga_r, ga_p,
     a_s, a_r, g_s, g_r, o_s, o_r, n_s, n_r,
     wx_s, wx_r, wqz_s, wqf_s, wqz_r, wqb_s, wqb_r, wiz_s, wif_s, wiz_r, wib_s, wib_r,
     wdz_s, wdf_s, wdz_r, wdb_s, wdb_r, woz_s, woz_r, wob_s, wob_r,
-    sib_s, sib_r, zq_s, zq_r, zv_s, zv_r, zo_s, zo_r, zi_s, zie_s, zi_r, zic_r, zd_s, zde_s, zd_r, zdc_r,
-    fq_s, fqb_s, fq_r, fo_s, fo_r, fi_s, fib_s, fi_r, fd_s, fd_r, sp_s, sp_r, sz_s, sz_r,
+    sib_s, sib_r, zq_s, zq_r, zv_s, zv_r, zo_s, zo_r, zi_s, zie_s, zi_r, zic_r, zd_s, zd_r,
+    fq_s, fqb_s, fq_r, fqb_r, fo_s, fo_r, fi_s, fib_s, fi_r, fib_r, fd_s, fd_r, sp_s, sp_r, sz_s, sz_r,
 ):
     c = lax.axis_index("ctx")
     f = lax.axis_index("fsdp")
@@ -348,11 +348,6 @@
             if i or j:
                 plane.append((ci, 2 * z + xj))
 
-    barrier = pltpu.get_barrier_semaphore()
-    for device in plane + [zdev(t) for t in zs]:
-        pl.semaphore_signal(barrier, inc=1, device_id=device, device_id_type=MESH_ID)
-    pl.semaphore_wait(barrier, 10)
-
     def recv(dst, sem):
         remote(dst, dst, sem, sem, sib).wait_recv()
 
@@ -362,51 +357,52 @@
     def block_half(buf, b, h):
         return buf.at[rows_at(b * TOKENS + 64 * h, 64)]
 
-    def gather_send(src, dst, send, got):
-        for h in range(2):
-            half_src = src.at[pl.ds(64 * h, 64)]
-            remote(half_src, block_half(dst, c, h), send.at[1, h], got.at[c, h], (2 * y + x, f1)).start()
-        for h in (1, 0):
-            half_src = src.at[pl.ds(64 * h, 64)]
-            remote(half_src, block_half(dst, c, h), send.at[2, h], got.at[c, h], (2 * y1 + x, f)).start()
-        for h in range(2):
-            half_src = src.at[pl.ds(64 * h, 64)]
-
-            @pl.when(k == x)
-            def _():
-                pltpu.make_async_copy(half_src, block_half(dst, c, h), got.at[c, h]).start()
-
-            @pl.when(k != x)
-            def _():
-                remote(half_src, block_half(dst, c, h), send.at[0, h], got.at[c, h], sib).start()
+    def gather_send(src, dst, send, got, passed):
+        halves = [src.at[pl.ds(64 * h, 64)] for h in range(2)]
+        places = [block_half(dst, c, h) for h in range(2)]
+        x_worker, y_worker = (2 * y + x, f1), (2 * y1 + x, f)
+        remote(halves[0], places[0], send, passed.at[k], x_worker).start()
+        remote(halves[1], places[1], send, passed.at[k], y_worker).start()
+        remote(halves[1], places[1], send, got.at[c], x_worker).start()
+        remote(halves[0], places[0], send, got.at[c], y_worker).start()
+        whole = dst.at[rows_at(c * TOKENS, TOKENS)]
+
+        @pl.when(k == x)
+        def _():
+            pltpu.make_async_copy(src, whole, got.at[c]).start()
+
+        @pl.when(k != x)
+        def _():
+            remote(src, whole, send, got.at[c], sib).start()
 
     same = 1 - lax.rem(x + k, 2)
     pass_y = y + same * (1 - 2 * y)
     pass_to = (same * c + (1 - same) * (2 * y1 + k), same * f1 + (1 - same) * f)
 
-    def gather_pass(dst, send, got):
+    def gather_pass(dst, send, got, passed):
         for i in range(2):
-            piece = block_half(dst, 2 * pass_y + i, same)
-            recv(piece, got.at[2 * pass_y + i, same])
-            remote(piece, piece, send.at[3, i], got.at[2 * pass_y + i, same], pass_to).start()
+            b = 2 * pass_y + i
+            piece = block_half(dst, b, same)
+            recv(piece, passed.at[i])
+            remote(piece, piece, send, got.at[b], pass_to).start()
 
     def gather_wait(dst, got, b):
-        for h in range(2):
-
-            @pl.when(jnp.logical_not((b // 2 == pass_y) & (same == h)))
-            def _():
-                recv(block_half(dst, b, h), got.at[b, h])
-
-    def gather_sent(src, dst, send):
-        for h in range(2):
-            half_src = src.at[pl.ds(64 * h, 64)]
-            sent(half_src, send.at[1, h])
-            sent(half_src, send.at[2, h])
-            sent(block_half(dst, 2 * pass_y + h, same), send.at[3, h])
-
-            @pl.when(k != x)
-            def _():
-                sent(half_src, send.at[0, h])
+        @pl.when(b // 2 == pass_y)
+        def _():
+            recv(block_half(dst, b, 1 - same), got.at[b])
+
+        @pl.when(b // 2 != pass_y)
+        def _():
+            recv(dst.at[rows_at(b * TOKENS, TOKENS)], got.at[b])
+
+    def four_sent(buf, send):
+        @pl.when(k == x)
+        def _():
+            sent(buf.at[pl.ds(0, 384)], send)
+
+        @pl.when(k != x)
+        def _():
+            sent(buf, send)
 
     def scatter_send(buf, dst, send, got, b):
         src = buf.at[rows_at(b * TOKENS, TOKENS)]
@@ -414,29 +410,18 @@
 
         @pl.when(here)
         def _():
-            pltpu.make_async_copy(src, dst.at[q], got.at[q]).start()
+            pltpu.make_async_copy(src, dst.at[q], got).start()
 
         @pl.when(jnp.logical_not(here))
         def _():
-            remote(src, dst.at[q], send.at[b], got.at[q], (b, 2 * z + k)).start()
-
-    def scatter_sent(buf, send):
-        for b in range(4):
-
-            @pl.when(jnp.logical_not((c == b) & (x == k)))
-            def _():
-                sent(buf.at[pl.ds(b * TOKENS, TOKENS)], send.at[b])
+            remote(src, dst.at[q], send, got, (b, 2 * z + k)).start()
 
     def half(fb, kk):
         return rows_at(fb * 128 + kk * 64, 64)
 
     def z_send(piece, send, got):
-        remote(piece, piece, send.at[1], got, zdev(far)).start()
-        remote(piece, piece, send.at[0], got, zdev(near)).start()
-
-    def z_sent(piece, send):
-        sent(piece, send.at[0])
-        sent(piece, send.at[1])
+        remote(piece, piece, send, got, zdev(far)).start()
+        remote(piece, piece, send, got, zdev(near)).start()
 
     def take(piece, got, bsend, bgot):
         recv(piece, got)
@@ -449,31 +434,15 @@
         return 2 * t + xx
 
     own_x = pltpu.make_async_copy(x_in.at[0], XO, loc.at[0])
-    own_x.start()
     own_c = pltpu.make_async_copy(cot_in.at[0], CO, loc.at[1])
-    own_c.start()
     own_pack = pltpu.make_async_copy(pack_in, GP.at[f], loc.at[2])
-    own_pack.start()
-    remote(pack_in, GP.at[f], gpx_s, gpx_r, xdev).start()
     proj = (wq_in, wk_in, wv_in)
     myrows = pl.ds(pl.multiple_of(128 * f, 128), 128)
     for w in range(3):
         for j in range(2):
             src = proj[w].at[:, pl.ds(pl.multiple_of(128 * (2 * (2 * y + j) + x), 128), 128)]
             pltpu.make_async_copy(src, WQKV.at[myrows, pl.ds(256 * w + 128 * j, 128)], loc.at[3]).start()
-    for w in range(3):
-        for j in range(2):
-            src = proj[w].at[rows_at(64 * k, 64), pl.ds(pl.multiple_of(128 * (2 * (2 * y + j) + x1), 128), 128)]
-            remote(src, WQKV.at[half(f, k), pl.ds(256 * w + 128 * j, 128)], wx_s.at[0], wx_r.at[0], xdev).start()
-    gather_send(x_in.at[0], XB, xb_s, xb_r)
-    for j in range(4):
-        src = wi_in.at[rows_at(64 * k, 64), pl.ds(pl.multiple_of(512 * (2 * j + x1) + 256 * y, 256), 256)]
-        remote(src, WIN.at[half(f, k), pl.ds(256 * j, 256)], wx_s.at[1], wx_r.at[1], xdev).start()
-    out_piece = WOUT.at[rows_at(128 * k, 128)]
-    out_other = WOUT.at[rows_at(128 * k1, 128)]
-
-    pltpu.make_async_copy(WQKV.at[myrows], WQKV.at[myrows], loc.at[3]).wait()
-    z_send(WQKV.at[half(f, k)], wqz_s.at[0], wqz_r.at[f])
+    own_pack.start()
     for j in range(4):
         src = wi_in.at[:, pl.ds(pl.multiple_of(512 * (2 * j + x) + 256 * y, 256), 256)]
         pltpu.make_async_copy(src, WIN.at[myrows, pl.ds(256 * j, 256)], loc.at[4]).start()
@@ -485,12 +454,64 @@
     def _():
         pltpu.make_async_copy(wo_in, WOUT.at[rows_at(128 * lax.rem(z, 2), 128)], loc.at[6]).start()
 
+    own_x.start()
+    own_c.start()
+
+    barrier = pltpu.get_barrier_semaphore()
+    for device in plane + [zdev(t) for t in zs]:
+        pl.semaphore_signal(barrier, inc=1, device_id=device, device_id_type=MESH_ID)
+    pl.semaphore_wait(barrier, 10)
+
+
+    remote(pack_in, GP.at[f], gpx_s, gpx_r, xdev).start()
+    for w in range(3):
+        for j in range(2):
+            src = proj[w].at[rows_at(64 * k, 64), pl.ds(pl.multiple_of(128 * (2 * (2 * y + j) + x1), 128), 128)]
+            remote(src, WQKV.at[half(f, k), pl.ds(256 * w + 128 * j, 128)], wx_s.at[0], wx_r.at[0], xdev).start()
+    pltpu.make_async_copy(WQKV.at[myrows], WQKV.at[myrows], loc.at[3]).wait()
+    z_send(WQKV.at[half(f, k)], wqz_s, wqz_r.at[f])
+    gather_send(x_in.at[0], XB, xb_s, xb_r, xb_p)
+    for j in range(4):
+        src = wi_in.at[rows_at(64 * k, 64), pl.ds(pl.multiple_of(512 * (2 * j + x1) + 256 * y, 256), 256)]
+        remote(src, WIN.at[half(f, k), pl.ds(256 * j, 256)], wx_s.at[1], wx_r.at[1], xdev).start()
+    out_piece = WOUT.at[rows_at(128 * k, 128)]
+    out_other = WOUT.at[rows_at(128 * k1, 128)]
+
     own_pack.wait()
     recv(GP.at[f1], gpx_r)
     for t in zs:
-        remote(GP.at[pl.ds(2 * z, 2)], GP.at[pl.ds(2 * z, 2)], gpz_s.at[t], gpz_r.at[z], zdev(t)).start()
-    for t in zs:
-        recv(GP.at[pl.ds(2 * t, 2)], gpz_r.at[t])
+        remote(GP.at[pl.ds(2 * z, 2)], GP.at[pl.ds(2 * z, 2)], gpz_s, gpz_r, zdev(t)).start()
+    recv(WQKV.at[half(f1, k)], wx_r.at[0])
+    z_send(WQKV.at[half(f1, k)], wqz_s, wqz_r.at[f1])
+    remote(WQKV.at[half(f1, k)], WQKV.at[half(f1, k)], wqb_s, wqb_r, sib).start()
+
+    @pl.when(z == c)
+    def _():
+        remote(wo_in, out_piece, woz_s, woz_r, zdev(far)).start()
+        remote(wo_in, out_piece, woz_s, woz_r, zdev(near)).start()
+
+    gather_pass(XB, xb_s, xb_r, xb_p)
+    gather_send(cot_in.at[0], COT, co_s, co_r, co_p)
+
+    def take_proj(xx):
+        g = of_row(near, xx)
+        take(WQKV.at[half(g, k)], wqz_r.at[g], wqb_s, wqb_r)
+        for n in range(2):
+            h = of_row(others[n], xx)
+            piece = WQKV.at[half(h, k)]
+            recv(piece, wqz_r.at[h])
+
+            @pl.when(middle)
+            def _():
+                pass_on(piece, wqf_s, wqz_r.at[h])
+
+            remote(piece, piece, wqb_s, wqb_r, sib).start()
+
+    @pl.when(middle)
+    def _():
+        take_proj(x)
+
+    recv(GP.at[pl.ds(0, 6)], gpz_r)
 
     def row_of(index):
         return jnp.concatenate([GP[g, index : index + 1, :] for g in range(8)], axis=1)
@@ -514,15 +535,6 @@
         spread = jnp.broadcast_to(offsets[h : h + 1, :], (128, WIDTH))
         BIAS[h] = pltpu.roll(spread, WIDTH - 127, 1, stride=1, stride_axis=0)
         BACC[h] = jnp.zeros((128, WIDTH), F32)
-
-    recv(WQKV.at[half(f1, k)], wx_r.at[0])
-    z_send(WQKV.at[half(f1, k)], wqz_s.at[1], wqz_r.at[f1])
-    remote(WQKV.at[half(f1, k)], WQKV.at[half(f1, k)], wqb_s.at[f1], wqb_r.at[f1], sib).start()
-
-    @pl.when(z == c)
-    def _():
-        remote(wo_in, out_piece, woz_s.at[1], woz_r, zdev(far)).start()
-        remote(wo_in, out_piece, woz_s.at[0], woz_r, zdev(near)).start()
 
     gain_one = row_of(0)
 
@@ -539,31 +551,20 @@
 
         return lax.fori_loop(0, 4, chunk, carry)
 
-    gather_pass(XB, xb_s, xb_r)
-    gather_send(cot_in.at[0], COT, co_s, co_r)
     lax.fori_loop(0, 4, norm_block, 0)
 
-    for r, own in enumerate((f, f1)):
-        z_sent(WQKV.at[half(own, k)], wqz_s.at[r])
+    sent(WQKV.at[pl.ds(0, 256)], wqz_s)
     pltpu.make_async_copy(WIN.at[myrows], WIN.at[myrows], loc.at[4]).wait()
-    z_send(WIN.at[half(f, k)], wiz_s.at[0], wiz_r.at[f])
+    z_send(WIN.at[half(f, k)], wiz_s, wiz_r.at[f])
     recv(WIN.at[half(f1, k)], wx_r.at[1])
-    z_send(WIN.at[half(f1, k)], wiz_s.at[1], wiz_r.at[f1])
-    remote(WIN.at[half(f1, k)], WIN.at[half(f1, k)], wib_s.at[f1], wib_r.at[f1], sib).start()
-    for xx in (x, x1):
-        g = of_row(near, xx)
-        take(WQKV.at[half(g, k)], wqz_r.at[g], wqb_s.at[g], wqb_r.at[g])
-    for i, xx in enumerate((x, x1)):
-        for n in range(2):
-            g = of_row(others[n], xx)
-            piece = WQKV.at[half(g, k)]
-            recv(piece, wqz_r.at[g])
-
-            @pl.when(middle)
-            def _():
-                pass_on(piece, wqf_s.at[n, i], wqz_r.at[g])
-
-            remote(piece, piece, wqb_s.at[g], wqb_r.at[g], sib).start()
+    z_send(WIN.at[half(f1, k)], wiz_s, wiz_r.at[f1])
+    remote(WIN.at[half(f1, k)], WIN.at[half(f1, k)], wib_s, wib_r, sib).start()
+
+    @pl.when(at_end)
+    def _():
+        take_proj(x)
+
+    take_proj(x1)
 
     @pl.when(z != c)
     def _():
@@ -571,18 +572,14 @@
 
         @pl.when(middle & (z // 2 != c // 2))
         def _():
-            pass_on(out_piece, woz_s.at[0], woz_r)
+            pass_on(out_piece, woz_s, woz_r)
 
         remote(out_piece, out_piece, wob_s, wob_r, sib).start()
 
     down_half = rows_at(256 * z + 128 * k, 128)
     pltpu.make_async_copy(WDOWN.at[rows_at(256 * z, 256)], WDOWN.at[rows_at(256 * z, 256)], loc.at[5]).wait()
     z_send(WDOWN.at[down_half], wdz_s, wdz_r.at[z])
-
-    for t in zs:
-        for xx in (x, x1):
-            recv(WQKV.at[half(2 * t + xx, k1)], wqb_r.at[2 * t + xx])
-    recv(WQKV.at[half(f1, k1)], wqb_r.at[f1])
+    recv(WQKV.at[pl.ds(0, 448)], wqb_r)
 
     def project(n, carry):
         cols = rows_at(256 * n, 256)
@@ -600,7 +597,7 @@
     def _():
         recv(out_other, wob_r)
 
-    gather_pass(COT, co_s, co_r)
+    gather_pass(COT, co_s, co_r, co_p)
 
     low_lanes = lax.broadcasted_iota(jnp.int32, (TOKENS, 128), 1) < 64
 
@@ -634,7 +631,7 @@
 
     for xx in (x, x1):
         g = of_row(near, xx)
-        take(WIN.at[half(g, k)], wiz_r.at[g], wib_s.at[g], wib_r.at[g])
+        take(WIN.at[half(g, k)], wiz_r.at[g], wib_s, wib_r)
 
     @pl.when(middle)
     def _():
@@ -642,14 +639,13 @@
             for n in range(2):
                 g = of_row(others[n], xx)
                 recv(WIN.at[half(g, k)], wiz_r.at[g])
-                pass_on(WIN.at[half(g, k)], wif_s.at[n, i], wiz_r.at[g])
-                remote(WIN.at[half(g, k)], WIN.at[half(g, k)], wib_s.at[g], wib_r.at[g], sib).start()
+                pass_on(WIN.at[half(g, k)], wif_s, wiz_r.at[g])
+                remote(WIN.at[half(g, k)], WIN.at[half(g, k)], wib_s, wib_r, sib).start()
 
     own_x.wait()
     own_c.wait()
     gain_two = row_of(1)
-    for s in range(4):
-        recv(RA.at[s], a_r.at[s])
+    recv(RA, a_r)
 
     def home_forward(r, carry):
         rows = rows_at(r * 32, 32)
@@ -662,34 +658,31 @@
         return carry
 
     lax.fori_loop(0, 4, home_forward, 0)
-    gather_send(NTS, NTB, nt_s, nt_r)
+    gather_send(NTS, NTB, nt_s, nt_r, nt_p)
 
     def down_piece(t, kk):
         return WDOWN.at[rows_at(256 * t + 128 * kk, 128)]
 
-    take(down_piece(near, k), wdz_r.at[near], wdb_s.at[near], wdb_r.at[near])
+    take(down_piece(near, k), wdz_r.at[near], wdb_s, wdb_r)
 
     @pl.when(middle)
     def _():
         for n in range(2):
             t = others[n]
             recv(down_piece(t, k), wdz_r.at[t])
-            pass_on(down_piece(t, k), wdf_s.at[n], wdz_r.at[t])
-            remote(down_piece(t, k), down_piece(t, k), wdb_s.at[t], wdb_r.at[t], sib).start()
+            pass_on(down_piece(t, k), wdf_s, wdz_r.at[t])
+            remote(down_piece(t, k), down_piece(t, k), wdb_s, wdb_r, sib).start()
 
     @pl.when(at_end)
     def _():
         for xx in (x, x1):
             for t in others:
                 g = of_row(t, xx)
-                take(WIN.at[half(g, k)], wiz_r.at[g], wib_s.at[g], wib_r.at[g])
-
-    recv(WIN.at[half(f1, k1)], wib_r.at[f1])
-    for t in zs:
-        for xx in (x, x1):
-            recv(WIN.at[half(2 * t + xx, k1)], wib_r.at[2 * t + xx])
-
-    gather_pass(NTB, nt_s, nt_r)
+                take(WIN.at[half(g, k)], wiz_r.at[g], wib_s, wib_r)
+
+    recv(WIN.at[pl.ds(0, 448)], wib_r)
+
+    gather_pass(NTB, nt_s, nt_r, nt_p)
 
     def feed(i, carry):
         yy = lax.rem(y + i, 2)
@@ -724,19 +717,9 @@
     @pl.when(at_end)
     def _():
         for t in others:
-            take(down_piece(t, k), wdz_r.at[t], wdb_s.at[t], wdb_r.at[t])
-
-    for t in zs:
-        recv(down_piece(t, k1), wdb_r.at[t])
-
-    def z_reduce_send(terms, got, send, esend, recv_sem):
-        @pl.when(at_end)
-        def _():
-            for n in range(2):
-                t = others[n]
-                remote(terms(t), got(t), esend.at[n], recv_sem.at[t], zdev(near)).start()
-
-        remote(terms(near), got(near), send, recv_sem.at[near], zdev(near)).start()
+            take(down_piece(t, k), wdz_r.at[t], wdb_s, wdb_r)
+
+    recv(WDOWN.at[pl.ds(0, 384)], wdb_r)
 
     recv(SIBD, sib_r.at[0])
 
@@ -745,7 +728,8 @@
         return carry
 
     lax.fori_loop(0, 4, join_down, 0)
-    z_reduce_send(lambda t: ZD.at[t], lambda t: RED.at[t], zd_s, zde_s, zd_r)
+    for t in zs:
+        remote(ZD.at[t], RZD.at[z], zd_s, zd_r, zdev(t)).start()
 
     def back_feed(i, carry):
         yy = lax.rem(y1 + i, 2)
@@ -794,20 +778,16 @@
         return carry
 
     lax.fori_loop(0, 8, join_in, 0)
-    z_reduce_send(
-        lambda t: ZI.at[pl.ds(2 * t, 2)], lambda t: REI.at[pl.ds(2 * t, 2)], zi_s, zie_s, zi_r
-    )
-
-    @pl.when(middle)
+    def in_rows(ref, t):
+        return ref.at[pl.ds(2 * t, 2)]
+
+    @pl.when(at_end)
     def _():
         for n in range(2):
             t = others[n]
-            recv(RED.at[t], zd_r.at[t])
-            ZD[t] = (ZD[t].astype(F32) + RED[t].astype(F32)).astype(BF)
-            remote(ZD.at[t], RCD, zde_s.at[n], zdc_r, zdev(t)).start()
-
-    for s in range(4):
-        recv(RG.at[s], g_r.at[s])
+            remote(in_rows(ZI, t), in_rows(REI, t), zie_s, zi_r.at[t], zdev(near)).start()
+
+    recv(RG, g_r)
 
     def home_back(r, total):
         rows = rows_at(r * 32, 32)
@@ -824,12 +804,13 @@
         return total + jnp.sum((grad * hidden * scale).reshape(4, 8, WIDTH), axis=0)
 
     mlp_gain_grad = lax.fori_loop(0, 4, home_back, jnp.zeros((8, WIDTH), F32))
-    gather_send(GALS, GAL, ga_s, ga_r)
+    gather_send(GALS, GAL, ga_s, ga_r, ga_p)
+
     mlp_gain_grad = jnp.sum(mlp_gain_grad, axis=0, keepdims=True)
     for g in range(8):
         SMALL[1, g : g + 1, :] = mlp_gain_grad[:, 128 * g : 128 * g + 128]
 
-    gather_pass(GAL, ga_s, ga_r)
+    gather_pass(GAL, ga_s, ga_r, ga_p)
 
     def back_out(i, carry):
         b = lax.rem(2 * y + i, 4)
@@ -888,7 +869,7 @@
     def z_scatter(cols, send, got):
         for t in zs:
             remote(
-                ZQ.at[pl.ds(2 * t, 2), :, cols], RZQ.at[z, :, :, cols], send.at[t], got.at[z], zdev(t)
+                ZQ.at[pl.ds(2 * t, 2), :, cols], RZQ.at[z, :, :, cols], send, got, zdev(t)
             ).start()
 
     recv(SIBQ.at[:, :, value_cols], sib_r.at[2])
@@ -908,20 +889,16 @@
     def _():
         remote(ZO, RZO.at[0], zo_s, zo_r.at[0], zdev(near)).start()
 
+    remote(in_rows(ZI, near), in_rows(REI, near), zi_s, zi_r.at[near], zdev(near)).start()
+
     @pl.when(middle)
     def _():
         for n in range(2):
             t = others[n]
-            recv(REI.at[pl.ds(2 * t, 2)], zi_r.at[t])
+            recv(in_rows(REI, t), zi_r.at[t])
             for xx in range(2):
                 ZI[2 * t + xx] = (ZI[2 * t + xx].astype(F32) + REI[2 * t + xx].astype(F32)).astype(BF)
-            remote(ZI.at[pl.ds(2 * t, 2)], RCI, zie_s.at[n], zic_r, zdev(t)).start()
-
-    @pl.when(jnp.logical_not(out_near) & middle)
-    def _():
-        recv(RZO.at[0], zo_r.at[0])
-        ZO[...] = (ZO[...].astype(F32) + RZO[0].astype(F32)).astype(BF)
-        remote(ZO, RZO.at[1], zo_s, zo_r.at[1], zdev(c)).start()
+            remote(in_rows(ZI, t), RCI, zie_s, zic_r, zdev(t)).start()
 
     def attend_back(i, carry):
         rows = rows_at(i * TOKENS, TOKENS)
@@ -971,6 +948,13 @@
     join_proj(0, 512)
     z_scatter(other_cols, zq_s, zq_r)
 
+    @pl.when(jnp.logical_not(out_near) & middle)
+    def _():
+        recv(RZO.at[0], zo_r.at[0])
+        ZO[...] = (ZO[...].astype(F32) + RZO[0].astype(F32)).astype(BF)
+        remote(ZO, RZO.at[1], zo_s, zo_r.at[1], zdev(c)).start()
+
+
     head_sums = []
     for h in range(4):
         rest = BACC[h]
@@ -994,43 +978,35 @@
 
     lax.fori_loop(0, 8, bucket_sums, 0)
 
-    recv(RED.at[z], zd_r.at[z])
-    recv(RCD, zdc_r)
-    FD[...] = (ZD[z].astype(F32) + RED[z].astype(F32) + RCD[...].astype(F32)).astype(BF)
+    recv(RZD.at[pl.ds(0, 3)], zd_r)
+    total = ZD[z].astype(F32)
+    for t in zs:
+        total = total + RZD[t].astype(F32)
+    FD[...] = total.astype(BF)
 
     def down_rows(cc):
         return odown.at[rows_at(128 * cc, 128)]
 
     y_core = (2 * y1 + k, f)
-    remote(FD, down_rows(c), fd_s.at[1], fd_r.at[c], y_core).start()
-    remote(FD, down_rows(c), fd_s.at[0], fd_r.at[c], sib).start()
-    pltpu.make_async_copy(FD, down_rows(c), fd_r.at[c]).start()
-
-    def spread(final, place, send, bsend, got):
-        remote(final.at[x1], place(q, k), send.at[2], got.at[q, k], (2 * y1 + k, f1)).start()
-        remote(final.at[x1], place(q, k), send.at[1], got.at[q, k], (c, f1)).start()
-        remote(final.at[x], place(q, k), send.at[0], got.at[q, k], y_core).start()
-        remote(final.at[x], place(q, k), bsend.at[0], got.at[q, k], sib).start()
-        pltpu.make_async_copy(final.at[x], place(q, k), got.at[q, k]).start()
+    four_sent(SN, n_s)
+    remote(FD, down_rows(c), fd_s, fd_r.at[1], y_core).start()
+    remote(FD, down_rows(c), fd_s, fd_r.at[2], sib).start()
+    pltpu.make_async_copy(FD, down_rows(c), fd_r.at[0]).start()
+
+    def spread(final, place, send, bsend, got, bgot):
+        remote(final.at[x1], place(q, k), send, got.at[3], (2 * y1 + k, f1)).start()
+        remote(final.at[x1], place(q, k), send, got.at[2], (c, f1)).start()
+        remote(final.at[x], place(q, k), send, got.at[1], y_core).start()
+        remote(final.at[x], place(q, k), bsend, bgot, sib).start()
+        pltpu.make_async_copy(final.at[x], place(q, k), got.at[0]).start()
 
     chips = (2 * x + y1, 2 * x1 + y, 2 * x1 + y1)
 
-    def spread_on(place, bsend, got):
+    def spread_on(place, bsend, got, bgot):
         for i in range(3):
             piece = place(chips[i], k)
-            recv(piece, got.at[chips[i], k])
-            remote(piece, piece, bsend.at[i + 1], got.at[chips[i], k], sib).start()
-
-    def spread_done(final, place, send, bsend, got):
-        recv(place(q, k), got.at[q, k])
-        for qq in (q,) + chips:
-            recv(place(qq, k1), got.at[qq, k1])
-        sent(final.at[x1], send.at[2])
-        sent(final.at[x1], send.at[1])
-        sent(final.at[x], send.at[0])
-        sent(final.at[x], bsend.at[0])
-        for i in range(3):
-            sent(place(chips[i], k), bsend.at[i + 1])
+            recv(piece, got.at[i + 1])
+            remote(piece, piece, bsend, bgot, sib).start()
 
     def in_place(qq, kk):
         return oin.at[:, qq, rows_at(64 * kk, 64), :]
@@ -1038,16 +1014,7 @@
     def proj_place(qq, kk):
         return oqkv.at[qq, rows_at(64 * kk, 64), :]
 
-    recv(REI.at[pl.ds(2 * z, 2)], zi_r.at[z])
-    recv(RCI, zic_r)
-    for xx in range(2):
-        total = ZI[2 * z + xx].astype(F32) + REI[2 * z + xx].astype(F32) + RCI[xx].astype(F32)
-        for j in range(4):
-            FI[xx, j] = total[:, 256 * j : 256 * j + 256].astype(BF)
-    spread(FI, in_place, fi_s, fib_s, fi_r)
-
-    for s in range(4):
-        recv(RO.at[s], o_r.at[s])
+    recv(RO, o_r)
 
     def home_out(r, carry):
         rows = rows_at(r * 32, 32)
@@ -1058,8 +1025,7 @@
         return carry
 
     lax.fori_loop(0, 4, home_out, 0)
-    for s in range(4):
-        recv(RN.at[s], n_r.at[s])
+    recv(RN, n_r)
 
     def home_inputs(r, total):
         rows = rows_at(r * 32, 32)
@@ -1083,17 +1049,24 @@
         ci = lax.rem(c + i, 4)
         for j, xj in enumerate((x, x1)):
             if i or j:
-                remote(SMALL, RSMALL.at[2 * c + x], sp_s.at[i, j], sp_r.at[2 * c + x], (ci, 2 * z + xj)).start()
-
-    for t in zs:
-        recv(RZQ.at[t, :, :, value_cols], zv_r.at[t])
-        recv(RZQ.at[t, :, :, other_cols], zq_r.at[t])
+                remote(SMALL, RSMALL.at[2 * c + x], sp_s, sp_r, (ci, 2 * z + xj)).start()
+
+    recv(in_rows(REI, z), zi_r.at[z])
+    recv(RCI, zic_r)
+    for xx in range(2):
+        total = ZI[2 * z + xx].astype(F32) + REI[2 * z + xx].astype(F32) + RCI[xx].astype(F32)
+        for j in range(4):
+            FI[xx, j] = total[:, 256 * j : 256 * j + 256].astype(BF)
+    spread(FI, in_place, fi_s, fib_s, fi_r, fib_r)
+
+    recv(RZQ.at[pl.ds(0, 3), :, :, value_cols], zv_r)
+    recv(RZQ.at[pl.ds(0, 3), :, :, other_cols], zq_r)
     for xx in range(2):
         total = ZQ[2 * z + xx].astype(F32)
         for t in zs:
             total = total + RZQ[t, xx].astype(F32)
         FQ[xx] = total.astype(BF)
-    spread(FQ, proj_place, fq_s, fqb_s, fq_r)
+    spread(FQ, proj_place, fq_s, fqb_s, fq_r, fqb_r)
 
     @pl.when(z == c)
     def _():
@@ -1101,96 +1074,85 @@
             recv(RZO.at[s], zo_r.at[s])
         FO[...] = (ZO[...].astype(F32) + RZO[0].astype(F32) + RZO[1].astype(F32)).astype(BF)
         pltpu.make_async_copy(FO, oout, fo_r).start()
-        remote(FO, oout, fo_s.at[1], fo_r, y_core).start()
-        remote(FO, oout, fo_s.at[0], fo_r, sib).start()
-
+        remote(FO, oout, fo_s, fo_r, y_core).start()
+        remote(FO, oout, fo_s, fo_r, sib).start()
+
+    recv(RSMALL.at[pl.ds(0, 7)], sp_r)
     plane_sum = SMALL[...]
     for i in range(4):
         ci = lax.rem(c + i, 4)
         for j, xj in enumerate((x, x1)):
             if i or j:
-                recv(RSMALL.at[2 * ci + xj], sp_r.at[2 * ci + xj])
                 plane_sum = plane_sum + RSMALL[2 * ci + xj]
     for t in range(4):
         for n in range(3):
             pair = plane_sum[n, 2 * t : 2 * t + 2, :]
             PSMALL[t, n : n + 1, :] = jnp.where(x == 0, pair[0:1], pair[1:2])
     for t in zs:
-        remote(PSMALL.at[t], RZSMALL.at[z], sz_s.at[t], sz_r.at[z], zdev(t)).start()
+        remote(PSMALL.at[t], RZSMALL.at[z], sz_s, sz_r, zdev(t)).start()
 
     y_rows = down_rows(2 * y1 + k)
-    recv(y_rows, fd_r.at[2 * y1 + k])
-    remote(y_rows, y_rows, fd_s.at[2], fd_r.at[2 * y1 + k], sib).start()
-    spread_on(in_place, fib_s, fi_r)
-    spread_on(proj_place, fqb_s, fq_r)
+    recv(y_rows, fd_r.at[1])
+    remote(y_rows, y_rows, fd_s, fd_r.at[2], sib).start()
+    spread_on(in_place, fib_s, fi_r, fib_r)
+    spread_on(proj_place, fqb_s, fq_r, fqb_r)
     recv(oout, fo_r)
     out_on = (y != z // 2) & (k == lax.rem(z, 2))
 
     @pl.when(out_on)
     def _():
-        remote(oout, oout, fo_s.at[0], fo_r, sib).start()
-
+        remote(oout, oout, fo_s, fo_r, sib).start()
+
+    recv(RZSMALL.at[pl.ds(0, 3)], sz_r)
     total = PSMALL[z]
     for t in zs:
-        recv(RZSMALL.at[t], sz_r.at[t])
         total = total + RZSMALL[t]
     small_ref[...] = total
 
-    recv(down_rows(c), fd_r.at[c])
-    recv(down_rows(2 * y + k1), fd_r.at[2 * y + k1])
-    recv(down_rows(2 * y1 + k1), fd_r.at[2 * y1 + k1])
-    spread_done(FI, in_place, fi_s, fib_s, fi_r)
-    spread_done(FQ, proj_place, fq_s, fqb_s, fq_r)
+    recv(down_rows(c), fd_r.at[0])
+    recv(odown.at[pl.ds(0, 256)], fd_r.at[2])
+    recv(in_place(q, k), fi_r.at[0])
+    recv(oin.at[:, :, rows_at(64 * k1, 64), :], fib_r)
+    recv(proj_place(q, k), fq_r.at[0])
+    recv(oqkv.at[:, rows_at(64 * k1, 64), :], fqb_r)
 
     sent(pack_in, gpx_s)
-    gather_sent(x_in.at[0], XB, xb_s)
-    gather_sent(cot_in.at[0], COT, co_s)
-    gather_sent(NTS, NTB, nt_s)
-    gather_sent(GALS, GAL, ga_s)
-    scatter_sent(SA, a_s)
-    scatter_sent(SG, g_s)
-    scatter_sent(SO, o_s)
-    scatter_sent(SN, n_s)
+    four_sent(XB, xb_s)
+    four_sent(COT, co_s)
+    four_sent(NTB, nt_s)
+    four_sent(GAL, ga_s)
+    four_sent(SA, a_s)
+    four_sent(SG, g_s)
+    four_sent(SO, o_s)
     sent(WQKV.at[half(f, k)], wx_s.at[0])
     sent(WIN.at[half(f, k)], wx_s.at[1])
-    for r, own in enumerate((f, f1)):
-        z_sent(WIN.at[half(own, k)], wiz_s.at[r])
-    z_sent(WDOWN.at[down_half], wdz_s)
-    sent(WQKV.at[half(f1, k)], wqb_s.at[f1])
-    sent(WIN.at[half(f1, k)], wib_s.at[f1])
-    for t in zs:
-        sent(GP.at[pl.ds(2 * z, 2)], gpz_s.at[t])
-        for xx in (x, x1):
-            sent(WQKV.at[half(2 * t + xx, k)], wqb_s.at[2 * t + xx])
-            sent(WIN.at[half(2 * t + xx, k)], wib_s.at[2 * t + xx])
-        sent(down_piece(t, k), wdb_s.at[t])
-        sent(ZQ.at[pl.ds(2 * t, 2), :, value_cols], zv_s.at[t])
-        sent(ZQ.at[pl.ds(2 * t, 2), :, other_cols], zq_s.at[t])
-        sent(PSMALL.at[t], sz_s.at[t])
-    sent(ZD.at[near], zd_s)
-    sent(ZI.at[pl.ds(2 * near, 2)], zi_s)
-    for n in range(2):
-        sent(ZD.at[others[n]], zde_s.at[n])
-        sent(ZI.at[pl.ds(2 * others[n], 2)], zie_s.at[n])
+    sent(WIN.at[pl.ds(0, 256)], wiz_s)
+    sent(WDOWN.at[pl.ds(0, 256)], wdz_s)
+    sent(WQKV.at[pl.ds(0, 448)], wqb_s)
+    sent(WIN.at[pl.ds(0, 448)], wib_s)
+    sent(WDOWN.at[pl.ds(0, 384)], wdb_s)
+    sent(GP.at[pl.ds(0, 6)], gpz_s)
+    sent(ZQ.at[pl.ds(0, 6), :, value_cols], zv_s)
+    sent(ZQ.at[pl.ds(0, 6), :, other_cols], zq_s)
+    sent(ZD.at[pl.ds(0, 3)], zd_s)
+    sent(PSMALL.at[pl.ds(0, 3)], sz_s)
+    sent(in_rows(ZI, near), zi_s)
+    sent(ZI.at[pl.ds(0, 4)], zie_s)
 
     @pl.when(middle)
     def _():
-        for n in range(2):
-            sent(down_piece(others[n], k), wdf_s.at[n])
-            for i, xx in enumerate((x, x1)):
-                g = of_row(others[n], xx)
-                sent(WQKV.at[half(g, k)], wqf_s.at[n, i])
-                sent(WIN.at[half(g, k)], wif_s.at[n, i])
+        sent(WDOWN.at[pl.ds(0, 256)], wdf_s)
+        sent(WQKV.at[pl.ds(0, 256)], wqf_s)
+        sent(WIN.at[pl.ds(0, 256)], wif_s)
 
     @pl.when(z == c)
     def _():
-        z_sent(out_piece, woz_s)
-        sent(FO, fo_s.at[0])
-        sent(FO, fo_s.at[1])
+        sent(WOUT, woz_s)
+        sent(odown.at[pl.ds(0, 256)], fo_s)
 
     @pl.when(out_on)
     def _():
-        sent(oout, fo_s.at[0])
+        sent(oout, fo_s)
 
     @pl.when(z != c)
     def _():
@@ -1199,19 +1161,19 @@
 
         @pl.when(middle & (z // 2 != c // 2))
         def _():
-            sent(out_piece, woz_s.at[0])
+            sent(out_piece, woz_s)
 
     sent(DD.at[k1], sib_s.at[0])
     sent(DI.at[k1], sib_s.at[1])
     sent(DQ.at[k1, :, :, value_cols], sib_s.at[2])
     sent(DO.at[k1], sib_s.at[3])
     sent(DQ.at[k1, :, :, other_cols], sib_s.at[4])
-    for i in range(3):
-        sent(FD, fd_s.at[i])
-    for i in range(4):
-        for j, xj in enumerate((x, x1)):
-            if i or j:
-                sent(SMALL, sp_s.at[i, j])
+    sent(odown.at[pl.ds(0, 384)], fd_s)
+    sent(oin.at[:, pl.ds(0, 3), pl.ds(0, 64), :], fi_s)
+    sent(oqkv.at[pl.ds(0, 3), pl.ds(0, 64), :], fq_s)
+    sent(oin.at[:, :, rows_at(64 * k, 64), :], fib_s)
+    sent(oqkv.at[:, rows_at(64 * k, 64), :], fqb_s)
+    sent(RSMALL.at[pl.ds(0, 7)], sp_s)
 
 
 def plane_shards(
@@ -1245,19 +1207,15 @@
         vm((8, 64, 768), BF), vm((128, 1024), BF), vm((8, 64, 1024), BF), vm((4, 128, 1024), BF),
         vm((8, 64, 768), BF), vm((128, 1024), BF), vm((8, 64, 1024), BF), vm((4, 128, 1024), BF),
         vm((4, 2, 64, 768), BF), vm((2, 128, 1024), BF), vm((8, 64, 1024), BF), vm((4, 128, 1024), BF),
-        vm((2, 64, 1024), BF), vm((128, 1024), BF),
+        vm((2, 64, 1024), BF),
         vm((2, 64, 768), BF), vm((128, 1024), BF), vm((2, 4, 64, 256), BF), vm((128, 1024), BF),
         vm((3, 8, 128), F32), vm((8, 3, 8, 128), F32), vm((4, 8, 128), F32), vm((4, 8, 128), F32),
-        dma((7,)), dma, dma, dma((4,)), dma((4,)),
-        dma((4, 2)), dma((4, 2)), dma((4, 2)), dma((4, 2)), dma((4, 2)), dma((4, 2)), dma((4, 2)), dma((4, 2)),
-        dma((4,)), dma((4,)), dma((4,)), dma((4,)), dma((4,)), dma((4,)), dma((4,)), dma((4,)),
-        dma((2,)), dma((2,)), dma((2, 2)), dma((2, 2)), dma((8,)), dma((8,)), dma((8,)),
-        dma((2, 2)), dma((2, 2)), dma((8,)), dma((8,)), dma((8,)),
-        dma((2,)), dma((2,)), dma((4,)), dma((4,)), dma((4,)), dma((2,)), dma, dma, dma,
-        dma((5,)), dma((5,)), dma((4,)), dma((4,)), dma((4,)), dma((4,)), dma, dma((2,)),
-        dma, dma((2,)), dma((4,)), dma, dma, dma((2,)), dma((4,)), dma,
-        dma((3,)), dma((4,)), dma((4, 2)), dma((2,)), dma, dma((3,)), dma((4,)), dma((4, 2)), dma((3,)), dma((4,)),
-        dma((4, 2)), dma((8,)), dma((4,)), dma((4,)),
+        dma((7,)), dma, dma, dma, dma, dma, dma((4,)), dma((2,)), dma, dma((4,)), dma((2,)), dma, dma((4,)), dma((2,)), dma, dma((4,)), dma((2,)),
+        dma, dma, dma, dma, dma, dma, dma, dma,
+        dma((2,)), dma((2,)), dma, dma, dma((8,)), dma, dma, dma, dma, dma((8,)), dma, dma,
+        dma, dma, dma((4,)), dma, dma, dma, dma, dma, dma,
+        dma((5,)), dma((5,)), dma, dma, dma, dma, dma, dma((2,)), dma, dma, dma((4,)), dma, dma, dma,
+        dma, dma, dma((4,)), dma, dma, dma, dma, dma, dma((4,)), dma, dma, dma((3,)), dma, dma, dma, dma,
     ]
     anywhere = pl.BlockSpec(memory_space=pl.ANY)
     in_vmem = pl.BlockSpec(memory_space=pltpu.VMEM)

time: 172 us -> 156 us (0.907)
  Pallas kernels: 165 us -> 150 us
    pallas_call x1, Pallas kernels: 160 us -> 146 us  [plane_shards(): pl.pallas_call(fused_layer, out_shape=(shape((1, TOKENS, WIDTH), BF), sha...]
where the time goes in v3:
time: 156 us; the launch traced here: 154 us
  Pallas kernels  150 us (96%)
  other arithmetic  1.99 us (1%)
    pallas_call x1, Pallas kernels, plane_shards(): pl.pallas_call(fused_layer, out_shape=(shape((1, TOKENS, WIDTH), BF), sha...  146 us
    pallas_call x1, Pallas kernels, finish(): pl.pallas_call(finish_kernel, out_shape=(shape(output.shape, BF), shape(g...  4.68 us

profile of v3, /device:TPU:0, one launch (start us, length us, event | category | flops | bytes accessed | tf_op | source)
XLA Modules:
  0.0 154.3 jit_solution(10961391529379687372)
XLA Ops:
  0.6 0.7 bitcast_convert_fusion.2
  1.3 0.1 pad.14.clone
  1.4 0.7 bitcast_convert_fusion
  2.1 0.7 maximum_maximum_fusion.pack_in
  2.7 1.3 pad.10
  4.0 145.6 %shard_map.203 = (bf16[1,128,1024]{2,1,0:T(8,128)(2,1)}, bf16[1,128,1024]{2,1,0:T(8,128)(2,1)}, bf16[4,128,768]{2,1,0:T(8,128)(2,1)}, bf16[128,1024]{1,0:T(8,128...) custom-call(bf16[1,128,1024]{2,1,0:T(8,128)(2,1)} %x_in.1, ...), custom_call_target="tpu_custom_call" | custom-call | flops 11000000512 | bytes 16777216 | tf_op jit(solution)/shard_map/pallas_call | solution.py:1223
  149.6 4.7 %shard_map.204 = (bf16[1,128,1024]{2,1,0:T(8,128)(2,1)}, bf16[1,128,1024]{2,1,0:T(8,128)(2,1)}, f32[128,1024]{1,0:T(8,128)}, f32[128,1024]{1,0:T(8,128)}, f32[12...) custom-call(bf16[1,128,1024]{2,1,0:T(8,128)(2,1)} %get-tuple-element, ...), custom_call_target="tpu_custom_call" | custom-call | bytes 10485760 | tf_op jit(solution)/shard_map/pallas_call | solution.py:1308
  (1 shorter events, 0.0 us)

commit v4 on v3

--- a/solution.py
+++ b/solution.py
@@ -307,18 +307,19 @@
 
 
 def fused_layer(
-    x_in, cot_in, wq_in, wk_in, wv_in, wo_in, wi_in, wd_in, pack_in, bucket_in,
+    x_in, cot_in, wq_in, wk_in, wv_in, wo_in, wi_in, wd_in, attn_in, mlp_in, table_in, bucket_in,
     out_ref, gin_ref, oqkv, oout, oin, odown, small_ref,
-    XO, CO, GP, XB, COT, N1, NTB, GAL, WQKV, WOUT, WIN, WDOWN,
+    XO, CO, PACK, BUCKET, STAGE, ACROSS, GP, XB, COT, N1, NTB, GAL, WQKV, WOUT, WIN, WDOWN,
     QKV, PROB, PLOW, BIAS, AT, ACT, SLOPE, GPRE, GATT, DQKV, DS, BACC,
     SA, SG, SO, SN, RA, RG, RO, RN, HID, GH, NTS, GALS,
-    DQ, DO, DI, DD, SIBQ, SIBO, SIBI, SIBD, ZQ, ZO, ZI, ZD, RZQ, RZO, REI, RZD, RCI, FQ, FO, FI, FD,
+    DQ, DO, DI, DD, SIBQ, SIBO, SIBI, SIBD, ZQ, ZO, ZI, ZD, REQ, REO, REI, RED, RCQ, RCO, RCI, RCD, FQ, FO, FI, FD,
     SMALL, RSMALL, PSMALL, RZSMALL,
-    loc, gpx_s, gpx_r, gpz_s, gpz_r, xb_s, xb_r, xb_p, co_s, co_r, co_p, nt_s, nt_r, nt_p, ga_s, ga_r, ga_p,
+    loc, gp_s, gp_r, xb_s, xb_r, xb_p, co_s, co_r, co_p, nt_s, nt_r, nt_p, ga_s, ga_r, ga_p,
     a_s, a_r, g_s, g_r, o_s, o_r, n_s, n_r,
     wx_s, wx_r, wqz_s, wqf_s, wqz_r, wqb_s, wqb_r, wiz_s, wif_s, wiz_r, wib_s, wib_r,
     wdz_s, wdf_s, wdz_r, wdb_s, wdb_r, woz_s, woz_r, wob_s, wob_r,
-    sib_s, sib_r, zq_s, zq_r, zv_s, zv_r, zo_s, zo_r, zi_s, zie_s, zi_r, zic_r, zd_s, zd_r,
+    sib_s, sib_r, sibd_r, zq_s, zqe_s, zq_r, zqc_r, zv_s, zve_s, zv_r, zvc_r, zo_s, zoe_s, zo_r, zoc_r,
+    zi_s, zie_s, zi_r, zic_r, zd_s, zde_s, zd_r, zdc_r,
     fq_s, fqb_s, fq_r, fqb_r, fo_s, fo_r, fi_s, fib_s, fi_r, fib_r, fd_s, fd_r, sp_s, sp_r, sz_s, sz_r,
 ):
     c = lax.axis_index("ctx")
@@ -419,9 +420,47 @@
     def half(fb, kk):
         return rows_at(fb * 128 + kk * 64, 64)
 
+    def z_far(piece, send, got, src=None):
+        remote(piece if src is None else src, piece, send, got, zdev(far)).start()
+
+    def z_near(piece, send, got, src=None):
+        remote(piece if src is None else src, piece, send, got, zdev(near)).start()
+
     def z_send(piece, send, got):
-        remote(piece, piece, send, got, zdev(far)).start()
-        remote(piece, piece, send, got, zdev(near)).start()
+        z_far(piece, send, got)
+        z_near(piece, send, got)
+
+    def down_of(ref, t):
+        return ref.at[t]
+
+    def in_of(ref, t):
+        return ref.at[pl.ds(2 * t, 2)]
+
+    def value_of(ref, t):
+        return ref.at[pl.ds(2 * t, 2), :, value_cols]
+
+    def other_of(ref, t):
+        return ref.at[pl.ds(2 * t, 2), :, other_cols]
+
+    value_cols, other_cols = pl.ds(512, 256), pl.ds(0, 512)
+
+    def reduce_others(of, terms, got, send, sem):
+        @pl.when(at_end)
+        def _():
+            for t in others:
+                remote(of(terms, t), of(got, t), send, sem.at[t], zdev(near)).start()
+
+    def reduce_near(of, terms, got, send, sem):
+        remote(of(terms, near), of(got, near), send, sem.at[near], zdev(near)).start()
+
+    def reduce_middle(of, terms, got, final, send, sem, final_sem):
+        @pl.when(middle)
+        def _():
+            for t in others:
+                recv(of(got, t), sem.at[t])
+                mine = of(terms, t)
+                mine[...] = (mine[...].astype(F32) + of(got, t)[...].astype(F32)).astype(BF)
+                remote(mine, final, send, final_sem, zdev(t)).start()
 
     def take(piece, got, bsend, bgot):
         recv(piece, got)
@@ -435,14 +474,9 @@
 
     own_x = pltpu.make_async_copy(x_in.at[0], XO, loc.at[0])
     own_c = pltpu.make_async_copy(cot_in.at[0], CO, loc.at[1])
-    own_pack = pltpu.make_async_copy(pack_in, GP.at[f], loc.at[2])
-    proj = (wq_in, wk_in, wv_in)
     myrows = pl.ds(pl.multiple_of(128 * f, 128), 128)
-    for w in range(3):
-        for j in range(2):
-            src = proj[w].at[:, pl.ds(pl.multiple_of(128 * (2 * (2 * y + j) + x), 128), 128)]
-            pltpu.make_async_copy(src, WQKV.at[myrows, pl.ds(256 * w + 128 * j, 128)], loc.at[3]).start()
-    own_pack.start()
+    for w, proj in enumerate((wq_in, wk_in, wv_in)):
+        pltpu.make_async_copy(proj, STAGE.at[w], loc.at[3]).start()
     for j in range(4):
         src = wi_in.at[:, pl.ds(pl.multiple_of(512 * (2 * j + x) + 256 * y, 256), 256)]
         pltpu.make_async_copy(src, WIN.at[myrows, pl.ds(256 * j, 256)], loc.at[4]).start()
@@ -450,52 +484,73 @@
         wd_in.at[rows_at(256 * y, 256)], WDOWN.at[rows_at(256 * z, 256)], loc.at[5]
     ).start()
 
-    @pl.when(z // 2 == y)
-    def _():
-        pltpu.make_async_copy(wo_in, WOUT.at[rows_at(128 * lax.rem(z, 2), 128)], loc.at[6]).start()
-
+    pltpu.make_async_copy(wo_in.at[rows_at(64 * y, 64)], WOUT.at[rows_at(64 * z, 64)], loc.at[6]).start()
     own_x.start()
     own_c.start()
 
     barrier = pltpu.get_barrier_semaphore()
-    for device in plane + [zdev(t) for t in zs]:
+    across = [(c, 2 * t + x1) for t in zs]
+    for device in plane + [zdev(t) for t in zs] + across:
         pl.semaphore_signal(barrier, inc=1, device_id=device, device_id_type=MESH_ID)
-    pl.semaphore_wait(barrier, 10)
-
-
-    remote(pack_in, GP.at[f], gpx_s, gpx_r, xdev).start()
-    for w in range(3):
-        for j in range(2):
-            src = proj[w].at[rows_at(64 * k, 64), pl.ds(pl.multiple_of(128 * (2 * (2 * y + j) + x1), 128), 128)]
-            remote(src, WQKV.at[half(f, k), pl.ds(256 * w + 128 * j, 128)], wx_s.at[0], wx_r.at[0], xdev).start()
-    pltpu.make_async_copy(WQKV.at[myrows], WQKV.at[myrows], loc.at[3]).wait()
+
+
+    PACK[...] = jnp.zeros((8, 128), F32)
+    PACK[0:1, :] = attn_in[...].astype(F32)
+    PACK[1:2, :] = mlp_in[...].astype(F32)
+    PACK[2:3, 0:64] = table_in[...].astype(F32)
+    BUCKET[...] = jnp.full((1, WIDTH), -1, jnp.int32)
+    BUCKET[0:1, 0 : WIDTH - 1] = bucket_in[...]
+    GP[f] = PACK[...]
+
+    pltpu.make_async_copy(STAGE, STAGE, loc.at[3]).wait()
+
+    def pack_heads(dst, dst_rows, src_rows, xx, count):
+        low = lax.broadcasted_iota(jnp.int32, (count, 128), 1) < 64
+        for w in range(3):
+            for j in range(2):
+                first, second = [
+                    STAGE[w, src_rows, pl.ds(pl.multiple_of(128 * (4 * j + 2 * n + xx), 128), 128)].astype(F32)
+                    for n in range(2)
+                ]
+                left = jnp.where(y == 0, first, pltpu.roll(first, 64, 1))
+                right = jnp.where(y == 0, pltpu.roll(second, 64, 1), second)
+                dst[dst_rows, 256 * w + 128 * j : 256 * w + 128 * j + 128] = jnp.where(low, left, right).astype(BF)
+
+    pack_heads(ACROSS, slice(0, 64), rows_at(64 * k, 64), x1, 64)
+    pack_heads(WQKV, myrows, slice(0, 128), x, 128)
+    pl.semaphore_wait(barrier, 13)
+    for device in [xdev] + [zdev(t) for t in zs] + across:
+        remote(PACK, GP.at[f], gp_s, gp_r, device).start()
+    remote(ACROSS, WQKV.at[half(f, k)], wx_s.at[0], wx_r.at[0], xdev).start()
     z_send(WQKV.at[half(f, k)], wqz_s, wqz_r.at[f])
     gather_send(x_in.at[0], XB, xb_s, xb_r, xb_p)
     for j in range(4):
         src = wi_in.at[rows_at(64 * k, 64), pl.ds(pl.multiple_of(512 * (2 * j + x1) + 256 * y, 256), 256)]
         remote(src, WIN.at[half(f, k), pl.ds(256 * j, 256)], wx_s.at[1], wx_r.at[1], xdev).start()
-    out_piece = WOUT.at[rows_at(128 * k, 128)]
-    out_other = WOUT.at[rows_at(128 * k1, 128)]
-
-    own_pack.wait()
-    recv(GP.at[f1], gpx_r)
-    for t in zs:
-        remote(GP.at[pl.ds(2 * z, 2)], GP.at[pl.ds(2 * z, 2)], gpz_s, gpz_r, zdev(t)).start()
+
     recv(WQKV.at[half(f1, k)], wx_r.at[0])
     z_send(WQKV.at[half(f1, k)], wqz_s, wqz_r.at[f1])
     remote(WQKV.at[half(f1, k)], WQKV.at[half(f1, k)], wqb_s, wqb_r, sib).start()
-
-    @pl.when(z == c)
-    def _():
-        remote(wo_in, out_piece, woz_s, woz_r, zdev(far)).start()
-        remote(wo_in, out_piece, woz_s, woz_r, zdev(near)).start()
-
-    gather_pass(XB, xb_s, xb_r, xb_p)
-    gather_send(cot_in.at[0], COT, co_s, co_r, co_p)
+    down_half = rows_at(256 * z + 128 * k, 128)
+    pltpu.make_async_copy(WIN.at[myrows], WIN.at[myrows], loc.at[4]).wait()
+
+    def out_piece(t):
+        return WOUT.at[rows_at(64 * t + 32 * k, 32)]
+
+    out_own = wo_in.at[rows_at(64 * y + 32 * k, 32)]
+    z_far(out_piece(z), woz_s, woz_r.at[z], out_own)
+
+    @pl.when(at_end)
+    def _():
+        z_near(out_piece(z), woz_s, woz_r.at[z], out_own)
+
+    z_far(WIN.at[half(f, k)], wiz_s, wiz_r.at[f])
+
+    @pl.when(at_end)
+    def _():
+        z_near(WIN.at[half(f, k)], wiz_s, wiz_r.at[f])
 
     def take_proj(xx):
-        g = of_row(near, xx)
-        take(WQKV.at[half(g, k)], wqz_r.at[g], wqb_s, wqb_r)
         for n in range(2):
             h = of_row(others[n], xx)
             piece = WQKV.at[half(h, k)]
@@ -507,24 +562,39 @@
 
             remote(piece, piece, wqb_s, wqb_r, sib).start()
 
+    def take_near(xx):
+        g = of_row(near, xx)
+        take(WQKV.at[half(g, k)], wqz_r.at[g], wqb_s, wqb_r)
+
     @pl.when(middle)
     def _():
         take_proj(x)
 
-    recv(GP.at[pl.ds(0, 6)], gpz_r)
+    gather_pass(XB, xb_s, xb_r, xb_p)
+    gather_send(cot_in.at[0], COT, co_s, co_r, co_p)
+    take_near(x)
+
+    @pl.when(middle)
+    def _():
+        take_proj(x1)
+        take_near(x1)
+
+        z_near(out_piece(z), woz_s, woz_r.at[z], out_own)
+
+    recv(GP.at[pl.ds(0, 7)], gp_r)
 
     def row_of(index):
         return jnp.concatenate([GP[g, index : index + 1, :] for g in range(8)], axis=1)
 
     lane = lax.broadcasted_iota(jnp.int32, (8, 128), 1)
     head_row = lax.broadcasted_iota(jnp.int32, (8, 128), 0)
-    head_of = 8 * y + 4 * lax.div(head_row, 2) + 2 * x + lax.rem(head_row, 2)
+    head_of = 4 * head_row + 2 * x + y
     head_mask = (lax.rem(lane, 16) == head_of) & (head_row < 4)
 
     def bucket_hot(g):
         index = lax.broadcasted_iota(jnp.int32, (128, WIDTH), 0)
         wanted = jnp.where(index < 64, 4 * g + lax.div(index, 16), -1)
-        return (bucket_in[0:1, :] == wanted)
+        return (BUCKET[0:1, :] == wanted)
 
     def add_bias(g, total):
         table = jnp.where(head_mask, jnp.broadcast_to(GP[g, 2:3, :], (8, 128)), 0.0).astype(BF)
@@ -553,32 +623,30 @@
 
     lax.fori_loop(0, 4, norm_block, 0)
 
-    sent(WQKV.at[pl.ds(0, 256)], wqz_s)
-    pltpu.make_async_copy(WIN.at[myrows], WIN.at[myrows], loc.at[4]).wait()
-    z_send(WIN.at[half(f, k)], wiz_s, wiz_r.at[f])
+    @pl.when(middle)
+    def _():
+        for t in others:
+            recv(out_piece(t), woz_r.at[t])
+            pass_on(out_piece(t), woz_s, woz_r.at[t])
+            remote(out_piece(t), out_piece(t), wob_s, wob_r, sib).start()
+
+        z_near(WIN.at[half(f, k)], wiz_s, wiz_r.at[f])
+
     recv(WIN.at[half(f1, k)], wx_r.at[1])
-    z_send(WIN.at[half(f1, k)], wiz_s, wiz_r.at[f1])
+    z_far(WIN.at[half(f1, k)], wiz_s, wiz_r.at[f1])
     remote(WIN.at[half(f1, k)], WIN.at[half(f1, k)], wib_s, wib_r, sib).start()
+    pltpu.make_async_copy(WDOWN.at[rows_at(256 * z, 256)], WDOWN.at[rows_at(256 * z, 256)], loc.at[5]).wait()
+    z_far(WDOWN.at[down_half], wdz_s, wdz_r.at[z])
+
+    z_near(WIN.at[half(f1, k)], wiz_s, wiz_r.at[f1])
 
     @pl.when(at_end)
     def _():
+        z_near(WDOWN.at[down_half], wdz_s, wdz_r.at[z])
+        take_near(x1)
         take_proj(x)
-
-    take_proj(x1)
-
-    @pl.when(z != c)
-    def _():
-        recv(out_piece, woz_r)
-
-        @pl.when(middle & (z // 2 != c // 2))
-        def _():
-            pass_on(out_piece, woz_s, woz_r)
-
-        remote(out_piece, out_piece, wob_s, wob_r, sib).start()
-
-    down_half = rows_at(256 * z + 128 * k, 128)
-    pltpu.make_async_copy(WDOWN.at[rows_at(256 * z, 256)], WDOWN.at[rows_at(256 * z, 256)], loc.at[5]).wait()
-    z_send(WDOWN.at[down_half], wdz_s, wdz_r.at[z])
+        take_proj(x1)
+
     recv(WQKV.at[pl.ds(0, 448)], wqb_r)
 
     def project(n, carry):
@@ -589,15 +657,11 @@
     lax.fori_loop(0, 3, project, 0)
 
 
-    @pl.when(z // 2 == y)
-    def _():
-        pltpu.make_async_copy(wo_in, out_piece, loc.at[6]).wait()
-
-    @pl.when(z != 2 * y + k1)
-    def _():
-        recv(out_other, wob_r)
-
     gather_pass(COT, co_s, co_r, co_p)
+
+    @pl.when(middle)
+    def _():
+        z_near(WDOWN.at[down_half], wdz_s, wdz_r.at[z])
 
     low_lanes = lax.broadcasted_iota(jnp.int32, (TOKENS, 128), 1) < 64
 
@@ -623,6 +687,19 @@
                 PLOW[h, rows, :] = low
                 outs.append(dot_nn(low, QKV[:, 512 + 128 * j : 640 + 128 * j]))
             AT[rows, 128 * j : 128 * j + 128] = jnp.where(low_lanes, outs[0], outs[1]).astype(BF)
+
+        @pl.when(i == 0)
+        def _():
+            take(out_piece(near), woz_r.at[near], wob_s, wob_r)
+
+            @pl.when(at_end)
+            def _():
+                for t in others:
+                    take(out_piece(t), woz_r.at[t], wob_s, wob_r)
+
+            pltpu.make_async_copy(WOUT.at[rows_at(64 * z, 64)], WOUT.at[rows_at(64 * z, 64)], loc.at[6]).wait()
+            recv(WOUT.at[pl.ds(0, 96)], wob_r)
+
         SA[rows, :] = dot_nn(AT[rows, :], WOUT[...]).astype(BF)
         scatter_send(SA, RA, a_s, a_r, b)
         return carry
@@ -705,14 +782,34 @@
     for b in range(4):
         gather_wait(COT, co_r, b)
 
-    def grad_down(m, carry):
+    order = (other, other + 1, near, z)
+
+    def grad_down(i, carry):
+        m = jnp.where(i < 2, other + i, jnp.where(i == 2, near, z))
         tile = dot_tn(ACT[:, rows_at(256 * m, 256)], COT[...]).astype(BF)
         DD[0, m] = tile[0:128]
         DD[1, m] = tile[128:256]
+        remote(DD.at[k1, m], SIBD.at[m], sib_s.at[0], sibd_r.at[i], sib).start()
         return carry
 
     lax.fori_loop(0, 4, grad_down, 0)
-    remote(DD.at[k1], SIBD, sib_s.at[0], sib_r.at[0], sib).start()
+
+    def join_down(i, carry):
+        m = jnp.where(i < 2, other + i, jnp.where(i == 2, near, z))
+        recv(SIBD.at[m], sibd_r.at[i])
+        ZD[m] = (DD[k, m].astype(F32) + SIBD[m].astype(F32)).astype(BF)
+
+        @pl.when(at_end & (i < 2))
+        def _():
+            remote(ZD.at[m], RED.at[m], zde_s, zd_r.at[m], zdev(near)).start()
+
+        @pl.when(middle & (i == 2))
+        def _():
+            remote(ZD.at[m], RED.at[m], zd_s, zd_r.at[m], zdev(near)).start()
+
+        return carry
+
+    lax.fori_loop(0, 4, join_down, 0)
 
     @pl.when(at_end)
     def _():
@@ -720,16 +817,6 @@
             take(down_piece(t, k), wdz_r.at[t], wdb_s, wdb_r)
 
     recv(WDOWN.at[pl.ds(0, 384)], wdb_r)
-
-    recv(SIBD, sib_r.at[0])
-
-    def join_down(m, carry):
-        ZD[m] = (DD[k, m].astype(F32) + SIBD[m].astype(F32)).astype(BF)
-        return carry
-
-    lax.fori_loop(0, 4, join_down, 0)
-    for t in zs:
-        remote(ZD.at[t], RZD.at[z], zd_s, zd_r, zdev(t)).start()
 
     def back_feed(i, carry):
         yy = lax.rem(y1 + i, 2)
@@ -778,14 +865,7 @@
         return carry
 
     lax.fori_loop(0, 8, join_in, 0)
-    def in_rows(ref, t):
-        return ref.at[pl.ds(2 * t, 2)]
-
-    @pl.when(at_end)
-    def _():
-        for n in range(2):
-            t = others[n]
-            remote(in_rows(ZI, t), in_rows(REI, t), zie_s, zi_r.at[t], zdev(near)).start()
+    reduce_others(in_of, ZI, REI, zie_s, zi_r)
 
     recv(RG, g_r)
 
@@ -805,6 +885,7 @@
 
     mlp_gain_grad = lax.fori_loop(0, 4, home_back, jnp.zeros((8, WIDTH), F32))
     gather_send(GALS, GAL, ga_s, ga_r, ga_p)
+    reduce_middle(down_of, ZD, RED, RCD, zde_s, zd_r, zdc_r)
 
     mlp_gain_grad = jnp.sum(mlp_gain_grad, axis=0, keepdims=True)
     for g in range(8):
@@ -855,50 +936,35 @@
 
         lax.fori_loop(0, 8, step, 0)
 
-    value_cols, other_cols = pl.ds(512, 256), pl.ds(0, 512)
     grad_proj(512, 256)
     remote(DQ.at[k1, :, :, value_cols], SIBQ.at[:, :, value_cols], sib_s.at[2], sib_r.at[2], sib).start()
 
     def grad_out_rows(m, carry):
-        DO[m] = dot_tn(AT[:, rows_at(128 * m, 128)], GAL[...]).astype(BF)
+        tile = dot_tn(AT[:, rows_at(128 * m, 128)], GAL[...]).astype(BF)
+        for n in range(2):
+            for kk in range(2):
+                DO[kk, 2 * m + n] = tile[64 * n + 32 * kk : 64 * n + 32 * kk + 32]
         return carry
 
     lax.fori_loop(0, 2, grad_out_rows, 0)
     remote(DO.at[k1], SIBO, sib_s.at[3], sib_r.at[3], sib).start()
 
-    def z_scatter(cols, send, got):
-        for t in zs:
-            remote(
-                ZQ.at[pl.ds(2 * t, 2), :, cols], RZQ.at[z, :, :, cols], send, got, zdev(t)
-            ).start()
-
     recv(SIBQ.at[:, :, value_cols], sib_r.at[2])
     join_proj(512, 256)
-    z_scatter(value_cols, zv_s, zv_r)
+    reduce_others(value_of, ZQ, REQ, zve_s, zv_r)
 
     recv(SIBO, sib_r.at[3])
     ZO[...] = (DO[k].astype(F32) + SIBO[...].astype(F32)).astype(BF)
 
-    out_near = z // 2 == c // 2
-
-    @pl.when((z != c) & out_near)
-    def _():
-        remote(ZO, RZO.at[0], zo_s, zo_r.at[0], zdev(c)).start()
-
-    @pl.when(jnp.logical_not(out_near) & at_end)
-    def _():
-        remote(ZO, RZO.at[0], zo_s, zo_r.at[0], zdev(near)).start()
-
-    remote(in_rows(ZI, near), in_rows(REI, near), zi_s, zi_r.at[near], zdev(near)).start()
+    reduce_others(down_of, ZO, REO, zoe_s, zo_r)
 
     @pl.when(middle)
     def _():
-        for n in range(2):
-            t = others[n]
-            recv(in_rows(REI, t), zi_r.at[t])
-            for xx in range(2):
-                ZI[2 * t + xx] = (ZI[2 * t + xx].astype(F32) + REI[2 * t + xx].astype(F32)).astype(BF)
-            remote(in_rows(ZI, t), RCI, zie_s, zic_r, zdev(t)).start()
+        reduce_near(in_of, ZI, REI, zi_s, zi_r)
+        reduce_near(value_of, ZQ, REQ, zv_s, zv_r)
+        reduce_near(down_of, ZO, REO, zo_s, zo_r)
+
+    reduce_middle(in_of, ZI, REI, RCI, zie_s, zi_r, zic_r)
 
     def attend_back(i, carry):
         rows = rows_at(i * TOKENS, TOKENS)
@@ -932,6 +998,12 @@
 
     lax.fori_loop(0, 2, grad_keys, 0)
 
+    @pl.when(at_end)
+    def _():
+        reduce_near(down_of, ZD, RED, zd_s, zd_r)
+
+    reduce_middle(value_of, ZQ, REQ, RCQ.at[:, :, value_cols], zve_s, zv_r, zvc_r)
+    reduce_middle(down_of, ZO, REO, RCO, zoe_s, zo_r, zoc_r)
     grad_proj(0, 512)
     remote(DQ.at[k1, :, :, other_cols], SIBQ.at[:, :, other_cols], sib_s.at[4], sib_r.at[4], sib).start()
     def back_project(i, carry):
@@ -946,14 +1018,15 @@
 
     recv(SIBQ.at[:, :, other_cols], sib_r.at[4])
     join_proj(0, 512)
-    z_scatter(other_cols, zq_s, zq_r)
-
-    @pl.when(jnp.logical_not(out_near) & middle)
-    def _():
-        recv(RZO.at[0], zo_r.at[0])
-        ZO[...] = (ZO[...].astype(F32) + RZO[0].astype(F32)).astype(BF)
-        remote(ZO, RZO.at[1], zo_s, zo_r.at[1], zdev(c)).start()
-
+    reduce_others(other_of, ZQ, REQ, zqe_s, zq_r)
+
+    @pl.when(at_end)
+    def _():
+        reduce_near(in_of, ZI, REI, zi_s, zi_r)
+        reduce_near(value_of, ZQ, REQ, zv_s, zv_r)
+        reduce_near(down_of, ZO, REO, zo_s, zo_r)
+
+    reduce_near(other_of, ZQ, REQ, zq_s, zq_r)
 
     head_sums = []
     for h in range(4):
@@ -978,17 +1051,15 @@
 
     lax.fori_loop(0, 8, bucket_sums, 0)
 
-    recv(RZD.at[pl.ds(0, 3)], zd_r)
-    total = ZD[z].astype(F32)
-    for t in zs:
-        total = total + RZD[t].astype(F32)
-    FD[...] = total.astype(BF)
+    reduce_middle(other_of, ZQ, REQ, RCQ.at[:, :, other_cols], zqe_s, zq_r, zqc_r)
+    recv(RED.at[z], zd_r.at[z])
+    recv(RCD, zdc_r)
+    FD[...] = (ZD[z].astype(F32) + RED[z].astype(F32) + RCD[...].astype(F32)).astype(BF)
 
     def down_rows(cc):
         return odown.at[rows_at(128 * cc, 128)]
 
     y_core = (2 * y1 + k, f)
-    four_sent(SN, n_s)
     remote(FD, down_rows(c), fd_s, fd_r.at[1], y_core).start()
     remote(FD, down_rows(c), fd_s, fd_r.at[2], sib).start()
     pltpu.make_async_copy(FD, down_rows(c), fd_r.at[0]).start()
@@ -1051,7 +1122,7 @@
             if i or j:
                 remote(SMALL, RSMALL.at[2 * c + x], sp_s, sp_r, (ci, 2 * z + xj)).start()
 
-    recv(in_rows(REI, z), zi_r.at[z])
+    recv(in_of(REI, z), zi_r.at[z])
     recv(RCI, zic_r)
     for xx in range(2):
         total = ZI[2 * z + xx].astype(F32) + REI[2 * z + xx].astype(F32) + RCI[xx].astype(F32)
@@ -1059,24 +1130,30 @@
             FI[xx, j] = total[:, 256 * j : 256 * j + 256].astype(BF)
     spread(FI, in_place, fi_s, fib_s, fi_r, fib_r)
 
-    recv(RZQ.at[pl.ds(0, 3), :, :, value_cols], zv_r)
-    recv(RZQ.at[pl.ds(0, 3), :, :, other_cols], zq_r)
+    recv(value_of(REQ, z), zv_r.at[z])
+    recv(other_of(REQ, z), zq_r.at[z])
+    recv(RCQ.at[:, :, value_cols], zvc_r)
+    recv(RCQ.at[:, :, other_cols], zqc_r)
     for xx in range(2):
-        total = ZQ[2 * z + xx].astype(F32)
-        for t in zs:
-            total = total + RZQ[t, xx].astype(F32)
+        total = ZQ[2 * z + xx].astype(F32) + REQ[2 * z + xx].astype(F32) + RCQ[xx].astype(F32)
         FQ[xx] = total.astype(BF)
     spread(FQ, proj_place, fq_s, fqb_s, fq_r, fqb_r)
 
-    @pl.when(z == c)
-    def _():
-        for s in range(2):
-            recv(RZO.at[s], zo_r.at[s])
-        FO[...] = (ZO[...].astype(F32) + RZO[0].astype(F32) + RZO[1].astype(F32)).astype(BF)
-        pltpu.make_async_copy(FO, oout, fo_r).start()
-        remote(FO, oout, fo_s, fo_r, y_core).start()
-        remote(FO, oout, fo_s, fo_r, sib).start()
-
+    recv(REO.at[z], zo_r.at[z])
+    recv(RCO, zoc_r)
+    FO[...] = (ZO[z].astype(F32) + REO[z].astype(F32) + RCO[...].astype(F32)).astype(BF)
+
+    def out_rows(cc):
+        return oout.at[rows_at(32 * cc, 32)]
+
+    remote(FO, out_rows(c), fo_s, fo_r.at[1], y_core).start()
+    remote(FO, out_rows(c), fo_s, fo_r.at[2], sib).start()
+    pltpu.make_async_copy(FO, out_rows(c), fo_r.at[0]).start()
+
+    y_rows = down_rows(2 * y1 + k)
+    recv(y_rows, fd_r.at[1])
+    remote(y_rows, y_rows, fd_s, fd_r.at[2], sib).start()
+    spread_on(in_place, fib_s, fi_r, fib_r)
     recv(RSMALL.at[pl.ds(0, 7)], sp_r)
     plane_sum = SMALL[...]
     for i in range(4):
@@ -1091,18 +1168,10 @@
     for t in zs:
         remote(PSMALL.at[t], RZSMALL.at[z], sz_s, sz_r, zdev(t)).start()
 
-    y_rows = down_rows(2 * y1 + k)
-    recv(y_rows, fd_r.at[1])
-    remote(y_rows, y_rows, fd_s, fd_r.at[2], sib).start()
-    spread_on(in_place, fib_s, fi_r, fib_r)
     spread_on(proj_place, fqb_s, fq_r, fqb_r)
-    recv(oout, fo_r)
-    out_on = (y != z // 2) & (k == lax.rem(z, 2))
-
-    @pl.when(out_on)
-    def _():
-        remote(oout, oout, fo_s, fo_r, sib).start()
-
+    y_out = out_rows(2 * y1 + k)
+    recv(y_out, fo_r.at[1])
+    remote(y_out, y_out, fo_s, fo_r.at[2], sib).start()
     recv(RZSMALL.at[pl.ds(0, 3)], sz_r)
     total = PSMALL[z]
     for t in zs:
@@ -1111,12 +1180,14 @@
 
     recv(down_rows(c), fd_r.at[0])
     recv(odown.at[pl.ds(0, 256)], fd_r.at[2])
+    recv(out_rows(c), fo_r.at[0])
+    recv(oout.at[pl.ds(0, 64)], fo_r.at[2])
     recv(in_place(q, k), fi_r.at[0])
     recv(oin.at[:, :, rows_at(64 * k1, 64), :], fib_r)
     recv(proj_place(q, k), fq_r.at[0])
     recv(oqkv.at[:, rows_at(64 * k1, 64), :], fqb_r)
 
-    sent(pack_in, gpx_s)
+    sent(GP.at[pl.ds(0, 7)], gp_s)
     four_sent(XB, xb_s)
     four_sent(COT, co_s)
     four_sent(NTB, nt_s)
@@ -1124,6 +1195,8 @@
     four_sent(SA, a_s)
     four_sent(SG, g_s)
     four_sent(SO, o_s)
+    four_sent(SN, n_s)
+    sent(WQKV.at[pl.ds(0, 256)], wqz_s)
     sent(WQKV.at[half(f, k)], wx_s.at[0])
     sent(WIN.at[half(f, k)], wx_s.at[1])
     sent(WIN.at[pl.ds(0, 256)], wiz_s)
@@ -1131,12 +1204,14 @@
     sent(WQKV.at[pl.ds(0, 448)], wqb_s)
     sent(WIN.at[pl.ds(0, 448)], wib_s)
     sent(WDOWN.at[pl.ds(0, 384)], wdb_s)
-    sent(GP.at[pl.ds(0, 6)], gpz_s)
-    sent(ZQ.at[pl.ds(0, 6), :, value_cols], zv_s)
-    sent(ZQ.at[pl.ds(0, 6), :, other_cols], zq_s)
-    sent(ZD.at[pl.ds(0, 3)], zd_s)
+    sent(value_of(ZQ, near), zv_s)
+    sent(other_of(ZQ, near), zq_s)
+    sent(ZQ.at[pl.ds(0, 4), :, value_cols], zve_s)
+    sent(ZQ.at[pl.ds(0, 4), :, other_cols], zqe_s)
+    sent(down_of(ZD, near), zd_s)
+    sent(ZD.at[pl.ds(0, 2)], zde_s)
     sent(PSMALL.at[pl.ds(0, 3)], sz_s)
-    sent(in_rows(ZI, near), zi_s)
+    sent(in_of(ZI, near), zi_s)
     sent(ZI.at[pl.ds(0, 4)], zie_s)
 
     @pl.when(middle)
@@ -1145,24 +1220,18 @@
         sent(WQKV.at[pl.ds(0, 256)], wqf_s)
         sent(WIN.at[pl.ds(0, 256)], wif_s)
 
-    @pl.when(z == c)
-    def _():
-        sent(WOUT, woz_s)
-        sent(odown.at[pl.ds(0, 256)], fo_s)
-
-    @pl.when(out_on)
-    def _():
-        sent(oout, fo_s)
-
-    @pl.when(z != c)
-    def _():
-        sent(out_piece, wob_s)
-        sent(ZO, zo_s)
-
-        @pl.when(middle & (z // 2 != c // 2))
-        def _():
-            sent(out_piece, woz_s)
-
+    @pl.when(middle)
+    def _():
+        sent(WOUT.at[pl.ds(0, 128)], woz_s)
+
+    @pl.when(at_end)
+    def _():
+        sent(WOUT.at[pl.ds(0, 64)], woz_s)
+
+    sent(WOUT.at[pl.ds(0, 96)], wob_s)
+    sent(ZO.at[near], zo_s)
+    sent(ZO.at[pl.ds(0, 2)], zoe_s)
+    sent(oout.at[pl.ds(0, 96)], fo_s)
     sent(DD.at[k1], sib_s.at[0])
     sent(DI.at[k1], sib_s.at[1])
     sent(DQ.at[k1, :, :, value_cols], sib_s.at[2])
@@ -1179,22 +1248,13 @@
 def plane_shards(
     inputs, cotangent, w_query, w_key, w_value, w_out, w_in, w_down, gain_attn, gain_mlp, rel_bias, buckets
 ):
-    pack = jnp.concatenate(
-        [
-            gain_attn.astype(F32)[None],
-            gain_mlp.astype(F32)[None],
-            jnp.pad(rel_bias.astype(F32), (0, 64))[None],
-            jnp.zeros((5, 128), F32),
-        ],
-        axis=0,
-    )
-    bucket_row = jnp.pad(buckets, (0, 1))[None]
     vm = pltpu.VMEM
     dma = pltpu.SemaphoreType.DMA
     block = lambda kind: vm((TOKENS, WIDTH), kind)
     tokens = lambda width, kind: vm((512, width), kind)
     scratch = [
-        block(BF), block(BF), vm((8, 8, 128), F32),
+        block(BF), block(BF), vm((8, 128), F32), vm((1, 1024), jnp.int32),
+        vm((3, 128, 1024), BF), vm((64, 768), BF), vm((8, 8, 128), F32),
         tokens(1024, BF), tokens(1024, BF), tokens(1024, BF), tokens(1024, BF), tokens(1024, BF),
         vm((1024, 768), BF), vm((256, 1024), BF), vm((1024, 1024), BF), vm((1024, 1024), BF),
         tokens(768, BF), vm((4, 512, 512), F32), vm((4, 512, 512), BF), vm((4, 128, 1024), F32),
@@ -1203,19 +1263,20 @@
         tokens(1024, BF), tokens(1024, BF), tokens(1024, BF), tokens(1024, BF),
         vm((4, 128, 1024), BF), vm((4, 128, 1024), BF), vm((4, 128, 1024), BF), vm((4, 128, 1024), BF),
         block(F32), block(F32), block(BF), block(BF),
-        vm((2, 8, 64, 768), BF), vm((2, 128, 1024), BF), vm((2, 8, 64, 1024), BF), vm((2, 4, 128, 1024), BF),
-        vm((8, 64, 768), BF), vm((128, 1024), BF), vm((8, 64, 1024), BF), vm((4, 128, 1024), BF),
-        vm((8, 64, 768), BF), vm((128, 1024), BF), vm((8, 64, 1024), BF), vm((4, 128, 1024), BF),
-        vm((4, 2, 64, 768), BF), vm((2, 128, 1024), BF), vm((8, 64, 1024), BF), vm((4, 128, 1024), BF),
-        vm((2, 64, 1024), BF),
-        vm((2, 64, 768), BF), vm((128, 1024), BF), vm((2, 4, 64, 256), BF), vm((128, 1024), BF),
+        vm((2, 8, 64, 768), BF), vm((2, 4, 32, 1024), BF), vm((2, 8, 64, 1024), BF), vm((2, 4, 128, 1024), BF),
+        vm((8, 64, 768), BF), vm((4, 32, 1024), BF), vm((8, 64, 1024), BF), vm((4, 128, 1024), BF),
+        vm((8, 64, 768), BF), vm((4, 32, 1024), BF), vm((8, 64, 1024), BF), vm((4, 128, 1024), BF),
+        vm((8, 64, 768), BF), vm((4, 32, 1024), BF), vm((8, 64, 1024), BF), vm((4, 128, 1024), BF),
+        vm((2, 64, 768), BF), vm((32, 1024), BF), vm((2, 64, 1024), BF), vm((128, 1024), BF),
+        vm((2, 64, 768), BF), vm((32, 1024), BF), vm((2, 4, 64, 256), BF), vm((128, 1024), BF),
         vm((3, 8, 128), F32), vm((8, 3, 8, 128), F32), vm((4, 8, 128), F32), vm((4, 8, 128), F32),
-        dma((7,)), dma, dma, dma, dma, dma, dma((4,)), dma((2,)), dma, dma((4,)), dma((2,)), dma, dma((4,)), dma((2,)), dma, dma((4,)), dma((2,)),
+        dma((7,)), dma, dma, dma, dma((4,)), dma((2,)), dma, dma((4,)), dma((2,)), dma, dma((4,)), dma((2,)), dma, dma((4,)), dma((2,)),
         dma, dma, dma, dma, dma, dma, dma, dma,
         dma((2,)), dma((2,)), dma, dma, dma((8,)), dma, dma, dma, dma, dma((8,)), dma, dma,
-        dma, dma, dma((4,)), dma, dma, dma, dma, dma, dma,
-        dma((5,)), dma((5,)), dma, dma, dma, dma, dma, dma((2,)), dma, dma, dma((4,)), dma, dma, dma,
-        dma, dma, dma((4,)), dma, dma, dma, dma, dma, dma((4,)), dma, dma, dma((3,)), dma, dma, dma, dma,
+        dma, dma, dma((4,)), dma, dma, dma, dma((4,)), dma, dma,
+        dma((5,)), dma((5,)), dma((4,)), dma, dma, dma((4,)), dma, dma, dma, dma((4,)), dma, dma, dma, dma((4,)), dma,
+        dma, dma, dma((4,)), dma, dma, dma, dma((4,)), dma,
+        dma, dma, dma((4,)), dma, dma, dma((3,)), dma, dma, dma((4,)), dma, dma, dma((3,)), dma, dma, dma, dma,
     ]
     anywhere = pl.BlockSpec(memory_space=pl.ANY)
     in_vmem = pl.BlockSpec(memory_space=pltpu.VMEM)
@@ -1231,14 +1292,14 @@
             shape((512, 1024), BF),
             shape((8, 128), F32),
         ),
-        in_specs=[anywhere] * 9 + [in_vmem],
+        in_specs=[anywhere] * 8 + [in_vmem] * 4,
         out_specs=(in_vmem, in_vmem, anywhere, anywhere, anywhere, anywhere, in_vmem),
         scratch_shapes=scratch,
         compiler_params=pltpu.CompilerParams(
             collective_id=0, has_side_effects=True, vmem_limit_bytes=63 << 20
         ),
         cost_estimate=pl.CostEstimate(flops=11 * 10**9, bytes_accessed=16 * 2**20, transcendentals=3 * 2**20),
-    )(inputs, cotangent, w_query, w_key, w_value, w_out, w_in, w_down, pack, bucket_row)
+    )(inputs, cotangent, w_query, w_key, w_value, w_out, w_in, w_down, gain_attn[None], gain_mlp[None], rel_bias[None], buckets[None])
     return finish(output, grad_inputs, proj, out, hidden, down, small)
 
 
@@ -1267,11 +1328,11 @@
 
     moves[0].wait()
     for w, place in enumerate((o_query, o_key, o_value)):
-        for q in range(4):
-            x, y = q // 2, q % 2
-            for j in range(2):
-                first = 512 * y + 256 * j + 128 * x
-                w_proj[w, :, first : first + 128] = b_proj[q, :, 256 * w + 128 * j : 256 * w + 128 * j + 128].astype(F32)
+        for shard in range(8):
+            z, x = shard // 2, shard % 2
+            lanes = slice(256 * w + 64 * z, 256 * w + 64 * z + 64)
+            parts = [b_proj[2 * x + y, :, lanes].astype(F32) for y in range(2)]
+            w_proj[w, :, 128 * shard : 128 * shard + 128] = jnp.concatenate(parts, axis=1)
         write(w_proj.at[w], place, w)
     moves[1].wait()
     for r in range(4):

time: 156 us -> 144 us (0.923); the launches traced: 154 us -> 144 us
  Pallas kernels: 150 us -> 143 us
  other arithmetic: 1.99 us -> 0 us
    pallas_call x1, Pallas kernels: 146 us -> 138 us  [plane_shards(): pl.pallas_call(fused_layer, out_shape=(shape((1, TOKENS, WIDTH), BF), sha...]
where the time goes in v4:
time: 144 us
  Pallas kernels  143 us (99%)
    pallas_call x1, Pallas kernels, plane_shards(): pl.pallas_call(fused_layer, out_shape=(shape((1, TOKENS, WIDTH), BF), sha...  138 us
    pallas_call x1, Pallas kernels, finish(): pl.pallas_call(finish_kernel, out_shape=(shape(output.shape, BF), shape(g...  4.8 us

profile of v4, /device:TPU:0, one launch (start us, length us, event | category | flops | bytes accessed | tf_op | source)
XLA Modules:
  0.0 143.9 jit_solution(3118107227851844279)
XLA Ops:
  0.6 138.4 %shard_map.203 = (bf16[1,128,1024]{2,1,0:T(8,128)(2,1)}, bf16[1,128,1024]{2,1,0:T(8,128)(2,1)}, bf16[4,128,768]{2,1,0:T(8,128)(2,1)}, bf16[128,1024]{1,0:T(8,128...) custom-call(bf16[1,128,1024]{2,1,0:T(8,128)(2,1)} %x_in.1, ...), custom_call_target="tpu_custom_call" | custom-call | flops 11000000512 | bytes 16777216 | tf_op jit(solution)/shard_map/pallas_call | solution.py:1284
  139.1 4.8 %shard_map.204 = (bf16[1,128,1024]{2,1,0:T(8,128)(2,1)}, bf16[1,128,1024]{2,1,0:T(8,128)(2,1)}, f32[128,1024]{1,0:T(8,128)}, f32[128,1024]{1,0:T(8,128)}, f32[12...) custom-call(bf16[1,128,1024]{2,1,0:T(8,128)(2,1)} %get-tuple-element, ...), custom_call_target="tpu_custom_call" | custom-call | bytes 10485760 | tf_op jit(solution)/shard_map/pallas_call | solution.py:1369

commit v5 on v4

--- a/solution.py
+++ b/solution.py
@@ -297,13 +297,19 @@
 
 
 def rows_at(start, count):
-    return pl.ds(pl.multiple_of(start, count), count)
+    return pl.ds(start if isinstance(start, int) else pl.multiple_of(start, count), count)
 
 
 def remote(src, dst, send, recv, device):
     return pltpu.make_async_remote_copy(
         src_ref=src, dst_ref=dst, send_sem=send, recv_sem=recv, device_id=device, device_id_type=MESH_ID
     )
+
+
+def steps(count, body, carry):
+    for i in range(count):
+        carry = body(i, carry)
+    return carry
 
 
 def fused_layer(
@@ -311,16 +317,16 @@
     out_ref, gin_ref, oqkv, oout, oin, odown, small_ref,
     XO, CO, PACK, BUCKET, STAGE, ACROSS, GP, XB, COT, N1, NTB, GAL, WQKV, WOUT, WIN, WDOWN,
     QKV, PROB, PLOW, BIAS, AT, ACT, SLOPE, GPRE, GATT, DQKV, DS, BACC,
-    SA, SG, SO, SN, RA, RG, RO, RN, HID, GH, NTS, GALS,
+    SA, SG, SO, SN, RA, RG, RO, RN, XA, XG, XS, XN, HID, GH, NTS, GALS,
     DQ, DO, DI, DD, SIBQ, SIBO, SIBI, SIBD, ZQ, ZO, ZI, ZD, REQ, REO, REI, RED, RCQ, RCO, RCI, RCD, FQ, FO, FI, FD,
     SMALL, RSMALL, PSMALL, RZSMALL,
     loc, gp_s, gp_r, xb_s, xb_r, xb_p, co_s, co_r, co_p, nt_s, nt_r, nt_p, ga_s, ga_r, ga_p,
-    a_s, a_r, g_s, g_r, o_s, o_r, n_s, n_r,
+    a_s, a_r, a_x, g_s, g_r, g_x, o_s, o_r, o_x, n_s, n_r, n_x,
     wx_s, wx_r, wqz_s, wqf_s, wqz_r, wqb_s, wqb_r, wiz_s, wif_s, wiz_r, wib_s, wib_r,
     wdz_s, wdf_s, wdz_r, wdb_s, wdb_r, woz_s, woz_r, wob_s, wob_r,
     sib_s, sib_r, sibd_r, zq_s, zqe_s, zq_r, zqc_r, zv_s, zve_s, zv_r, zvc_r, zo_s, zoe_s, zo_r, zoc_r,
     zi_s, zie_s, zi_r, zic_r, zd_s, zde_s, zd_r, zdc_r,
-    fq_s, fqb_s, fq_r, fqb_r, fo_s, fo_r, fi_s, fib_s, fi_r, fib_r, fd_s, fd_r, sp_s, sp_r, sz_s, sz_r,
+    fq_s, fqb_s, fq_r, fqb_r, fv_s, fvb_s, fv_r, fvb_r, fo_s, fo_r, fi_s, fib_s, fi_r, fib_r, fd_s, fd_r, sp_s, sp_r, sz_s, sz_r,
 ):
     c = lax.axis_index("ctx")
     f = lax.axis_index("fsdp")
@@ -405,17 +411,40 @@
         def _():
             sent(buf, send)
 
-    def scatter_send(buf, dst, send, got, b):
-        src = buf.at[rows_at(b * TOKENS, TOKENS)]
-        here = (b == c) & (x == k)
-
-        @pl.when(here)
-        def _():
-            pltpu.make_async_copy(src, dst.at[q], got).start()
-
-        @pl.when(jnp.logical_not(here))
-        def _():
-            remote(src, dst.at[q], send, got, (b, 2 * z + k)).start()
+    first_pair = 1 - pass_y
+
+    def scatter_first(buf, dst, send, got, cross, cross_got, i):
+        b = 2 * first_pair + i
+
+        @pl.when(k != x)
+        def _():
+            remote(block_half(buf, b, 0), cross.at[i], send, cross_got.at[i], (2 * y1 + k, f)).start()
+            remote(block_half(buf, b, 1), cross.at[i], send, cross_got.at[i], (c, f1)).start()
+
+        whole = buf.at[rows_at(b * TOKENS, TOKENS)]
+
+        @pl.when((k == x) & (i == k))
+        def _():
+            pltpu.make_async_copy(whole, dst.at[0], got).start()
+
+        @pl.when((k == x) & (i != k))
+        def _():
+            remote(whole, dst.at[0], send, got, sib).start()
+
+    def scatter_half(buf, dst, send, got, i, h):
+        b = 2 * pass_y + i
+        place = dst.at[1 + same, rows_at(64 * h, 64)]
+        remote(block_half(buf, b, h), place, send, got, (b, 2 * z + k)).start()
+
+    def scatter_second(buf, dst, send, got, i):
+        scatter_half(buf, dst, send, got, i, 1 - same)
+
+    def scatter_sums(buf, dst, send, got, cross, cross_got):
+        for i in range(2):
+            recv(cross.at[i], cross_got.at[i])
+            rows = rows_at((2 * pass_y + i) * TOKENS + 64 * same, 64)
+            buf[rows, :] = (buf[rows, :].astype(F32) + cross[i].astype(F32)).astype(BF)
+            scatter_half(buf, dst, send, got, i, same)
 
     def half(fb, kk):
         return rows_at(fb * 128 + kk * 64, 64)
@@ -619,7 +648,7 @@
             N1[rows, :] = (values * scale * gain_one).astype(BF)
             return inner
 
-        return lax.fori_loop(0, 4, chunk, carry)
+        return steps(4, chunk, carry)
 
     lax.fori_loop(0, 4, norm_block, 0)
 
@@ -654,7 +683,7 @@
         QKV[:, cols] = dot_nn(N1[...], WQKV[:, cols]).astype(BF)
         return carry
 
-    lax.fori_loop(0, 3, project, 0)
+    steps(3, project, 0)
 
 
     gather_pass(COT, co_s, co_r, co_p)
@@ -670,9 +699,8 @@
         return jnp.where(keep, values, jnp.zeros_like(values))
 
     def attend(i, carry):
-        b = lax.rem(2 * y1 + i, 4)
+        b = lax.rem(2 * first_pair + i, 4)
         rows = rows_at(b * TOKENS, TOKENS)
-        window = rows_at(384 - 128 * b, 128)
         window = pl.ds(pl.multiple_of(384 - 128 * b, 128), 512)
         for j in range(2):
             outs = []
@@ -701,10 +729,19 @@
             recv(WOUT.at[pl.ds(0, 96)], wob_r)
 
         SA[rows, :] = dot_nn(AT[rows, :], WOUT[...]).astype(BF)
-        scatter_send(SA, RA, a_s, a_r, b)
+
+        @pl.when(i < 2)
+        def _():
+            scatter_first(SA, RA, a_s, a_r, XA, a_x, i)
+
+        @pl.when(i >= 2)
+        def _():
+            scatter_second(SA, RA, a_s, a_r, i - 2)
+
         return carry
 
     lax.fori_loop(0, 4, attend, 0)
+    scatter_sums(SA, RA, a_s, a_r, XA, a_x)
 
     for xx in (x, x1):
         g = of_row(near, xx)
@@ -727,14 +764,14 @@
     def home_forward(r, carry):
         rows = rows_at(r * 32, 32)
         hidden = XO[rows, :].astype(F32)
-        for s in range(4):
+        for s in range(3):
             hidden = hidden + RA[s, rows, :].astype(F32)
         HID[rows, :] = hidden
         scale = lax.rsqrt(jnp.mean(hidden * hidden, axis=-1, keepdims=True) + EPS)
         NTS[rows, :] = (hidden * scale * gain_two).astype(BF)
         return carry
 
-    lax.fori_loop(0, 4, home_forward, 0)
+    steps(4, home_forward, 0)
     gather_send(NTS, NTB, nt_s, nt_r, nt_p)
 
     def down_piece(t, kk):
@@ -775,7 +812,7 @@
             SLOPE[rows, cols] = cdf + pre * jnp.exp(-0.5 * pre * pre) * 0.3989422804014327
             return inner
 
-        return lax.fori_loop(0, 4, hidden_units, carry)
+        return steps(4, hidden_units, carry)
 
     lax.fori_loop(0, 2, feed, 0)
 
@@ -792,7 +829,7 @@
         remote(DD.at[k1, m], SIBD.at[m], sib_s.at[0], sibd_r.at[i], sib).start()
         return carry
 
-    lax.fori_loop(0, 4, grad_down, 0)
+    steps(4, grad_down, 0)
 
     def join_down(i, carry):
         m = jnp.where(i < 2, other + i, jnp.where(i == 2, near, z))
@@ -809,7 +846,7 @@
 
         return carry
 
-    lax.fori_loop(0, 4, join_down, 0)
+    steps(4, join_down, 0)
 
     @pl.when(at_end)
     def _():
@@ -819,7 +856,7 @@
     recv(WDOWN.at[pl.ds(0, 384)], wdb_r)
 
     def back_feed(i, carry):
-        yy = lax.rem(y1 + i, 2)
+        yy = lax.rem(first_pair + i, 2)
         rows = rows_at(256 * yy, 256)
 
         def back_act(n, inner):
@@ -827,16 +864,25 @@
             GPRE[rows, cols] = (dot_nt(COT[rows, :], WDOWN[cols, :]) * SLOPE[rows, cols]).astype(BF)
             return inner
 
-        lax.fori_loop(0, 4, back_act, 0)
+        steps(4, back_act, 0)
 
         def back_normed(n, inner):
             cols = rows_at(256 * n, 256)
             SG[rows, cols] = dot_nt(GPRE[rows, :], WIN[cols, :]).astype(BF)
             return inner
 
-        lax.fori_loop(0, 4, back_normed, 0)
-        scatter_send(SG, RG, g_s, g_r, 2 * yy)
-        scatter_send(SG, RG, g_s, g_r, 2 * yy + 1)
+        steps(4, back_normed, 0)
+
+        @pl.when(i == 0)
+        def _():
+            for n in range(2):
+                scatter_first(SG, RG, g_s, g_r, XG, g_x, n)
+
+        @pl.when(i == 1)
+        def _():
+            for n in range(2):
+                scatter_second(SG, RG, g_s, g_r, n)
+
         return carry
 
     lax.fori_loop(0, 2, back_feed, 0)
@@ -848,7 +894,8 @@
             DI[1, 2 * m + part] = tile[128 * part + 64 : 128 * part + 128]
         return carry
 
-    lax.fori_loop(0, 4, grad_in, 0)
+    steps(4, grad_in, 0)
+    scatter_sums(SG, RG, g_s, g_r, XG, g_x)
     remote(DI.at[k1], SIBI, sib_s.at[1], sib_r.at[1], sib).start()
 
     def down_project(n, carry):
@@ -856,7 +903,7 @@
         SO[:, cols] = dot_nn(ACT[...], WDOWN[:, cols]).astype(BF)
         return carry
 
-    lax.fori_loop(0, 4, down_project, 0)
+    steps(4, down_project, 0)
 
     recv(SIBI, sib_r.at[1])
 
@@ -864,15 +911,21 @@
         ZI[m] = (DI[k, m].astype(F32) + SIBI[m].astype(F32)).astype(BF)
         return carry
 
-    lax.fori_loop(0, 8, join_in, 0)
+    steps(8, join_in, 0)
     reduce_others(in_of, ZI, REI, zie_s, zi_r)
+
+    @pl.when(at_end)
+    def _():
+        reduce_near(down_of, ZD, RED, zd_s, zd_r)
+
+    reduce_near(in_of, ZI, REI, zi_s, zi_r)
 
     recv(RG, g_r)
 
     def home_back(r, total):
         rows = rows_at(r * 32, 32)
         grad = RG[0, rows, :].astype(F32)
-        for s in range(1, 4):
+        for s in range(1, 3):
             grad = grad + RG[s, rows, :].astype(F32)
         hidden = HID[rows, :]
         scale = lax.rsqrt(jnp.mean(hidden * hidden, axis=-1, keepdims=True) + EPS)
@@ -883,7 +936,7 @@
         GALS[rows, :] = back.astype(BF)
         return total + jnp.sum((grad * hidden * scale).reshape(4, 8, WIDTH), axis=0)
 
-    mlp_gain_grad = lax.fori_loop(0, 4, home_back, jnp.zeros((8, WIDTH), F32))
+    mlp_gain_grad = steps(4, home_back, jnp.zeros((8, WIDTH), F32))
     gather_send(GALS, GAL, ga_s, ga_r, ga_p)
     reduce_middle(down_of, ZD, RED, RCD, zde_s, zd_r, zdc_r)
 
@@ -892,83 +945,26 @@
         SMALL[1, g : g + 1, :] = mlp_gain_grad[:, 128 * g : 128 * g + 128]
 
     gather_pass(GAL, ga_s, ga_r, ga_p)
-
-    def back_out(i, carry):
+    for i in range(2):
+        scatter_first(SO, RO, o_s, o_r, XS, o_x, i)
+        scatter_second(SO, RO, o_s, o_r, i)
+
+    all_low = lax.broadcasted_iota(jnp.int32, (512, 128), 1) < 64
+
+    def pick_all(values, hh):
+        keep = all_low if hh == 0 else jnp.logical_not(all_low)
+        return jnp.where(keep, values, jnp.zeros_like(values))
+
+    def attend_back(i, carry):
         b = lax.rem(2 * y + i, 4)
         rows = rows_at(b * TOKENS, TOKENS)
         gather_wait(GAL, ga_r, b)
+
+        @pl.when(i == 2)
+        def _():
+            reduce_middle(in_of, ZI, REI, RCI, zie_s, zi_r, zic_r)
+
         GATT[rows, :] = dot_nt(GAL[rows, :], WOUT[...]).astype(BF)
-        return carry
-
-    lax.fori_loop(0, 4, back_out, 0)
-    for i in range(4):
-        scatter_send(SO, RO, o_s, o_r, lax.rem(2 * y1 + i, 4))
-    all_low = lax.broadcasted_iota(jnp.int32, (512, 128), 1) < 64
-
-    def pick_all(values, hh):
-        keep = all_low if hh == 0 else jnp.logical_not(all_low)
-        return jnp.where(keep, values, jnp.zeros_like(values))
-
-    def grad_values(j, carry):
-        grad_att = GATT[:, rows_at(128 * j, 128)]
-        first = dot_tn(PLOW[2 * j], pick_all(grad_att, 0))
-        second = dot_tn(PLOW[2 * j + 1], pick_all(grad_att, 1))
-        DQKV[:, pl.ds(pl.multiple_of(512 + 128 * j, 128), 128)] = jnp.where(all_low, first, second).astype(BF)
-        return carry
-
-    lax.fori_loop(0, 2, grad_values, 0)
-
-    def grad_proj(first, width):
-        def step(m, carry):
-            tile = dot_tn(N1[:, rows_at(256 * m, 256)], DQKV[:, first : first + width]).astype(BF)
-            for part in range(2):
-                DQ[0, 2 * m + part, :, first : first + width] = tile[128 * part : 128 * part + 64]
-                DQ[1, 2 * m + part, :, first : first + width] = tile[128 * part + 64 : 128 * part + 128]
-            return carry
-
-        lax.fori_loop(0, 4, step, 0)
-
-    def join_proj(first, width):
-        def step(m, carry):
-            total = DQ[k, m, :, first : first + width].astype(F32) + SIBQ[m, :, first : first + width].astype(F32)
-            ZQ[m, :, first : first + width] = total.astype(BF)
-            return carry
-
-        lax.fori_loop(0, 8, step, 0)
-
-    grad_proj(512, 256)
-    remote(DQ.at[k1, :, :, value_cols], SIBQ.at[:, :, value_cols], sib_s.at[2], sib_r.at[2], sib).start()
-
-    def grad_out_rows(m, carry):
-        tile = dot_tn(AT[:, rows_at(128 * m, 128)], GAL[...]).astype(BF)
-        for n in range(2):
-            for kk in range(2):
-                DO[kk, 2 * m + n] = tile[64 * n + 32 * kk : 64 * n + 32 * kk + 32]
-        return carry
-
-    lax.fori_loop(0, 2, grad_out_rows, 0)
-    remote(DO.at[k1], SIBO, sib_s.at[3], sib_r.at[3], sib).start()
-
-    recv(SIBQ.at[:, :, value_cols], sib_r.at[2])
-    join_proj(512, 256)
-    reduce_others(value_of, ZQ, REQ, zve_s, zv_r)
-
-    recv(SIBO, sib_r.at[3])
-    ZO[...] = (DO[k].astype(F32) + SIBO[...].astype(F32)).astype(BF)
-
-    reduce_others(down_of, ZO, REO, zoe_s, zo_r)
-
-    @pl.when(middle)
-    def _():
-        reduce_near(in_of, ZI, REI, zi_s, zi_r)
-        reduce_near(value_of, ZQ, REQ, zv_s, zv_r)
-        reduce_near(down_of, ZO, REO, zo_s, zo_r)
-
-    reduce_middle(in_of, ZI, REI, RCI, zie_s, zi_r, zic_r)
-
-    def attend_back(i, carry):
-        rows = rows_at(i * TOKENS, TOKENS)
-        window = pl.ds(pl.multiple_of(384 - 128 * i, 128), 512)
         for j in range(2):
             pair = slice(128 * j, 128 * j + 128)
             keys = QKV[:, 256 + 128 * j : 384 + 128 * j]
@@ -982,12 +978,12 @@
                 inner = jnp.sum(probs * grad_probs, axis=-1, keepdims=True)
                 grad_scores = (probs * (grad_probs - inner)).astype(BF)
                 DS[h, rows, :] = grad_scores
-                BACC[h, :, window] = BACC[h, :, window] + grad_scores.astype(F32)
                 outs.append(dot_nn(grad_scores, keys))
             DQKV[rows, pair] = jnp.where(low_lanes, outs[0], outs[1]).astype(BF)
         return carry
 
     lax.fori_loop(0, 4, attend_back, 0)
+    scatter_sums(SO, RO, o_s, o_r, XS, o_x)
 
     def grad_keys(j, carry):
         query = QKV[:, rows_at(128 * j, 128)]
@@ -996,22 +992,55 @@
         DQKV[:, pl.ds(pl.multiple_of(256 + 128 * j, 128), 128)] = jnp.where(all_low, first, second).astype(BF)
         return carry
 
-    lax.fori_loop(0, 2, grad_keys, 0)
-
-    @pl.when(at_end)
-    def _():
-        reduce_near(down_of, ZD, RED, zd_s, zd_r)
-
-    reduce_middle(value_of, ZQ, REQ, RCQ.at[:, :, value_cols], zve_s, zv_r, zvc_r)
-    reduce_middle(down_of, ZO, REO, RCO, zoe_s, zo_r, zoc_r)
+    steps(2, grad_keys, 0)
+
+    def grad_values(j, carry):
+        grad_att = GATT[:, rows_at(128 * j, 128)]
+        first = dot_tn(PLOW[2 * j], pick_all(grad_att, 0))
+        second = dot_tn(PLOW[2 * j + 1], pick_all(grad_att, 1))
+        DQKV[:, pl.ds(pl.multiple_of(512 + 128 * j, 128), 128)] = jnp.where(all_low, first, second).astype(BF)
+        return carry
+
+    steps(2, grad_values, 0)
+
+    def grad_proj(first, width):
+        def step(m, carry):
+            tile = dot_tn(N1[:, rows_at(256 * m, 256)], DQKV[:, first : first + width]).astype(BF)
+            for part in range(2):
+                DQ[0, 2 * m + part, :, first : first + width] = tile[128 * part : 128 * part + 64]
+                DQ[1, 2 * m + part, :, first : first + width] = tile[128 * part + 64 : 128 * part + 128]
+            return carry
+
+        steps(4, step, 0)
+
+    def join_proj(first, width):
+        def step(m, carry):
+            total = DQ[k, m, :, first : first + width].astype(F32) + SIBQ[m, :, first : first + width].astype(F32)
+            ZQ[m, :, first : first + width] = total.astype(BF)
+            return carry
+
+        steps(8, step, 0)
+
     grad_proj(0, 512)
     remote(DQ.at[k1, :, :, other_cols], SIBQ.at[:, :, other_cols], sib_s.at[4], sib_r.at[4], sib).start()
+    grad_proj(512, 256)
+    remote(DQ.at[k1, :, :, value_cols], SIBQ.at[:, :, value_cols], sib_s.at[2], sib_r.at[2], sib).start()
+
     def back_project(i, carry):
-        yy = lax.rem(y1 + i, 2)
+        yy = lax.rem(first_pair + i, 2)
         rows = rows_at(256 * yy, 256)
         SN[rows, :] = dot_nt(DQKV[rows, :], WQKV[...]).astype(BF)
-        scatter_send(SN, RN, n_s, n_r, 2 * yy)
-        scatter_send(SN, RN, n_s, n_r, 2 * yy + 1)
+
+        @pl.when(i == 0)
+        def _():
+            for n in range(2):
+                scatter_first(SN, RN, n_s, n_r, XN, n_x, n)
+
+        @pl.when(i == 1)
+        def _():
+            for n in range(2):
+                scatter_second(SN, RN, n_s, n_r, n)
+
         return carry
 
     lax.fori_loop(0, 2, back_project, 0)
@@ -1020,14 +1049,34 @@
     join_proj(0, 512)
     reduce_others(other_of, ZQ, REQ, zqe_s, zq_r)
 
-    @pl.when(at_end)
-    def _():
-        reduce_near(in_of, ZI, REI, zi_s, zi_r)
-        reduce_near(value_of, ZQ, REQ, zv_s, zv_r)
-        reduce_near(down_of, ZO, REO, zo_s, zo_r)
-
+    def grad_out_rows(m, carry):
+        tile = dot_tn(AT[:, rows_at(128 * m, 128)], GAL[...]).astype(BF)
+        for n in range(2):
+            for kk in range(2):
+                DO[kk, 2 * m + n] = tile[64 * n + 32 * kk : 64 * n + 32 * kk + 32]
+        return carry
+
+    steps(2, grad_out_rows, 0)
+    remote(DO.at[k1], SIBO, sib_s.at[3], sib_r.at[3], sib).start()
+    scatter_sums(SN, RN, n_s, n_r, XN, n_x)
+    recv(SIBQ.at[:, :, value_cols], sib_r.at[2])
+    join_proj(512, 256)
+    reduce_others(value_of, ZQ, REQ, zve_s, zv_r)
+    recv(SIBO, sib_r.at[3])
+    ZO[...] = (DO[k].astype(F32) + SIBO[...].astype(F32)).astype(BF)
+    reduce_others(down_of, ZO, REO, zoe_s, zo_r)
     reduce_near(other_of, ZQ, REQ, zq_s, zq_r)
-
+    reduce_near(value_of, ZQ, REQ, zv_s, zv_r)
+    reduce_near(down_of, ZO, REO, zo_s, zo_r)
+
+    def place_scores(i, carry):
+        rows = rows_at(i * TOKENS, TOKENS)
+        window = pl.ds(pl.multiple_of(384 - 128 * i, 128), 512)
+        for h in range(4):
+            BACC[h, :, window] = BACC[h, :, window] + DS[h, rows, :].astype(F32)
+        return carry
+
+    lax.fori_loop(0, 4, place_scores, 0)
     head_sums = []
     for h in range(4):
         rest = BACC[h]
@@ -1051,7 +1100,6 @@
 
     lax.fori_loop(0, 8, bucket_sums, 0)
 
-    reduce_middle(other_of, ZQ, REQ, RCQ.at[:, :, other_cols], zqe_s, zq_r, zqc_r)
     recv(RED.at[z], zd_r.at[z])
     recv(RCD, zdc_r)
     FD[...] = (ZD[z].astype(F32) + RED[z].astype(F32) + RCD[...].astype(F32)).astype(BF)
@@ -1082,26 +1130,23 @@
     def in_place(qq, kk):
         return oin.at[:, qq, rows_at(64 * kk, 64), :]
 
-    def proj_place(qq, kk):
-        return oqkv.at[qq, rows_at(64 * kk, 64), :]
-
     recv(RO, o_r)
 
     def home_out(r, carry):
         rows = rows_at(r * 32, 32)
         result = HID[rows, :]
-        for s in range(4):
+        for s in range(3):
             result = result + RO[s, rows, :].astype(F32)
         out_ref[0, rows, :] = result.astype(BF)
         return carry
 
-    lax.fori_loop(0, 4, home_out, 0)
+    steps(4, home_out, 0)
     recv(RN, n_r)
 
     def home_inputs(r, total):
         rows = rows_at(r * 32, 32)
         grad = RN[0, rows, :].astype(F32)
-        for s in range(1, 4):
+        for s in range(1, 3):
             grad = grad + RN[s, rows, :].astype(F32)
         values = XO[rows, :].astype(F32)
         scale = lax.rsqrt(jnp.mean(values * values, axis=-1, keepdims=True) + EPS)
@@ -1111,7 +1156,7 @@
         gin_ref[0, rows, :] = back.astype(BF)
         return total + jnp.sum((grad * values * scale).reshape(4, 8, WIDTH), axis=0)
 
-    attn_gain_grad = lax.fori_loop(0, 4, home_inputs, jnp.zeros((8, WIDTH), F32))
+    attn_gain_grad = steps(4, home_inputs, jnp.zeros((8, WIDTH), F32))
     attn_gain_grad = jnp.sum(attn_gain_grad, axis=0, keepdims=True)
     for g in range(8):
         SMALL[0, g : g + 1, :] = attn_gain_grad[:, 128 * g : 128 * g + 128]
@@ -1130,30 +1175,31 @@
             FI[xx, j] = total[:, 256 * j : 256 * j + 256].astype(BF)
     spread(FI, in_place, fi_s, fib_s, fi_r, fib_r)
 
-    recv(value_of(REQ, z), zv_r.at[z])
-    recv(other_of(REQ, z), zq_r.at[z])
-    recv(RCQ.at[:, :, value_cols], zvc_r)
-    recv(RCQ.at[:, :, other_cols], zqc_r)
-    for xx in range(2):
-        total = ZQ[2 * z + xx].astype(F32) + REQ[2 * z + xx].astype(F32) + RCQ[xx].astype(F32)
-        FQ[xx] = total.astype(BF)
-    spread(FQ, proj_place, fq_s, fqb_s, fq_r, fqb_r)
-
-    recv(REO.at[z], zo_r.at[z])
-    recv(RCO, zoc_r)
-    FO[...] = (ZO[z].astype(F32) + REO[z].astype(F32) + RCO[...].astype(F32)).astype(BF)
+    reduce_middle(other_of, ZQ, REQ, RCQ.at[:, :, other_cols], zqe_s, zq_r, zqc_r)
+    reduce_middle(value_of, ZQ, REQ, RCQ.at[:, :, value_cols], zve_s, zv_r, zvc_r)
+    reduce_middle(down_of, ZO, REO, RCO, zoe_s, zo_r, zoc_r)
+
+    def final_proj(of, cols, first, width, sem, final_sem):
+        recv(of(REQ, z), sem.at[z])
+        recv(RCQ.at[:, :, cols], final_sem)
+        for xx in range(2):
+            total = ZQ[2 * z + xx, :, first : first + width].astype(F32)
+            total = total + REQ[2 * z + xx, :, first : first + width].astype(F32)
+            total = total + RCQ[xx, :, first : first + width].astype(F32)
+            FQ[xx, :, first : first + width] = total.astype(BF)
+
+    def other_place(qq, kk):
+        return oqkv.at[qq, rows_at(64 * kk, 64), other_cols]
+
+    def value_place(qq, kk):
+        return oqkv.at[qq, rows_at(64 * kk, 64), value_cols]
 
     def out_rows(cc):
         return oout.at[rows_at(32 * cc, 32)]
-
-    remote(FO, out_rows(c), fo_s, fo_r.at[1], y_core).start()
-    remote(FO, out_rows(c), fo_s, fo_r.at[2], sib).start()
-    pltpu.make_async_copy(FO, out_rows(c), fo_r.at[0]).start()
 
     y_rows = down_rows(2 * y1 + k)
     recv(y_rows, fd_r.at[1])
     remote(y_rows, y_rows, fd_s, fd_r.at[2], sib).start()
-    spread_on(in_place, fib_s, fi_r, fib_r)
     recv(RSMALL.at[pl.ds(0, 7)], sp_r)
     plane_sum = SMALL[...]
     for i in range(4):
@@ -1168,7 +1214,19 @@
     for t in zs:
         remote(PSMALL.at[t], RZSMALL.at[z], sz_s, sz_r, zdev(t)).start()
 
-    spread_on(proj_place, fqb_s, fq_r, fqb_r)
+    final_proj(other_of, other_cols, 0, 512, zq_r, zqc_r)
+    spread(FQ.at[:, :, other_cols], other_place, fq_s, fqb_s, fq_r, fqb_r)
+    final_proj(value_of, value_cols, 512, 256, zv_r, zvc_r)
+    spread(FQ.at[:, :, value_cols], value_place, fv_s, fvb_s, fv_r, fvb_r)
+    spread_on(in_place, fib_s, fi_r, fib_r)
+    recv(REO.at[z], zo_r.at[z])
+    recv(RCO, zoc_r)
+    FO[...] = (ZO[z].astype(F32) + REO[z].astype(F32) + RCO[...].astype(F32)).astype(BF)
+    remote(FO, out_rows(c), fo_s, fo_r.at[1], y_core).start()
+    remote(FO, out_rows(c), fo_s, fo_r.at[2], sib).start()
+    pltpu.make_async_copy(FO, out_rows(c), fo_r.at[0]).start()
+    spread_on(other_place, fqb_s, fq_r, fqb_r)
+    spread_on(value_place, fvb_s, fv_r, fvb_r)
     y_out = out_rows(2 * y1 + k)
     recv(y_out, fo_r.at[1])
     remote(y_out, y_out, fo_s, fo_r.at[2], sib).start()
@@ -1184,8 +1242,10 @@
     recv(oout.at[pl.ds(0, 64)], fo_r.at[2])
     recv(in_place(q, k), fi_r.at[0])
     recv(oin.at[:, :, rows_at(64 * k1, 64), :], fib_r)
-    recv(proj_place(q, k), fq_r.at[0])
-    recv(oqkv.at[:, rows_at(64 * k1, 64), :], fqb_r)
+    recv(other_place(q, k), fq_r.at[0])
+    recv(oqkv.at[:, rows_at(64 * k1, 64), other_cols], fqb_r)
+    recv(value_place(q, k), fv_r.at[0])
+    recv(oqkv.at[:, rows_at(64 * k1, 64), value_cols], fvb_r)
 
     sent(GP.at[pl.ds(0, 7)], gp_s)
     four_sent(XB, xb_s)
@@ -1239,9 +1299,11 @@
     sent(DQ.at[k1, :, :, other_cols], sib_s.at[4])
     sent(odown.at[pl.ds(0, 384)], fd_s)
     sent(oin.at[:, pl.ds(0, 3), pl.ds(0, 64), :], fi_s)
-    sent(oqkv.at[pl.ds(0, 3), pl.ds(0, 64), :], fq_s)
+    sent(oqkv.at[pl.ds(0, 3), pl.ds(0, 64), other_cols], fq_s)
+    sent(oqkv.at[pl.ds(0, 3), pl.ds(0, 64), value_cols], fv_s)
     sent(oin.at[:, :, rows_at(64 * k, 64), :], fib_s)
-    sent(oqkv.at[:, rows_at(64 * k, 64), :], fqb_s)
+    sent(oqkv.at[:, rows_at(64 * k, 64), other_cols], fqb_s)
+    sent(oqkv.at[:, rows_at(64 * k, 64), value_cols], fvb_s)
     sent(RSMALL.at[pl.ds(0, 7)], sp_s)
 
 
@@ -1261,7 +1323,8 @@
         tokens(256, BF), tokens(1024, BF), tokens(1024, F32), tokens(1024, BF),
         tokens(256, BF), tokens(768, BF), vm((4, 512, 512), BF), vm((4, 128, 1024), F32),
         tokens(1024, BF), tokens(1024, BF), tokens(1024, BF), tokens(1024, BF),
-        vm((4, 128, 1024), BF), vm((4, 128, 1024), BF), vm((4, 128, 1024), BF), vm((4, 128, 1024), BF),
+        vm((3, 128, 1024), BF), vm((3, 128, 1024), BF), vm((3, 128, 1024), BF), vm((3, 128, 1024), BF),
+        vm((2, 64, 1024), BF), vm((2, 64, 1024), BF), vm((2, 64, 1024), BF), vm((2, 64, 1024), BF),
         block(F32), block(F32), block(BF), block(BF),
         vm((2, 8, 64, 768), BF), vm((2, 4, 32, 1024), BF), vm((2, 8, 64, 1024), BF), vm((2, 4, 128, 1024), BF),
         vm((8, 64, 768), BF), vm((4, 32, 1024), BF), vm((8, 64, 1024), BF), vm((4, 128, 1024), BF),
@@ -1271,12 +1334,12 @@
         vm((2, 64, 768), BF), vm((32, 1024), BF), vm((2, 4, 64, 256), BF), vm((128, 1024), BF),
         vm((3, 8, 128), F32), vm((8, 3, 8, 128), F32), vm((4, 8, 128), F32), vm((4, 8, 128), F32),
         dma((7,)), dma, dma, dma, dma((4,)), dma((2,)), dma, dma((4,)), dma((2,)), dma, dma((4,)), dma((2,)), dma, dma((4,)), dma((2,)),
-        dma, dma, dma, dma, dma, dma, dma, dma,
+        dma, dma, dma((2,)), dma, dma, dma((2,)), dma, dma, dma((2,)), dma, dma, dma((2,)),
         dma((2,)), dma((2,)), dma, dma, dma((8,)), dma, dma, dma, dma, dma((8,)), dma, dma,
         dma, dma, dma((4,)), dma, dma, dma, dma((4,)), dma, dma,
         dma((5,)), dma((5,)), dma((4,)), dma, dma, dma((4,)), dma, dma, dma, dma((4,)), dma, dma, dma, dma((4,)), dma,
         dma, dma, dma((4,)), dma, dma, dma, dma((4,)), dma,
-        dma, dma, dma((4,)), dma, dma, dma((3,)), dma, dma, dma((4,)), dma, dma, dma((3,)), dma, dma, dma, dma,
+        dma, dma, dma((4,)), dma, dma, dma, dma((4,)), dma, dma, dma((3,)), dma, dma, dma((4,)), dma, dma, dma((3,)), dma, dma, dma, dma,
     ]
     anywhere = pl.BlockSpec(memory_space=pl.ANY)
     in_vmem = pl.BlockSpec(memory_space=pltpu.VMEM)

time: 144 us -> 135 us (0.938)
  Pallas kernels: 143 us -> 134 us
    pallas_call x1, Pallas kernels: 138 us -> 130 us  [plane_shards(): pl.pallas_call(fused_layer, out_shape=(shape((1, TOKENS, WIDTH), BF), sha...]
where the time goes in v5:
time: 135 us
  Pallas kernels  134 us (99%)
    pallas_call x1, Pallas kernels, plane_shards(): pl.pallas_call(fused_layer, out_shape=(shape((1, TOKENS, WIDTH), BF), sha...  130 us
    pallas_call x1, Pallas kernels, finish(): pl.pallas_call(finish_kernel, out_shape=(shape(output.shape, BF), shape(g...  4.8 us

profile of v5, /device:TPU:0, one launch (start us, length us, event | category | flops | bytes accessed | tf_op | source)
XLA Modules:
  0.0 135.1 jit_solution(6136524727972160268)
XLA Ops:
  0.6 129.5 %shard_map.203 = (bf16[1,128,1024]{2,1,0:T(8,128)(2,1)}, bf16[1,128,1024]{2,1,0:T(8,128)(2,1)}, bf16[4,128,768]{2,1,0:T(8,128)(2,1)}, bf16[128,1024]{1,0:T(8,128...) custom-call(bf16[1,128,1024]{2,1,0:T(8,128)(2,1)} %x_in.1, ...), custom_call_target="tpu_custom_call" | custom-call | flops 11000000512 | bytes 16777216 | tf_op jit(solution)/shard_map/pallas_call | solution.py:1347
  130.2 4.8 %shard_map.204 = (bf16[1,128,1024]{2,1,0:T(8,128)(2,1)}, bf16[1,128,1024]{2,1,0:T(8,128)(2,1)}, f32[128,1024]{1,0:T(8,128)}, f32[128,1024]{1,0:T(8,128)}, f32[12...) custom-call(bf16[1,128,1024]{2,1,0:T(8,128)(2,1)} %get-tuple-element, ...), custom_call_target="tpu_custom_call" | custom-call | bytes 10485760 | tf_op jit(solution)/shard_map/pallas_call | solution.py:1432

commit v6 on v5

--- a/solution.py
+++ b/solution.py
@@ -629,7 +629,7 @@
         table = jnp.where(head_mask, jnp.broadcast_to(GP[g, 2:3, :], (8, 128)), 0.0).astype(BF)
         return total + dot_nn(table, bucket_hot(g).astype(BF))
 
-    offsets = lax.fori_loop(0, 8, add_bias, jnp.zeros((8, WIDTH), F32))
+    offsets = steps(8, add_bias, jnp.zeros((8, WIDTH), F32))
     for h in range(4):
         spread = jnp.broadcast_to(offsets[h : h + 1, :], (128, WIDTH))
         BIAS[h] = pltpu.roll(spread, WIDTH - 127, 1, stride=1, stride_axis=0)
@@ -650,7 +650,7 @@
 
         return steps(4, chunk, carry)
 
-    lax.fori_loop(0, 4, norm_block, 0)
+    steps(4, norm_block, 0)
 
     @pl.when(middle)
     def _():
@@ -904,6 +904,9 @@
         return carry
 
     steps(4, down_project, 0)
+    for i in range(2):
+        scatter_first(SO, RO, o_s, o_r, XS, o_x, i)
+
 
     recv(SIBI, sib_r.at[1])
 
@@ -946,8 +949,9 @@
 
     gather_pass(GAL, ga_s, ga_r, ga_p)
     for i in range(2):
-        scatter_first(SO, RO, o_s, o_r, XS, o_x, i)
         scatter_second(SO, RO, o_s, o_r, i)
+
+    scatter_sums(SO, RO, o_s, o_r, XS, o_x)
 
     all_low = lax.broadcasted_iota(jnp.int32, (512, 128), 1) < 64
 
@@ -983,7 +987,6 @@
         return carry
 
     lax.fori_loop(0, 4, attend_back, 0)
-    scatter_sums(SO, RO, o_s, o_r, XS, o_x)
 
     def grad_keys(j, carry):
         query = QKV[:, rows_at(128 * j, 128)]
@@ -1021,29 +1024,30 @@
 
         steps(8, step, 0)
 
+    def back_project(i, carry):
+        yy = lax.rem(first_pair + i, 2)
+        rows = rows_at(256 * yy, 256)
+        SN[rows, :] = dot_nt(DQKV[rows, :], WQKV[...]).astype(BF)
+
+        @pl.when(i == 0)
+        def _():
+            for n in range(2):
+                scatter_first(SN, RN, n_s, n_r, XN, n_x, n)
+
+        @pl.when(i == 1)
+        def _():
+            for n in range(2):
+                scatter_second(SN, RN, n_s, n_r, n)
+
+        return carry
+
+    lax.fori_loop(0, 2, back_project, 0)
+
     grad_proj(0, 512)
     remote(DQ.at[k1, :, :, other_cols], SIBQ.at[:, :, other_cols], sib_s.at[4], sib_r.at[4], sib).start()
     grad_proj(512, 256)
     remote(DQ.at[k1, :, :, value_cols], SIBQ.at[:, :, value_cols], sib_s.at[2], sib_r.at[2], sib).start()
 
-    def back_project(i, carry):
-        yy = lax.rem(first_pair + i, 2)
-        rows = rows_at(256 * yy, 256)
-        SN[rows, :] = dot_nt(DQKV[rows, :], WQKV[...]).astype(BF)
-
-        @pl.when(i == 0)
-        def _():
-            for n in range(2):
-                scatter_first(SN, RN, n_s, n_r, XN, n_x, n)
-
-        @pl.when(i == 1)
-        def _():
-            for n in range(2):
-                scatter_second(SN, RN, n_s, n_r, n)
-
-        return carry
-
-    lax.fori_loop(0, 2, back_project, 0)
 
     recv(SIBQ.at[:, :, other_cols], sib_r.at[4])
     join_proj(0, 512)
@@ -1076,7 +1080,7 @@
             BACC[h, :, window] = BACC[h, :, window] + DS[h, rows, :].astype(F32)
         return carry
 
-    lax.fori_loop(0, 4, place_scores, 0)
+    steps(4, place_scores, 0)
     head_sums = []
     for h in range(4):
         rest = BACC[h]
@@ -1098,7 +1102,7 @@
         SMALL[2, pl.ds(g, 1), :] = jnp.sum(jnp.where(both_masks, sums, 0.0), axis=0, keepdims=True)
         return carry
 
-    lax.fori_loop(0, 8, bucket_sums, 0)
+    steps(8, bucket_sums, 0)
 
     recv(RED.at[z], zd_r.at[z])
     recv(RCD, zdc_r)

time: 135 us -> 131 us (0.970)
  Pallas kernels: 134 us -> 130 us
    pallas_call x1, Pallas kernels: 130 us -> 126 us  [plane_shards(): pl.pallas_call(fused_layer, out_shape=(shape((1, TOKENS, WIDTH), BF), sha...]
where the time goes in v6:
time: 131 us
  Pallas kernels  130 us (99%)
    pallas_call x1, Pallas kernels, plane_shards(): pl.pallas_call(fused_layer, out_shape=(shape((1, TOKENS, WIDTH), BF), sha...  126 us
    pallas_call x1, Pallas kernels, finish(): pl.pallas_call(finish_kernel, out_shape=(shape(output.shape, BF), shape(g...  4.8 us

profile of v6, /device:TPU:0, one launch (start us, length us, event | category | flops | bytes accessed | tf_op | source)
XLA Modules:
  0.0 131.2 jit_solution(16781373314358105669)
XLA Ops:
  0.6 125.6 %shard_map.203 = (bf16[1,128,1024]{2,1,0:T(8,128)(2,1)}, bf16[1,128,1024]{2,1,0:T(8,128)(2,1)}, bf16[4,128,768]{2,1,0:T(8,128)(2,1)}, bf16[128,1024]{1,0:T(8,128...) custom-call(bf16[1,128,1024]{2,1,0:T(8,128)(2,1)} %x_in.1, ...), custom_call_target="tpu_custom_call" | custom-call | flops 11000000512 | bytes 16777216 | tf_op jit(solution)/shard_map/pallas_call | solution.py:1351
  126.3 4.8 %shard_map.204 = (bf16[1,128,1024]{2,1,0:T(8,128)(2,1)}, bf16[1,128,1024]{2,1,0:T(8,128)(2,1)}, f32[128,1024]{1,0:T(8,128)}, f32[128,1024]{1,0:T(8,128)}, f32[12...) custom-call(bf16[1,128,1024]{2,1,0:T(8,128)(2,1)} %get-tuple-element, ...), custom_call_target="tpu_custom_call" | custom-call | bytes 10485760 | tf_op jit(solution)/shard_map/pallas_call | solution.py:1436

commit v7 on v6

--- a/solution.py
+++ b/solution.py
@@ -1375,16 +1375,17 @@
     o_output, o_inputs, o_query, o_key, o_value, o_out, o_in, o_down, o_attn, o_mlp, o_bias,
     b_output, b_inputs, b_proj, b_out, b_hidden, b_down, b_small, w_proj, w_out, w_in, w_down, got, left,
 ):
+    quarters = [pl.ds(128 * r, 128) for r in range(4)]
+    downs = [pltpu.make_async_copy(down.at[rows], b_down.at[rows], got.at[6 + r]) for r, rows in enumerate(quarters)]
     moves = [
         pltpu.make_async_copy(proj, b_proj, got.at[0]),
         pltpu.make_async_copy(hidden, b_hidden, got.at[1]),
-        pltpu.make_async_copy(down, b_down, got.at[2]),
-        pltpu.make_async_copy(out, b_out, got.at[3]),
-        pltpu.make_async_copy(small, b_small, got.at[4]),
-        pltpu.make_async_copy(output, b_output, got.at[5]),
-        pltpu.make_async_copy(grad_inputs, b_inputs, got.at[6]),
+        pltpu.make_async_copy(out, b_out, got.at[2]),
+        pltpu.make_async_copy(small, b_small, got.at[3]),
+        pltpu.make_async_copy(output, b_output, got.at[4]),
+        pltpu.make_async_copy(grad_inputs, b_inputs, got.at[5]),
     ]
-    for move in moves:
+    for move in downs + moves:
         move.start()
     sends = []
 
@@ -1393,6 +1394,11 @@
         copy.start()
         sends.append(copy)
 
+    for r in range(4):
+        downs[r].wait()
+        rows = slice(128 * r, 128 * r + 128)
+        w_down[rows, :] = b_down[rows, :].astype(F32)
+        write(w_down.at[quarters[r]], o_down.at[quarters[r]], 7 + r)
     moves[0].wait()
     for w, place in enumerate((o_query, o_key, o_value)):
         for shard in range(8):
@@ -1409,20 +1415,15 @@
                 w_in[rows, 256 * (4 * z + q) : 256 * (4 * z + q) + 256] = b_hidden[z, q, rows, :].astype(F32)
         write(w_in.at[pl.ds(32 * r, 32)], o_in.at[pl.ds(32 * r, 32)], 3 + r)
     moves[2].wait()
-    for r in range(4):
-        rows = slice(128 * r, 128 * r + 128)
-        w_down[rows, :] = b_down[rows, :].astype(F32)
-        write(w_down.at[pl.ds(128 * r, 128)], o_down.at[pl.ds(128 * r, 128)], 7 + r)
-    moves[3].wait()
     w_out[...] = b_out[...].astype(F32)
     write(w_out, o_out, 11)
-    moves[4].wait()
+    moves[3].wait()
     o_attn[...] = b_small[0:1, :]
     o_mlp[...] = b_small[1:2, :]
     o_bias[...] = b_small[2:3, 0:64]
+    moves[4].wait()
+    write(b_output, o_output, 12)
     moves[5].wait()
-    write(b_output, o_output, 12)
-    moves[6].wait()
     write(b_inputs, o_inputs, 13)
     for copy in sends:
         copy.wait()
@@ -1453,7 +1454,7 @@
         scratch_shapes=[
             vm(output.shape, BF), vm(grad_inputs.shape, BF), vm(proj.shape, BF), vm(out.shape, BF), vm(hidden.shape, BF), vm(down.shape, BF), vm(small.shape, F32),
             vm((3, 128, 1024), F32), vm((128, 1024), F32), vm((128, 4096), F32), vm((512, 1024), F32),
-            pltpu.SemaphoreType.DMA((7,)), pltpu.SemaphoreType.DMA((14,)),
+            pltpu.SemaphoreType.DMA((10,)), pltpu.SemaphoreType.DMA((14,)),
         ],
         compiler_params=pltpu.CompilerParams(vmem_limit_bytes=63 << 20),
         cost_estimate=pl.CostEstimate(flops=0, bytes_accessed=10 * 2**20, transcendentals=0),

time: 131 us -> 131 us (level)
  no operation moved by 1% of the time
where the time goes in v7:
time: 131 us
  Pallas kernels  130 us (99%)
    pallas_call x1, Pallas kernels, plane_shards(): pl.pallas_call(fused_layer, out_shape=(shape((1, TOKENS, WIDTH), BF), sha...  126 us
    pallas_call x1, Pallas kernels, finish(): pl.pallas_call(finish_kernel, out_shape=(shape(output.shape, BF), shape(g...  4.51 us

profile of v7, /device:TPU:0, one launch (start us, length us, event | category | flops | bytes accessed | tf_op | source)
XLA Modules:
  0.0 131.0 jit_solution(16359209729525988928)
XLA Ops:
  0.6 125.6 %shard_map.203 = (bf16[1,128,1024]{2,1,0:T(8,128)(2,1)}, bf16[1,128,1024]{2,1,0:T(8,128)(2,1)}, bf16[4,128,768]{2,1,0:T(8,128)(2,1)}, bf16[128,1024]{1,0:T(8,128...) custom-call(bf16[1,128,1024]{2,1,0:T(8,128)(2,1)} %x_in.1, ...), custom_call_target="tpu_custom_call" | custom-call | flops 11000000512 | bytes 16777216 | tf_op jit(solution)/shard_map/pallas_call | solution.py:1351
  126.3 4.5 %shard_map.204 = (bf16[1,128,1024]{2,1,0:T(8,128)(2,1)}, bf16[1,128,1024]{2,1,0:T(8,128)(2,1)}, f32[128,1024]{1,0:T(8,128)}, f32[128,1024]{1,0:T(8,128)}, f32[12...) custom-call(bf16[1,128,1024]{2,1,0:T(8,128)(2,1)} %get-tuple-element, ...), custom_call_target="tpu_custom_call" | custom-call | bytes 10485760 | tf_op jit(solution)/shard_map/pallas_call | solution.py:1437
